TPU v7x, 128 devices: a whole 4x4x4 slice. The times are simulated.
128 devices in a mesh: tm: 8 (over x, core), row: 4 (over z), col: 4 (over y).
Axes of the slice: x: 4, y: 4, z: 4, core: 2. Of those that a mesh axis runs over, the one named last changes fastest.
Arguments:
- frames_in: bfloat16 [64, 32, 640, 128], P('tm', 'row', 'col'), may hold values from -6 to 6
- clip_frames: int32 [4], replicated, may hold values from 1 to 32, 64 in all
- conv_weight: bfloat16 [3, 3, 3, 128, 256], replicated, may hold values from -0.109375 to 0.109375
- norm_gain: float32 [256], replicated, may hold values from 0.1 to 1.9
- norm_shift: float32 [256], replicated, may hold values from -3 to 3
Outputs:
- activated: bfloat16 [64, 32, 640, 256], P('tm', 'row', 'col')
Inputs may be any that keep to these rules, and one draw needn't show every extreme that they name: `clip_frames`: every clip has at least one frame; the longest has exactly 32.
All inputs are finite; a program needn't handle non-finite values.
Results may differ from a plain program's by a relative error of at most 0.0005.
Values may be sent and summed in bfloat16 or wider, within the bound.
No kernel may reach another device: no remote copies, remote signals or barrier semaphores. Data moves between devices by JAX's collectives and lax.ppermute only.
A program may use at most 128 MiB of HBM per device.

v0:
```python
import jax
import jax.numpy as jnp
from jax import lax
from jax.sharding import PartitionSpec as P

COUT = 256
GROUPS = 32
CLIPS = 4


def shifted(value, axis, steps):
    count = lax.axis_size(axis)
    first, last = (max(0, -steps), min(count, count - steps))
    return lax.ppermute(value, axis, [(source, source + steps) for source in range(first, last)])


def with_halo(block, sides, width):
    for axis, dim in sides:
        count = lax.axis_size(axis)
        forward = [(i, i + 1) for i in range(count - 1)]
        backward = [(target, source) for source, target in forward]
        low = lax.ppermute(
            lax.slice_in_dim(block, block.shape[dim] - width, None, axis=dim), axis, forward
        )
        high = lax.ppermute(lax.slice_in_dim(block, 0, width, axis=dim), axis, backward)
        block = jnp.concatenate([low, block, high], axis=dim)
    return block


def plane_conv(frames, kernel):
    return lax.conv_general_dilated(
        frames,
        kernel,
        (1, 1),
        "VALID",
        dimension_numbers=("NHWC", "HWIO", "NHWC"),
        preferred_element_type=jnp.float32,
    )


def clamp_edges(padded):
    row_index = lax.axis_index("row")
    last_row = lax.axis_size("row") - 1
    top_rim = jnp.where(row_index == 0, padded[:, 1:2], padded[:, 0:1])
    bottom_rim = jnp.where(row_index == last_row, padded[:, -2:-1], padded[:, -1:])
    padded = jnp.concatenate([top_rim, padded[:, 1:-1], bottom_rim], axis=1)
    col_index = lax.axis_index("col")
    last_col = lax.axis_size("col") - 1
    left_rim = jnp.where(col_index == 0, padded[:, :, 1:2], padded[:, :, 0:1])
    right_rim = jnp.where(col_index == last_col, padded[:, :, -2:-1], padded[:, :, -1:])
    return jnp.concatenate([left_rim, padded[:, :, 1:-1], right_rim], axis=2)


def shards(frames_in, clip_frames, conv_weight, norm_gain, norm_shift):
    count_frames, tile_rows, tile_cols, _ = frames_in.shape
    first = lax.axis_index("tm") * count_frames
    starts = jnp.cumsum(clip_frames) - clip_frames
    glob = first + jnp.arange(count_frames, dtype=jnp.int32)
    member = (glob[:, None] >= starts[None, :]).astype(jnp.int32)
    clip_of = jnp.sum(member, axis=1) - 1
    onehot = clip_of[:, None] == jnp.arange(CLIPS, dtype=jnp.int32)[None, :]
    start_of = jnp.sum(onehot.astype(jnp.int32) * starts[None, :], axis=1)
    previous = shifted(frames_in[count_frames - 2 :], "tm", 1)
    extended = jnp.concatenate([previous, frames_in], axis=0)
    padded = with_halo(extended, (("row", 1), ("col", 2)), 1)
    padded = clamp_edges(padded)
    conv = jnp.zeros((count_frames, tile_rows, tile_cols, COUT), jnp.float32)
    for tap in range(3):
        source = jnp.maximum(glob - 2 + tap, start_of) - (first - 2)
        conv = conv + plane_conv(jnp.take(padded, source, axis=0), conv_weight[tap])
    share = COUT // GROUPS
    full_cells = tile_rows * lax.axis_size("row") * tile_cols * lax.axis_size("col")
    onef = onehot.astype(jnp.float32)
    count = (clip_frames.astype(jnp.float32) * (full_cells * share))[:, None]
    grouped = conv.reshape(count_frames, tile_rows * tile_cols, GROUPS, share)
    frame_sums = jnp.sum(grouped, axis=(1, 3))
    local_sums = jnp.dot(onef.T, frame_sums, precision=lax.Precision.HIGHEST)
    mean = lax.psum(local_sums, ("tm", "row", "col")) / count
    mean_frames = jnp.dot(onef, mean, precision=lax.Precision.HIGHEST)
    centred = grouped - mean_frames[:, None, :, None]
    frame_sq = jnp.sum(centred * centred, axis=(1, 3))
    local_sq = jnp.dot(onef.T, frame_sq, precision=lax.Precision.HIGHEST)
    var = lax.psum(local_sq, ("tm", "row", "col")) / count
    scale_frames = jnp.dot(onef, lax.rsqrt(var + 1e-06), precision=lax.Precision.HIGHEST)
    normed = (centred * scale_frames[:, None, :, None]).reshape(
        count_frames, tile_rows, tile_cols, COUT
    )
    return jax.nn.silu(normed * norm_gain + norm_shift).astype(jnp.bfloat16)


def solution(mesh):
    return jax.shard_map(
        shards,
        mesh=mesh,
        in_specs=(P("tm", "row", "col", None), P(), P(), P(), P()),
        out_specs=P("tm", "row", "col", None),
        check_vma=False,
    )
```

profile of v0, /device:TPU:1, one launch (start us, length us, event | category | flops | bytes accessed | tf_op | source)
XLA Modules:
  0.0 250.1 jit_solution(17048078075494836377)
XLA Ops:
  0.0 1.1 slice.54
  1.1 0.0 copy-start.7
  1.1 4.5 %collective-permute-start = (bf16[2,8,160,128]{3,2,1,0:T(8,128)(2,1)S(1)}, bf16[2,8,160,128]{3,2,1,0:T(8,128)(2,1)}, u32[]{:S(2)}, u32[]{:S(2)}) collective-permute-start(bf16[2,8,160,128]{3,2,1,0:T(8,128)(2,1)S(1)} %slice.54), channel_id=1, source_target_pairs={{0,16},{16,32},{32,48},{48,64},{64,80},{80,96},{96,112},{1,17},{17... | collective-permute-start | bytes 1966088 | tf_op jit(solution)/shard_map/ppermute | solution.py:14
  5.7 0.8 reduce-window.9
  6.5 0.7 bitcast_subtract_fusion
  7.2 0.1 convert_reduce_fusion
  7.3 0.1 select_reduce_fusion
  7.4 5.8 %collective-permute-done = bf16[2,8,160,128]{3,2,1,0:T(8,128)(2,1)} collective-permute-done((bf16[2,8,160,128]{3,2,1,0:T(8,128)(2,1)S(1)}, bf16[2,8,160,128]{3,2,1,0:T(8,128)(2,1)}, u32[]{:S(2)}, u32[]{:S(2)}) %collective-permute-start) | collective-permute-done | bytes 655392 | tf_op jit(solution)/shard_map/ppermute | solution.py:14
  13.2 1.1 constant_dynamic-update-slice_fusion.1
  14.3 2.1 constant_dynamic-update-slice_fusion
  16.4 0.1 fusion.30
  16.5 3.6 %collective-permute-start.1 = (bf16[10,1,160,128]{3,2,1,0:T(8,128)(2,1)S(1)}, bf16[10,1,160,128]{3,2,1,0:T(8,128)(2,1)S(1)}, u32[]{:S(2)}, u32[]{:S(2)}) collective-permute-start(bf16[10,1,160,128]{3,2,1,0:T(8,128)(2,1)S(1)} %get-tuple-element.16), channel_id=1, source_target_pairs={{0,4},{4,8},{8,12},{1,5},{5,9},{9,13},{2,6},{6,10},{10,14},{3,7},{... | collective-permute-start | bytes 1228808 | tf_op jit(solution)/shard_map/ppermute | solution.py:22
  20.1 1.3 collective-permute-start.2
  21.4 0.0 copy-done.7
  21.4 3.5 %collective-permute-done.1 = bf16[10,1,160,128]{3,2,1,0:T(8,128)(2,1)S(1)} collective-permute-done((bf16[10,1,160,128]{3,2,1,0:T(8,128)(2,1)S(1)}, bf16[10,1,160,128]{3,2,1,0:T(8,128)(2,1)S(1)}, u32[]{:S(2)}, u32[]{:S(2)}) %collective-permute-start.1) | collective-permute-done | bytes 409632 | tf_op jit(solution)/shard_map/ppermute | solution.py:22
  24.9 4.0 %collective-permute-done.2 = bf16[10,1,160,128]{3,2,1,0:T(8,128)(2,1)S(1)} collective-permute-done((bf16[10,1,160,128]{3,2,1,0:T(8,128)(2,1)S(1)}, bf16[10,1,160,128]{3,2,1,0:T(8,128)(2,1)S(1)}, u32[]{:S(2)}, u32[]{:S(2)}) %collective-permute-start.2) | collective-permute-done | bytes 409632 | tf_op jit(solution)/shard_map/ppermute | solution.py:25
  28.9 0.0 copy-done
  28.9 0.1 pad_maximum_fusion.5
  29.0 0.7 copy-done.2
  29.7 3.2 %collective-permute-start.3 = (bf16[10,10,1,128]{3,2,1,0:T(2,128)(2,1)S(1)}, bf16[10,10,1,128]{3,2,1,0:T(2,128)(2,1)S(1)}, u32[]{:S(2)}, u32[]{:S(2)}) collective-permute-start(bf16[10,10,1,128]{3,2,1,0:T(2,128)(2,1)S(1)} %get-tuple-element.14), channel_id=1, source_target_pairs={{0,1},{1,2},{2,3},{4,5},{5,6},{6,7},{8,9},{9,10},{10,11},{12,13},{... | collective-permute-start | bytes 76808 | tf_op jit(solution)/shard_map/ppermute | solution.py:22
  32.9 1.3 collective-permute-start.4
  34.2 0.0 collective-permute-done.3
  34.2 3.5 %collective-permute-done.4 = bf16[10,10,1,128]{3,2,1,0:T(2,128)(2,1)S(1)} collective-permute-done((bf16[10,10,1,128]{3,2,1,0:T(2,128)(2,1)S(1)}, bf16[10,10,1,128]{3,2,1,0:T(2,128)(2,1)S(1)}, u32[]{:S(2)}, u32[]{:S(2)}) %collective-permute-start.4) | collective-permute-done | bytes 25632 | tf_op jit(solution)/shard_map/ppermute | solution.py:25
  37.7 3.4 %pad_maximum_fusion = bf16[10,10,162,128]{3,2,1,0:T(8,128)(2,1)S(1)} fusion(bf16[10,10,1,128]{3,2,1,0:T(2,128)(2,1)S(1)} %collective-permute-done.4, bf16[10,1,160,128]{3,2,1,0:T(8,128)(2,1)} %copy-done.2, bf16[10,8,160,128]{3,2,1,0:T(8,128)(2,1)S(1)} %constant_dynamic-update-slice_fusion, bf16[10,1,160,128]{3,2,1,0:T(8,128)(2,1)} %copy-done, ...), kind=kLoop, calls=%fused_computation.6 | loop fusion | flops 20736000 | bytes 8294400 | tf_op jit(solution)/shard_map/concatenate | solution.py:26
  41.1 0.0 copy-start.1
  41.1 0.0 copy-start.3
  41.1 0.3 slice.80
  41.4 0.7 copy-done.1
  42.1 0.1 copy-done.3
  42.2 0.3 maximum_select_fusion.1
  42.5 0.3 maximum_select_fusion
  42.8 0.6 pad_maximum_fusion.1
  43.4 2.1 slice.81
  45.5 0.2 broadcast_select_fusion.4
  45.6 3.3 %pad_maximum_fusion.2 = bf16[10,10,162,128]{3,2,1,0:T(8,128)(2,1)} fusion(bf16[10,10,1,128]{3,2,1,0:T(2,128)(2,1)S(1)} %get-tuple-element.13, bf16[10,10,160,128]{3,2,1,0:T(8,128)(2,1)S(1)} %slice.81, bf16[10,10,1,128]{3,2,1,0:T(2,128)(2,1)S(1)} %get-tuple-element.12), kind=kLoop, calls=%fused_computation.8 | loop fusion | flops 12441600 | bytes 8294400 | tf_op jit(solution)/shard_map/concatenate | solution.py:51
  49.0 4.9 %gather_fusion.2 = bf16[8,10,162,128]{3,2,1,0:T(8,128)(2,1)} fusion(bf16[10,10,162,128]{3,2,1,0:T(8,128)(2,1)} %pad_maximum_fusion.2, s32[1024]{0:T(1024)S(1)} %pad_clamp_fusion), kind=kCustom, calls=%fused_computation.2.clone | custom fusion | bytes 6635552 | tf_op jit(solution)/shard_map/jit(_take)/gather | solution.py:70
  53.9 5.0 %gather_fusion.1 = bf16[8,10,162,128]{3,2,1,0:T(8,128)(2,1)} fusion(bf16[10,10,162,128]{3,2,1,0:T(8,128)(2,1)} %pad_maximum_fusion.2, s32[1024]{0:T(1024)S(1)} %pad_clamp_fusion.1), kind=kCustom, calls=%fused_computation.1.clone | custom fusion | bytes 6635552 | tf_op jit(solution)/shard_map/jit(_take)/gather | solution.py:70
  58.9 3.4 %gather_fusion = bf16[8,10,162,128]{3,2,1,0:T(8,128)(2,1)S(1)} fusion(bf16[10,10,162,128]{3,2,1,0:T(8,128)(2,1)} %pad_maximum_fusion.2, s32[1024]{0:T(1024)S(1)} %pad_clamp_fusion.2), kind=kCustom, calls=%fused_computation.clone | custom fusion | bytes 6635552 | tf_op jit(solution)/shard_map/jit(_take)/gather | solution.py:70
  62.3 0.0 copy-start.6
  62.4 3.8 %broadcast_select_fusion = (bf16[8,10,162,128]{3,2,1,0:T(8,128)(2,1)S(1)}, bf16[8,10,162,128]{3,2,1,0:T(8,128)(2,1)S(1)}) fusion(bf16[8,10,162,128]{3,2,1,0:T(8,128)(2,1)} %gather_fusion.2, pred[8]{0:T(512)(128)(4,1)S(1)} %get-tuple-element.20, bf16[8,10,162,128]{3,2,1,0:T(8,128)(2,1)} %gather_fusion.1, pred[8]{0:T(512)(128)(4,1)S(1)} %get-tuple-element.18), kind=kLoop, calls=%fused_computation.9 | loop fusion | flops 3317760 | bytes 13271056 | tf_op jit(solution)/shard_map/jit(_take)/select_n | solution.py:70
  66.2 0.0 copy-done.6
  66.2 10.0 %fusion = f32[8,8,160,256]{3,0,2,1:T(8,128)} fusion(bf16[8,10,162,128]{3,2,1,0:T(8,128)(2,1)S(1)} %get-tuple-element.24, bf16[3,3,3,128,256]{4,3,2,1,0:T(8,128)(2,1)S(1)} %copy-done.6), kind=kOutput, calls=%fused_computation.12 | convolution fusion | flops 6039797760 | bytes 14516224 | tf_op jit(solution)/shard_map/conv_general_dilated | solution.py:31
  76.1 9.9 %fusion.2 = f32[8,8,160,256]{3,0,2,1:T(8,128)} fusion(bf16[8,10,162,128]{3,2,1,0:T(8,128)(2,1)S(1)} %get-tuple-element.25, bf16[3,3,3,128,256]{4,3,2,1,0:T(8,128)(2,1)S(1)} %copy-done.6), kind=kOutput, calls=%fused_computation.14 | convolution fusion | flops 6039797760 | bytes 14516224 | tf_op jit(solution)/shard_map/conv_general_dilated | solution.py:31
  86.1 0.4 broadcast_select_fusion.2
  86.5 14.4 %fusion.31 = (f32[8,256]{1,0:T(8,128)S(1)}, f32[8,8,160,256]{3,0,2,1:T(8,128)}) fusion(f32[8,8,160,256]{3,0,2,1:T(8,128)} %fusion, f32[8,8,160,256]{3,0,2,1:T(8,128)} %fusion.2, bf16[3,3,3,128,256]{4,3,2,1,0:T(8,128)(2,1)S(1)} %copy-done.6, bf16[8,10,162,128]{3,2,1,0:T(8,128)(2,1)S(1)} %broadcast_select_fusion.2), kind=kOutput, calls=%fused_computation.66 | convolution fusion | flops 6047660032 | bytes 35495936 | tf_op jit(solution)/shard_map/conv_general_dilated | solution.py:31
  100.9 0.1 reduce_sum.53
  101.0 0.1 reduce_sum.54
  101.1 0.1 fusion.20
  101.3 68.7 %psum.14 = f32[4,32]{1,0:T(4,128)S(1)} all-reduce(f32[4,32]{1,0:T(4,128)S(1)} %fusion.20), channel_id=1, replica_groups=mesh['tm'=8,'row'=4,'col'=4] {'tm','row','col'}, use_global_device_ids=true, to_apply=%region_5.7 | all-reduce | flops 128 | bytes 1024 | tf_op jit(solution)/shard_map/psum | solution.py:78
  169.9 0.2 fusion.19
  170.1 0.1 sub.52
  170.2 0.1 sub.53
  170.4 0.0 copy-start.4
  170.4 0.0 copy-start.5
  170.4 5.4 %multiply_reduce_fusion = f32[8,256]{1,0:T(8,128)S(1)} fusion(f32[8,8,160,256]{3,0,2,1:T(8,128)} %get-tuple-element.23, f32[8,256]{1,0:T(8,128)S(1)} %sub.53), kind=kLoop, calls=%fused_computation.4 | loop fusion | flops 7862272 | bytes 10502144 | tf_op jit(solution)/shard_map/reduce_sum | solution.py:81
  175.8 0.1 reduce_sum.56
  175.9 0.1 reduce_sum.57
  176.0 0.1 fusion.18
  176.1 63.7 %psum.15 = f32[4,32]{1,0:T(4,128)S(1)} all-reduce(f32[4,32]{1,0:T(4,128)S(1)} %fusion.18), channel_id=1, replica_groups=mesh['tm'=8,'row'=4,'col'=4] {'tm','row','col'}, use_global_device_ids=true, to_apply=%region_8.10 | all-reduce | flops 128 | bytes 1024 | tf_op jit(solution)/shard_map/psum | solution.py:83
  239.8 0.2 fusion.14
  240.0 0.1 mul.45
  240.1 0.1 mul.46
  240.3 6.2 %multiply_convert_fusion = bf16[8,8,160,256]{3,0,2,1:T(8,128)(2,1)S(1)} fusion(f32[8,8,160,256]{3,0,2,1:T(8,128)} %get-tuple-element.23, f32[256]{0:T(256)S(1)} %copy-done.4, f32[256]{0:T(256)S(1)} %copy-done.5, f32[8,256]{1,0:T(8,128)S(1)} %mul.46, f32[8,256]{1,0:T(8,128)S(1)} %sub.53), kind=kLoop, calls=%fused_computation.3 | loop fusion | flops 23592960 | bytes 15747072 | tf_op jit(solution)/shard_map/convert_element_type | solution.py:88
  246.5 3.6 %copy.17 = bf16[8,8,160,256]{3,2,1,0:T(8,128)(2,1)} copy(bf16[8,8,160,256]{3,0,2,1:T(8,128)(2,1)S(1)} %multiply_convert_fusion) | data formatting | bytes 10485760 | tf_op jit(solution)/shard_map/convert_element_type | solution.py:88
  (11 shorter events, 0.1 us)
Async XLA Ops:
  1.1 20.2 %copy-start.7 = (s32[4]{0:T(128)S(1)}, s32[4]{0:T(128)}, u32[]{:S(2)}) copy-start(s32[4]{0:T(128)} %param.8) | copy-start | bytes 52
  1.1 12.0 %collective-permute-start = (bf16[2,8,160,128]{3,2,1,0:T(8,128)(2,1)S(1)}, bf16[2,8,160,128]{3,2,1,0:T(8,128)(2,1)}, u32[]{:S(2)}, u32[]{:S(2)}) collective-permute-start(bf16[2,8,160,128]{3,2,1,0:T(8,128)(2,1)S(1)} %slice.54), channel_id=1, source_target_pairs={{0,16},{16,32},{32,48},{48,64},{64,80},{80,96},{96,112},{1,17},{17... | collective-permute-start | bytes 1966088 | tf_op jit(solution)/shard_map/ppermute | solution.py:14
  16.5 8.4 %collective-permute-start.1 = (bf16[10,1,160,128]{3,2,1,0:T(8,128)(2,1)S(1)}, bf16[10,1,160,128]{3,2,1,0:T(8,128)(2,1)S(1)}, u32[]{:S(2)}, u32[]{:S(2)}) collective-permute-start(bf16[10,1,160,128]{3,2,1,0:T(8,128)(2,1)S(1)} %get-tuple-element.16), channel_id=1, source_target_pairs={{0,4},{4,8},{8,12},{1,5},{5,9},{9,13},{2,6},{6,10},{10,14},{3,7},{... | collective-permute-start | bytes 1228808 | tf_op jit(solution)/shard_map/ppermute | solution.py:22
  20.1 8.9 %collective-permute-start.2 = (bf16[10,1,160,128]{3,2,1,0:T(8,128)(2,1)S(1)}, bf16[10,1,160,128]{3,2,1,0:T(8,128)(2,1)S(1)}, u32[]{:S(2)}, u32[]{:S(2)}) collective-permute-start(bf16[10,1,160,128]{3,2,1,0:T(8,128)(2,1)S(1)} %get-tuple-element.17), channel_id=1, source_target_pairs={{4,0},{8,4},{12,8},{5,1},{9,5},{13,9},{6,2},{10,6},{14,10},{7,3},{... | collective-permute-start | bytes 1228808 | tf_op jit(solution)/shard_map/ppermute | solution.py:25
  24.9 4.0 %copy-start = (bf16[10,1,160,128]{3,2,1,0:T(8,128)(2,1)}, bf16[10,1,160,128]{3,2,1,0:T(8,128)(2,1)S(1)}, u32[]{:S(2)}) copy-start(bf16[10,1,160,128]{3,2,1,0:T(8,128)(2,1)S(1)} %collective-permute-done.1) | copy-start | bytes 1228804
  28.9 0.8 copy-start.2
  29.7 4.5 %collective-permute-start.3 = (bf16[10,10,1,128]{3,2,1,0:T(2,128)(2,1)S(1)}, bf16[10,10,1,128]{3,2,1,0:T(2,128)(2,1)S(1)}, u32[]{:S(2)}, u32[]{:S(2)}) collective-permute-start(bf16[10,10,1,128]{3,2,1,0:T(2,128)(2,1)S(1)} %get-tuple-element.14), channel_id=1, source_target_pairs={{0,1},{1,2},{2,3},{4,5},{5,6},{6,7},{8,9},{9,10},{10,11},{12,13},{... | collective-permute-start | bytes 76808 | tf_op jit(solution)/shard_map/ppermute | solution.py:22
  32.9 4.9 %collective-permute-start.4 = (bf16[10,10,1,128]{3,2,1,0:T(2,128)(2,1)S(1)}, bf16[10,10,1,128]{3,2,1,0:T(2,128)(2,1)S(1)}, u32[]{:S(2)}, u32[]{:S(2)}) collective-permute-start(bf16[10,10,1,128]{3,2,1,0:T(2,128)(2,1)S(1)} %get-tuple-element.15), channel_id=1, source_target_pairs={{1,0},{2,1},{3,2},{5,4},{6,5},{7,6},{9,8},{10,9},{11,10},{13,12},{... | collective-permute-start | bytes 76808 | tf_op jit(solution)/shard_map/ppermute | solution.py:25
  41.1 1.0 copy-start.1
  41.1 1.1 copy-start.3
  62.3 3.8 %copy-start.6 = (bf16[3,3,3,128,256]{4,3,2,1,0:T(8,128)(2,1)S(1)}, bf16[3,3,3,128,256]{4,3,2,1,0:T(8,128)(2,1)}, u32[]{:S(2)}) copy-start(bf16[3,3,3,128,256]{4,3,2,1,0:T(8,128)(2,1)} %param.9) | copy-start | bytes 5308420
  170.4 69.9 %copy-start.4 = (f32[256]{0:T(256)S(1)}, f32[256]{0:T(256)}, u32[]{:S(2)}) copy-start(f32[256]{0:T(256)} %param.11) | copy-start | bytes 3076
  170.4 69.9 %copy-start.5 = (f32[256]{0:T(256)S(1)}, f32[256]{0:T(256)}, u32[]{:S(2)}) copy-start(f32[256]{0:T(256)} %param.10) | copy-start | bytes 3076
where the time goes:
time: 251 us; the launch traced here: 250 us
  blocking collectives  132 us (53%)
  matrix products  35 us (14%)
  local copies, waits for them, and re-layouts  25.8 us (10%)
  other arithmetic  25.8 us (10%)
  waiting for transfers between devices  16.8 us (7%)
  starting transfers between devices  13.9 us (6%)
    psum x1, blocking collectives, shards(): mean = lax.psum(local_sums, ('tm', 'row', 'col')) / count  68.7 us
    psum x1, blocking collectives, shards(): var = lax.psum(local_sq, ('tm', 'row', 'col')) / count  63.7 us
    conv_general_dilated x3, matrix products, plane_conv(): lax.conv_general_dilated(frames, kernel, (1, 1), 'VALID', dimension_numbe...  34.4 us
    gather x3, local copies, waits for them, and re-layouts, shards(): conv = conv + plane_conv(jnp.take(padded, source, axis=0), conv_weight[tap])  13.3 us
    ppermute x2, waiting for transfers between devices, with_halo(): lax.ppermute(lax.slice_in_dim(block, 0, width, axis=dim), axis, backward)  7.52 us
    ppermute x2, starting transfers between devices, with_halo(): lax.ppermute(lax.slice_in_dim(block, block.shape[dim] - width, None, axis...  6.76 us
    convert_element_type x1, other arithmetic, shards(): return jax.nn.silu(normed * norm_gain + norm_shift).astype(jnp.bfloat16)  6.23 us
    ppermute x1, waiting for transfers between devices, shifted(): lax.ppermute(value, axis, [(source, source + steps) for source in range(f...  5.81 us
  transfers between devices with their start and end apart: 5, of which 4 were waited for; matrix products, arithmetic and copies ran while one was open for 1% of the time, Pallas kernels for 0%

commit v1 on v0

v1 whole, which is shorter than its diff:
```python
import functools

import jax
import jax.numpy as jnp
from jax import lax
from jax.experimental import pallas as pl
from jax.experimental.pallas import tpu as pltpu
from jax.sharding import PartitionSpec as P

COUT = 256
GROUPS = 32
CLIPS = 4
SHARE = COUT // GROUPS
F, H, W, C = 8, 8, 160, 128
C3 = 3 * C
BF, F32 = jnp.bfloat16, jnp.float32
VMEM = pl.BlockSpec(memory_space=pltpu.VMEM)
SMEM = pl.BlockSpec(memory_space=pltpu.SMEM)
ANY = pl.BlockSpec(memory_space=pl.ANY)
HIGH = lax.Precision.HIGHEST


def clip_starts(frames_ref):
    starts = [0]
    for c in range(CLIPS - 1):
        starts.append(starts[-1] + frames_ref[c])
    return starts


def source(starts, first, f, k):
    g = first + f
    start = 0
    for s in starts[1:]:
        start = jnp.where(g >= s, s, start)
    return jnp.maximum(g - 2 + k, start) - first


def clip_index(starts, g):
    c = (g >= starts[1]).astype(jnp.int32)
    for s in starts[2:]:
        c = c + (g >= s).astype(jnp.int32)
    return c


def edges():
    row, col = lax.axis_index("row"), lax.axis_index("col")
    return row == 0, row == lax.axis_size("row") - 1, col == 0, col == lax.axis_size("col") - 1


def put_columns(xc, at, x, low, high):
    xc[(*at, slice(None), slice(0, C))] = jnp.concatenate([low, x[:, :-1]], axis=1)
    xc[(*at, slice(None), slice(C, 2 * C))] = x
    xc[(*at, slice(None), slice(2 * C, 3 * C))] = jnp.concatenate([x[:, 1:], high], axis=1)


def own_columns(xc, x_ref, frames):
    _, _, left, right = edges()

    def step(f, carry):
        x = x_ref[f]
        low = jnp.where(left, x[:, :1], jnp.zeros_like(x[:, :1]))
        high = jnp.where(right, x[:, -1:], jnp.zeros_like(x[:, -1:]))
        put_columns(xc, (f + 2, slice(1, H + 1)), x, low, high)
        return carry

    lax.fori_loop(frames[0], frames[1], step, 0)


def inner_taps(xc, w_ref, sources):
    rows = H - 2
    parts = [
        xc[s, 1 + dy : 1 + dy + rows].reshape(rows * W, C3) for _, s in sources for dy in range(3)
    ]
    k0 = sources[0][0]
    weights = w_ref[k0 * 3 * C3 : (k0 + len(sources)) * 3 * C3]
    out = jnp.dot(jnp.concatenate(parts, axis=1), weights, preferred_element_type=F32)
    return out.reshape(rows, W, COUT)


def first_kernel(frames_ref, x_ref, w_ref, xc, conv):
    first = lax.axis_index("tm") * F
    starts = clip_starts(frames_ref)
    own_columns(xc, x_ref, (0, 5))
    src = lambda f, k: source(starts, first, f, k) + 2
    conv[0, 1 : H - 1] = inner_taps(xc, w_ref, [(2, 2)])
    conv[1, 1 : H - 1] = inner_taps(xc, w_ref, [(1, src(1, 1)), (2, 3)])

    def step(f, carry):
        conv[f, 1 : H - 1] = inner_taps(xc, w_ref, [(0, src(f, 0)), (1, src(f, 1)), (2, f + 2)])
        return carry

    lax.fori_loop(2, 5, step, 0)


def second_kernel(frames_ref, x_ref, w_ref, xc_in, conv_in, xc, conv):
    del xc_in, conv_in
    first = lax.axis_index("tm") * F
    starts = clip_starts(frames_ref)
    own_columns(xc, x_ref, (5, 8))
    src = lambda f, k: source(starts, first, f, k) + 2

    def step(f, carry):
        conv[f, 1 : H - 1] = inner_taps(xc, w_ref, [(0, src(f, 0)), (1, src(f, 1)), (2, f + 2)])
        return carry

    lax.fori_loop(5, 8, step, 0)


def strip_kernel(x_ref, before, above, below, above_before, below_before, low_out, high_out):
    top, bottom, _, _ = edges()
    for out, at, pick in ((low_out, 0, 0), (high_out, W - 16, 15)):
        tile = lambda ref, f, r: ref[f, r, at : at + 16].astype(F32)[pick : pick + 1]
        for f in range(F + 2):
            own, over, under, g = (
                (before, above_before, below_before, f) if f < 2 else (x_ref, above, below, f - 2)
            )
            rows = [tile(own, g, r) for r in range(H)]
            head = jnp.where(top, rows[0], tile(over, g, 0))
            tail = jnp.where(bottom, rows[-1], tile(under, g, 0))
            pad = jnp.zeros((16 - H - 2, C), F32)
            out[f] = jnp.concatenate([head, *rows, tail, pad], axis=0).astype(BF)


def outer_kernel(
    frames_ref,
    w_ref,
    before,
    above,
    below,
    above_before,
    below_before,
    low_ref,
    high_ref,
    xc_in,
    conv_in,
    xc,
    conv,
    stats,
):
    del xc_in, conv_in
    first = lax.axis_index("tm") * F
    starts = clip_starts(frames_ref)
    top, bottom, left, right = edges()
    src = lambda f, k: source(starts, first, f, k) + 2
    tile_row = lax.broadcasted_iota(jnp.int32, (16, C), 0)

    def ends(ref, f, r):
        return ref[f].astype(F32)[r : r + 1]

    def fill_row(f, r, x):
        low = jnp.where(left, x[:1].astype(F32), ends(low_ref, f, r)).astype(BF)
        high = jnp.where(right, x[-1:].astype(F32), ends(high_ref, f, r)).astype(BF)
        put_columns(xc, (f, slice(r, r + 1)), x[None], low[None], high[None])

    for f in range(2):
        rows = [before[f, r] for r in range(H)]
        head = jnp.where(top, rows[0], above_before[f, 0])
        tail = jnp.where(bottom, rows[-1], below_before[f, 0])
        for r, x in enumerate([head, *rows, tail]):
            fill_row(f, r, x)
    for f in range(F):
        for r, edge, halo, own in ((0, top, above, 1), (H + 1, bottom, below, H)):
            fill_row(f + 2, r, jnp.where(edge, xc[f + 2, own, :, C : 2 * C], halo[f, 0]))
        for r in range(1, H + 1) if f < 2 else (1, 2, H - 1, H):
            low = xc[f + 2, r, 0:16, 0:C].astype(F32)
            low = jnp.where((tile_row == 0) & ~left, ends(low_ref, f + 2, r), low)
            xc[f + 2, r, 0:16, 0:C] = low.astype(BF)
            high = xc[f + 2, r, W - 16 : W, 2 * C : C3].astype(F32)
            high = jnp.where((tile_row == 15) & ~right, ends(high_ref, f + 2, r), high)
            xc[f + 2, r, W - 16 : W, 2 * C : C3] = high.astype(BF)

    def outer_rows(f, carry):
        parts = []
        for k in range(3):
            s = src(f, k)
            for dy in range(3):
                parts.append(jnp.concatenate([xc[s, dy], xc[s, H - 1 + dy]], axis=0))
        out = jnp.dot(jnp.concatenate(parts, axis=1), w_ref[...], preferred_element_type=F32)
        conv[f, 0] = out[:W]
        conv[f, H - 1] = out[W:]
        return carry

    lax.fori_loop(0, F, outer_rows, 0)
    conv[0, 1 : H - 1] += inner_taps(xc, w_ref, [(0, src(0, 0)), (1, src(0, 1))])
    conv[1, 1 : H - 1] += inner_taps(xc, w_ref, [(0, src(1, 0))])

    rows = H - 2
    sublane = lax.broadcasted_iota(jnp.int32, (8, COUT), 0)
    for ref, dx, at, pick in ((low_ref, 0, 0, 0), (high_ref, 2, W - 8, 7)):
        lhs = []
        for f in range(F):
            parts = []
            for k in range(3):
                strip = jnp.zeros((16, C), F32) if f + k < 2 else ref[src(f, k)].astype(F32)
                parts += [strip[1 + dy : 1 + dy + 8] for dy in range(3)]
            lhs.append(jnp.concatenate(parts, axis=1))
        lhs = jnp.concatenate(lhs, axis=0).astype(BF)
        weights = jnp.concatenate(
            [w_ref[(t * 3 + dx) * C : (t * 3 + dx + 1) * C] for t in range(9)], axis=0
        )
        out = jnp.dot(lhs, weights, preferred_element_type=F32)
        for f in range(F):
            for r in range(rows):
                add = out[f * 8 + r : f * 8 + r + 1]
                conv[f, 1 + r, at : at + 8] += jnp.where(sublane == pick, add, 0.0)

    def sums(f, carry):
        return jnp.where(
            frame_row == f, jnp.sum(conv[f].reshape(H * W, COUT), axis=0, keepdims=True), carry
        )

    frame_row = lax.broadcasted_iota(jnp.int32, (F, COUT), 0)
    zero = jnp.zeros((F, COUT), F32)
    totals = lax.fori_loop(0, F, sums, zero)
    channel = lax.broadcasted_iota(jnp.int32, (COUT, COUT), 0) // SHARE
    same_group = channel == lax.broadcasted_iota(jnp.int32, (COUT, COUT), 1) // SHARE
    grouped = jnp.dot(totals, same_group.astype(F32), precision=HIGH, preferred_element_type=F32)
    clip = clip_index(starts, first + frame_row)
    clip_sum, clip_count = zero, zero
    for f in range(F):
        same = clip == clip[f : f + 1]
        clip_sum = clip_sum + jnp.where(same, grouped[f : f + 1], 0.0)
        clip_count = clip_count + jnp.where(same, float(H * W * SHARE), 0.0)
    centre = clip_sum / clip_count

    def squares(f, carry):
        mean = jnp.sum(jnp.where(frame_row == f, centre, 0.0), axis=0, keepdims=True)
        off = conv[f].reshape(H * W, COUT) - mean
        return jnp.where(frame_row == f, jnp.sum(off * off, axis=0, keepdims=True), carry)

    spread = lax.fori_loop(0, F, squares, zero)
    lane = lax.broadcasted_iota(jnp.int32, (COUT, CLIPS * GROUPS), 1)
    pick = lax.broadcasted_iota(jnp.int32, (COUT, CLIPS * GROUPS), 0) // SHARE == lane % GROUPS
    mine = lax.broadcasted_iota(jnp.int32, (F, CLIPS * GROUPS), 1) // GROUPS
    mine = mine == clip[:, : CLIPS * GROUPS]
    for i, value in enumerate((totals, spread)):
        packed = jnp.dot(value, pick.astype(F32), precision=HIGH, preferred_element_type=F32)
        packed = jnp.sum(jnp.where(mine, packed, 0.0), axis=0, keepdims=True)
        stats[:, i * CLIPS * GROUPS : (i + 1) * CLIPS * GROUPS] = packed


def norm_kernel(cells, frames_ref, all_ref, gain, shift, conv, out_ref, held, sems):
    first = lax.axis_index("tm") * F
    starts = clip_starts(frames_ref)
    lanes = CLIPS * GROUPS
    count = all_ref.shape[0]
    value = all_ref[...]
    total, spread = value[:, :lanes], value[:, lanes:]
    which = lax.broadcasted_iota(jnp.int32, (count, lanes), 1) // GROUPS
    begin, length = jnp.zeros_like(which), jnp.zeros_like(which)
    for c in range(CLIPS):
        begin = jnp.where(which == c, starts[c], begin)
        length = jnp.where(which == c, frames_ref[c], length)
    slab = lax.broadcasted_iota(jnp.int32, (count, lanes), 0) // (count // lax.axis_size("tm")) * F
    part = jnp.minimum(slab + F, begin + length) - jnp.maximum(slab, begin)
    part = jnp.maximum(part, 0).astype(F32) * float(H * W * SHARE)
    whole = length[:1].astype(F32) * float(cells * SHARE)
    mean = jnp.sum(total, axis=0, keepdims=True) / whole
    off = total / jnp.maximum(part, 1.0) - mean
    var = jnp.sum(spread + part * (off * off), axis=0, keepdims=True) / whole
    var = var + 1e-06
    scale = lax.rsqrt(var)
    scale = scale * (1.5 - 0.5 * var * scale * scale)

    frame_row = lax.broadcasted_iota(jnp.int32, (F, lanes), 0)
    mine = clip_index(starts, first + frame_row)
    mine = mine == lax.broadcasted_iota(jnp.int32, (F, lanes), 1) // GROUPS
    lane = lax.broadcasted_iota(jnp.int32, (lanes, COUT), 0) % GROUPS
    spreadout = (lane == lax.broadcasted_iota(jnp.int32, (lanes, COUT), 1) // SHARE).astype(F32)

    def per_channel(v):
        v = jnp.where(mine, v, 0.0)
        return jnp.dot(v, spreadout, precision=HIGH, preferred_element_type=F32)

    mean, scale = per_channel(mean), per_channel(scale) * (0.5 * gain[...])
    half = 0.5 * shift[...]

    copies = []
    for f in range(F):

        def row(h, carry):
            u = (conv[f, h] - mean[f : f + 1]) * scale[f : f + 1] + half
            held[f, h] = (u + u * jnp.tanh(u)).astype(BF)
            return carry

        lax.fori_loop(0, H, row, 0)
        copy = pltpu.make_async_copy(held.at[f], out_ref.at[f], sems.at[f])
        copy.start()
        copies.append(copy)
    for copy in copies:
        copy.wait()


def params(mib):
    return pltpu.CompilerParams(vmem_limit_bytes=mib << 20)


def cost(flops, moved):
    return pl.CostEstimate(flops=flops, bytes_accessed=moved, transcendentals=0)


def shards(frames_in, clip_frames, conv_weight, norm_gain, norm_shift):
    n_tm, n_row, n_col = (lax.axis_size(a) for a in ("tm", "row", "col"))
    weights = conv_weight.reshape(27 * C, COUT)
    tail = frames_in[F - 2 :]
    before = lax.ppermute(tail, "tm", [(i, i + 1) for i in range(n_tm - 1)])
    down = [(i, i + 1) for i in range(n_row - 1)]
    up = [(i + 1, i) for i in range(n_row - 1)]
    above = lax.ppermute(frames_in[:, H - 1 :], "row", down)
    below = lax.ppermute(frames_in[:, :1], "row", up)

    def diagonal(pairs):
        return [
            (t * n_row + i, (t + 1) * n_row + j) for t in range(n_tm - 1) for i, j in pairs
        ]

    above_before = lax.ppermute(tail[:, H - 1 :], ("tm", "row"), diagonal(down))
    below_before = lax.ppermute(tail[:, :1], ("tm", "row"), diagonal(up))

    xc_shape = pltpu.VMEM((F + 2, H + 2, W, C3), BF)
    conv_shape = pltpu.VMEM((F, H, W, COUT), F32)
    macs = 6 * W * 3 * C3 * COUT
    xc, conv = pl.pallas_call(
        first_kernel,
        out_shape=(xc_shape, conv_shape),
        in_specs=[SMEM, VMEM, VMEM],
        out_specs=(VMEM, VMEM),
        compiler_params=params(20),
        cost_estimate=cost(2 * 12 * macs, 5 << 20),
        name="inner_first",
    )(clip_frames, frames_in, weights)
    low, high = pl.pallas_call(
        strip_kernel,
        out_shape=[jax.ShapeDtypeStruct((F + 2, 16, C), BF)] * 2,
        in_specs=[VMEM] * 6,
        out_specs=[VMEM] * 2,
        compiler_params=params(20),
        cost_estimate=cost(1 << 20, 1 << 16),
        name="strips",
    )(frames_in, before, above, below, above_before, below_before)
    from_left = lax.ppermute(high, "col", [(i, i + 1) for i in range(n_col - 1)])
    from_right = lax.ppermute(low, "col", [(i + 1, i) for i in range(n_col - 1)])
    xc, conv = pl.pallas_call(
        second_kernel,
        out_shape=(xc_shape, conv_shape),
        in_specs=[SMEM, VMEM, VMEM, VMEM, VMEM],
        out_specs=(VMEM, VMEM),
        input_output_aliases={3: 0, 4: 1},
        compiler_params=params(20),
        cost_estimate=cost(2 * 9 * macs, 5 << 20),
        name="inner_second",
    )(clip_frames, frames_in, weights, xc, conv)
    _, conv, stats = pl.pallas_call(
        outer_kernel,
        out_shape=(xc_shape, conv_shape, jax.ShapeDtypeStruct((1, 2 * CLIPS * GROUPS), F32)),
        in_specs=[SMEM] + [VMEM] * 10,
        out_specs=(VMEM, VMEM, VMEM),
        input_output_aliases={9: 0, 10: 1},
        compiler_params=params(24),
        cost_estimate=cost(2 * 12 * macs, 5 << 20),
        name="outer",
    )(
        clip_frames,
        weights,
        before,
        above,
        below,
        above_before,
        below_before,
        from_left,
        from_right,
        xc,
        conv,
    )
    count = n_tm * n_row * n_col
    every = jnp.broadcast_to(stats[None], (count, *stats.shape))
    every = lax.all_to_all(every, ("tm", "row", "col"), 0, 0).reshape(count, -1)
    return pl.pallas_call(
        functools.partial(norm_kernel, H * n_row * W * n_col),
        out_shape=jax.ShapeDtypeStruct((F, H, W, COUT), BF),
        in_specs=[SMEM] + [VMEM] * 4,
        out_specs=ANY,
        scratch_shapes=[pltpu.VMEM((F, H, W, COUT), BF), pltpu.SemaphoreType.DMA((F,))],
        compiler_params=params(24),
        cost_estimate=cost(1 << 24, 16 << 20),
        name="norm_silu",
    )(clip_frames, every, norm_gain[None], norm_shift[None], conv)


def solution(mesh):
    return jax.shard_map(
        shards,
        mesh=mesh,
        in_specs=(P("tm", "row", "col", None), P(), P(), P(), P()),
        out_specs=P("tm", "row", "col", None),
        check_vma=False,
    )
```

time: 251 us -> 92.7 us (0.37)
  blocking collectives: 132 us -> 20.4 us
  matrix products: 35 us -> 0 us
  Pallas kernels: 0 us -> 34.5 us
  other arithmetic: 25.8 us -> 0 us
  waiting for transfers between devices: 16.8 us -> 0.02 us
  local copies, waits for them, and re-layouts: 25.8 us -> 16.1 us
  starting transfers between devices: 13.9 us -> 21 us
    psum x2 -> x0, blocking collectives: 132 us -> none  [the longest x1 68.7 us: shards(): mean = lax.psum(local_sums, ('tm', 'row', 'col')) / count]
    pallas_call x0 -> x5, Pallas kernels: none -> 34.5 us  [the longest x1 13.5 us: shards(): pl.pallas_call(outer_kernel, out_shape=(xc_shape, conv_shape, jax.ShapeDt...]
    conv_general_dilated x3 -> x0, matrix products: 34.4 us -> none  [plane_conv(): lax.conv_general_dilated(frames, kernel, (1, 1), 'VALID', dimension_numbe...]
    all_to_all x0 -> x1, blocking collectives: none -> 20.4 us  [shards(): every = lax.all_to_all(every, ('tm', 'row', 'col'), 0, 0).reshape(count, -1)]
    ppermute x5 -> x7, waiting for transfers between devices: 16.8 us -> 0.02 us  [the longest x1 0.01 us: shards(): below_before = lax.ppermute(tail[:, :1], ('tm', 'row'), diagonal(up))]
    gather x3 -> x0, local copies, waits for them, and re-layouts: 13.3 us -> none  [shards(): conv = conv + plane_conv(jnp.take(padded, source, axis=0), conv_weight[tap])]
    unnamed x17 -> x19, local copies, waits for them, and re-layouts: 2.62 us -> 12.8 us
    concatenate x3 -> x0, other arithmetic: 7.3 us -> none  [the longest x1 3.37 us: with_halo(): block = jnp.concatenate([low, block, high], axis=dim)]
  transfers between devices with their start and end apart: 5 -> 7, of which waited for: 4 -> 0; matrix products, arithmetic and copies ran while one was open for 1% -> 2% of each run, Pallas kernels for 0% -> 18%
where the time goes in v1:
time: 92.7 us; the launch traced here: 92.2 us
  Pallas kernels  34.5 us (37%)
  starting transfers between devices  21 us (23%)
  blocking collectives  20.4 us (22%)
  local copies, waits for them, and re-layouts  16.1 us (17%)
    all_to_all x1, blocking collectives, shards(): every = lax.all_to_all(every, ('tm', 'row', 'col'), 0, 0).reshape(count, -1)  20.4 us
    pallas_call x1, Pallas kernels, shards(): pl.pallas_call(outer_kernel, out_shape=(xc_shape, conv_shape, jax.ShapeDt...  13.5 us
    unnamed x19, local copies, waits for them, and re-layouts  12.8 us
    pallas_call x1, Pallas kernels, shards(): pl.pallas_call(first_kernel, out_shape=(xc_shape, conv_shape), in_specs=[...  9.4 us
    pallas_call x1, Pallas kernels, shards(): pl.pallas_call(second_kernel, out_shape=(xc_shape, conv_shape), in_specs=...  7.02 us
    ppermute x1, starting transfers between devices, shards(): above_before = lax.ppermute(tail[:, H - 1:], ('tm', 'row'), diagonal(down))  6.49 us
    pallas_call x1, Pallas kernels, shards(): pl.pallas_call(functools.partial(norm_kernel, H * n_row * W * n_col), out...  4.53 us
    ppermute x1, starting transfers between devices, shards(): above = lax.ppermute(frames_in[:, H - 1:], 'row', down)  4.19 us
  transfers between devices with their start and end apart: 7, of which 0 were waited for; matrix products, arithmetic and copies ran while one was open for 2% of the time, Pallas kernels for 18%

profile of v1, /device:TPU:1, one launch (start us, length us, event | category | flops | bytes accessed | tf_op | source)
XLA Modules:
  0.0 92.2 jit_solution(9572909413512069672)
XLA Ops:
  0.0 0.9 %fusion = (bf16[2,1,160,128]{3,2,1,0:T(8,128)(2,1)S(1)}, bf16[2,1,160,128]{3,2,1,0:T(8,128)(2,1)S(1)}) fusion(bf16[8,8,160,128]{3,2,1,0:T(8,128)(2,1)} %x_ref.5), kind=kLoop, calls=%fused_computation.1 | loop fusion | bytes 327680 | tf_op jit(solution)/shard_map/slice | solution.py:318
  0.9 1.3 %collective-permute-start.4 = (bf16[2,1,160,128]{3,2,1,0:T(8,128)(2,1)S(1)}, bf16[2,1,160,128]{3,2,1,0:T(8,128)(2,1)S(1)}, u32[]{:S(2)}, u32[]{:S(2)}) collective-permute-start(bf16[2,1,160,128]{3,2,1,0:T(8,128)(2,1)S(1)} %get-tuple-element.21), channel_id=1, source_target_pairs={{4,16},{8,20},{12,24},{20,32},{24,36},{28,40},{36,48},{40,52},{44,... | collective-permute-start | bytes 245768 | tf_op jit(solution)/shard_map/ppermute | solution.py:318
  2.2 6.5 %collective-permute-start.3 = (bf16[2,1,160,128]{3,2,1,0:T(8,128)(2,1)S(1)}, bf16[2,1,160,128]{3,2,1,0:T(8,128)(2,1)S(1)}, u32[]{:S(2)}, u32[]{:S(2)}) collective-permute-start(bf16[2,1,160,128]{3,2,1,0:T(8,128)(2,1)S(1)} %get-tuple-element.22), channel_id=1, source_target_pairs={{0,20},{4,24},{8,28},{16,36},{20,40},{24,44},{32,52},{36,56},{40,6... | collective-permute-start | bytes 245768 | tf_op jit(solution)/shard_map/ppermute | solution.py:317
  8.7 1.1 %slice.17 = bf16[2,8,160,128]{3,2,1,0:T(8,128)(2,1)S(1)} slice(bf16[8,8,160,128]{3,2,1,0:T(8,128)(2,1)} %x_ref.5), slice={[6:8], [0:8], [0:160], [0:128]} | slice | bytes 1310720 | tf_op jit(solution)/shard_map/slice | solution.py:305
  9.9 3.2 %collective-permute-start = (bf16[2,8,160,128]{3,2,1,0:T(8,128)(2,1)S(1)}, bf16[2,8,160,128]{3,2,1,0:T(8,128)(2,1)S(1)}, u32[]{:S(2)}, u32[]{:S(2)}) collective-permute-start(bf16[2,8,160,128]{3,2,1,0:T(8,128)(2,1)S(1)} %slice.17), channel_id=1, source_target_pairs={{0,16},{16,32},{32,48},{48,64},{64,80},{80,96},{96,112},{1,17},{17... | collective-permute-start | bytes 1966088 | tf_op jit(solution)/shard_map/ppermute | solution.py:306
  13.1 1.1 %fusion.1 = (bf16[8,1,160,128]{3,2,1,0:T(8,128)(2,1)S(1)}, bf16[8,1,160,128]{3,2,1,0:T(8,128)(2,1)S(1)}) fusion(bf16[8,8,160,128]{3,2,1,0:T(8,128)(2,1)} %x_ref.5), kind=kLoop, calls=%fused_computation.2 | loop fusion | bytes 1310720 | tf_op jit(solution)/shard_map/slice | solution.py:310
  14.2 1.3 %collective-permute-start.2 = (bf16[8,1,160,128]{3,2,1,0:T(8,128)(2,1)S(1)}, bf16[8,1,160,128]{3,2,1,0:T(8,128)(2,1)S(1)}, u32[]{:S(2)}, u32[]{:S(2)}) collective-permute-start(bf16[8,1,160,128]{3,2,1,0:T(8,128)(2,1)S(1)} %get-tuple-element.23), channel_id=1, source_target_pairs={{4,0},{8,4},{12,8},{5,1},{9,5},{13,9},{6,2},{10,6},{14,10},{7,3},{... | collective-permute-start | bytes 983048 | tf_op jit(solution)/shard_map/ppermute | solution.py:310
  15.5 4.2 %collective-permute-start.1 = (bf16[8,1,160,128]{3,2,1,0:T(8,128)(2,1)S(1)}, bf16[8,1,160,128]{3,2,1,0:T(8,128)(2,1)S(1)}, u32[]{:S(2)}, u32[]{:S(2)}) collective-permute-start(bf16[8,1,160,128]{3,2,1,0:T(8,128)(2,1)S(1)} %get-tuple-element.24), channel_id=1, source_target_pairs={{0,4},{4,8},{8,12},{1,5},{5,9},{9,13},{2,6},{6,10},{10,14},{3,7},{... | collective-permute-start | bytes 983048 | tf_op jit(solution)/shard_map/ppermute | solution.py:309
  19.7 0.0 copy-start.2
  19.7 1.7 %copy-done.2 = bf16[8,8,160,128]{3,2,1,0:T(8,128)(2,1)S(1)} copy-done((bf16[8,8,160,128]{3,2,1,0:T(8,128)(2,1)S(1)}, bf16[8,8,160,128]{3,2,1,0:T(8,128)(2,1)}, u32[]{:S(2)}) %copy-start.2) | copy-done | bytes 2621464
  21.5 0.0 copy-start.3
  21.5 1.5 %copy-done.3 = bf16[3,3,3,128,256]{4,3,2,1,0:T(8,128)(2,1)S(1)} copy-done((bf16[3,3,3,128,256]{4,3,2,1,0:T(8,128)(2,1)S(1)}, bf16[3,3,3,128,256]{4,3,2,1,0:T(8,128)(2,1)}, u32[]{:S(2)}) %copy-start.3) | copy-done | bytes 1769496
  22.9 0.0 copy-start.5
  22.9 0.7 copy-done.5
  23.6 0.0 copy-start.4
  23.6 9.4 %inner_first.1 = (bf16[10,10,160,384]{3,2,1,0:T(8,128)(2,1)S(1)}, f32[8,8,160,256]{3,2,1,0:T(8,128)S(1)}) custom-call(s32[4]{0:T(128)S(1)} %copy-done.5, bf16[8,8,160,128]{3,2,1,0:T(8,128)(2,1)S(1)} %copy-done.2, bf16[3456,256]{1,0:T(8,128)(2,1)S(1)} %bitcast.7), custom_call_target="tpu_custom_call" | custom-call | flops 6794772480 | bytes 5242880 | tf_op jit(solution)/shard_map/inner_first/pallas_call | solution.py:323
  33.0 0.0 collective-permute-done.4.below_before
  33.0 0.0 collective-permute-done.3.above_before
  33.0 0.0 collective-permute-done.2.below
  33.0 0.0 collective-permute-done.1.above
  33.1 0.0 collective-permute-done.before
  33.1 0.1 strips.1
  33.2 3.2 %collective-permute-start.5 = (bf16[10,16,128]{2,1,0:T(8,128)(2,1)S(1)}, bf16[10,16,128]{2,1,0:T(8,128)(2,1)S(1)}, u32[]{:S(2)}, u32[]{:S(2)}) collective-permute-start(bf16[10,16,128]{2,1,0:T(8,128)(2,1)S(1)} %get-tuple-element.13), channel_id=1, source_target_pairs={{0,1},{1,2},{2,3},{4,5},{5,6},{6,7},{8,9},{9,10},{10,11},{12,13},{... | collective-permute-start | bytes 122888 | tf_op jit(solution)/shard_map/ppermute | solution.py:341
  36.4 1.3 %collective-permute-start.6 = (bf16[10,16,128]{2,1,0:T(8,128)(2,1)S(1)}, bf16[10,16,128]{2,1,0:T(8,128)(2,1)S(1)}, u32[]{:S(2)}, u32[]{:S(2)}) collective-permute-start(bf16[10,16,128]{2,1,0:T(8,128)(2,1)S(1)} %get-tuple-element.14), channel_id=1, source_target_pairs={{1,0},{2,1},{3,2},{5,4},{6,5},{7,6},{9,8},{10,9},{11,10},{13,12},{... | collective-permute-start | bytes 122888 | tf_op jit(solution)/shard_map/ppermute | solution.py:342
  37.7 0.0 copy-done.4
  37.7 0.0 copy-start.6
  37.7 7.0 %inner_second.1 = (bf16[10,10,160,384]{3,2,1,0:T(8,128)(2,1)S(1)}, f32[8,8,160,256]{3,2,1,0:T(8,128)S(1)}) custom-call(s32[4]{0:T(128)S(1)} %copy-done.5, bf16[8,8,160,128]{3,2,1,0:T(8,128)(2,1)S(1)} %copy-done.2, bf16[3456,256]{1,0:T(8,128)(2,1)S(1)} %bitcast.8, ...), custom_call_target="tpu_custom_call", output_to_operand_aliasing={{0}: (3, {}), {1}: (4, {})} | custom-call | flops 5096079360 | bytes 5242880 | tf_op jit(solution)/shard_map/inner_second/pallas_call | solution.py:343
  44.7 0.0 copy-start
  44.7 4.5 %copy-done = bf16[10,10,160,384]{3,2,1,0:T(8,128)(2,1)} copy-done((bf16[10,10,160,384]{3,2,1,0:T(8,128)(2,1)}, bf16[10,10,160,384]{3,2,1,0:T(8,128)(2,1)S(1)}, u32[]{:S(2)}) %copy-start) | copy-done | bytes 12288024
  49.2 0.0 collective-permute-done.5.low_ref
  49.2 0.0 collective-permute-done.6.high_ref
  49.2 0.0 copy-done.6
  49.2 0.0 copy-start.1
  49.2 4.5 %copy-done.1 = bf16[10,10,160,384]{3,2,1,0:T(8,128)(2,1)S(1)} copy-done((bf16[10,10,160,384]{3,2,1,0:T(8,128)(2,1)S(1)}, bf16[10,10,160,384]{3,2,1,0:T(8,128)(2,1)}, u32[]{:S(2)}) %copy-start.1) | copy-done | bytes 12288024
  53.7 0.0 copy-start.7
  53.7 0.0 copy-start.8
  53.7 13.5 %outer.1 = (bf16[10,10,160,384]{3,2,1,0:T(8,128)(2,1)S(1)}, f32[8,8,160,256]{3,2,1,0:T(8,128)S(1)}, f32[1,256]{1,0:T(1,128)S(1)}) custom-call(s32[4]{0:T(128)S(1)} %copy-done.6, bf16[3456,256]{1,0:T(8,128)(2,1)S(1)} %bitcast.9, bf16[2,8,160,128]{3,2,1,0:T(8,128)(2,1)S(1)} %collective-permute-done.before, ...), custom_call_target="tpu_custom_call", output_to_operand_aliasing={{0}: (9, {}), {1}: (10, {})} | custom-call | flops 6794772480 | bytes 5242880 | tf_op jit(solution)/shard_map/outer/pallas_call | solution.py:353
  67.2 0.1 broadcast_in_dim.15
  67.3 20.4 %all_to_all.5 = f32[128,1,256]{2,1,0:T(1,128)S(1)} all-to-all(f32[128,1,256]{2,1,0:T(1,128)S(1)} %broadcast_in_dim.15), channel_id=1, replica_groups=mesh['tm'=8,'row'=4,'col'=4] {'tm','row','col'}, dimensions={0} | all-to-all | bytes 262144 | tf_op jit(solution)/shard_map/all_to_all | solution.py:377
  87.7 0.0 copy-done.7
  87.7 0.0 copy-done.8
  87.7 4.5 %norm_silu.1 = bf16[8,8,160,256]{3,2,1,0:T(8,128)(2,1)} custom-call(s32[4]{0:T(128)S(1)} %copy-done.6, f32[128,256]{1,0:T(8,128)S(1)} %bitcast.10, f32[1,256]{1,0:T(1,128)S(1)} %bitcast.11, f32[1,256]{1,0:T(1,128)S(1)} %bitcast.12, f32[8,8,160,256]{3,2,1,0:T(8,128)S(1)} %get-tuple-element.20.conv), custom_call_target="tpu_custom_call" | custom-call | flops 16777216 | bytes 16777216 | tf_op jit(solution)/shard_map/norm_silu/pallas_call | solution.py:378
  (1 shorter events, 0.0 us)
Async XLA Ops:
  0.9 32.1 %collective-permute-start.4 = (bf16[2,1,160,128]{3,2,1,0:T(8,128)(2,1)S(1)}, bf16[2,1,160,128]{3,2,1,0:T(8,128)(2,1)S(1)}, u32[]{:S(2)}, u32[]{:S(2)}) collective-permute-start(bf16[2,1,160,128]{3,2,1,0:T(8,128)(2,1)S(1)} %get-tuple-element.21), channel_id=1, source_target_pairs={{4,16},{8,20},{12,24},{20,32},{24,36},{28,40},{36,48},{40,52},{44,... | collective-permute-start | bytes 245768 | tf_op jit(solution)/shard_map/ppermute | solution.py:318
  2.2 30.8 %collective-permute-start.3 = (bf16[2,1,160,128]{3,2,1,0:T(8,128)(2,1)S(1)}, bf16[2,1,160,128]{3,2,1,0:T(8,128)(2,1)S(1)}, u32[]{:S(2)}, u32[]{:S(2)}) collective-permute-start(bf16[2,1,160,128]{3,2,1,0:T(8,128)(2,1)S(1)} %get-tuple-element.22), channel_id=1, source_target_pairs={{0,20},{4,24},{8,28},{16,36},{20,40},{24,44},{32,52},{36,56},{40,6... | collective-permute-start | bytes 245768 | tf_op jit(solution)/shard_map/ppermute | solution.py:317
  9.9 23.2 %collective-permute-start = (bf16[2,8,160,128]{3,2,1,0:T(8,128)(2,1)S(1)}, bf16[2,8,160,128]{3,2,1,0:T(8,128)(2,1)S(1)}, u32[]{:S(2)}, u32[]{:S(2)}) collective-permute-start(bf16[2,8,160,128]{3,2,1,0:T(8,128)(2,1)S(1)} %slice.17), channel_id=1, source_target_pairs={{0,16},{16,32},{32,48},{48,64},{64,80},{80,96},{96,112},{1,17},{17... | collective-permute-start | bytes 1966088 | tf_op jit(solution)/shard_map/ppermute | solution.py:306
  14.2 18.8 %collective-permute-start.2 = (bf16[8,1,160,128]{3,2,1,0:T(8,128)(2,1)S(1)}, bf16[8,1,160,128]{3,2,1,0:T(8,128)(2,1)S(1)}, u32[]{:S(2)}, u32[]{:S(2)}) collective-permute-start(bf16[8,1,160,128]{3,2,1,0:T(8,128)(2,1)S(1)} %get-tuple-element.23), channel_id=1, source_target_pairs={{4,0},{8,4},{12,8},{5,1},{9,5},{13,9},{6,2},{10,6},{14,10},{7,3},{... | collective-permute-start | bytes 983048 | tf_op jit(solution)/shard_map/ppermute | solution.py:310
  15.5 17.5 %collective-permute-start.1 = (bf16[8,1,160,128]{3,2,1,0:T(8,128)(2,1)S(1)}, bf16[8,1,160,128]{3,2,1,0:T(8,128)(2,1)S(1)}, u32[]{:S(2)}, u32[]{:S(2)}) collective-permute-start(bf16[8,1,160,128]{3,2,1,0:T(8,128)(2,1)S(1)} %get-tuple-element.24), channel_id=1, source_target_pairs={{0,4},{4,8},{8,12},{1,5},{5,9},{9,13},{2,6},{6,10},{10,14},{3,7},{... | collective-permute-start | bytes 983048 | tf_op jit(solution)/shard_map/ppermute | solution.py:309
  19.7 1.7 %copy-start.2 = (bf16[8,8,160,128]{3,2,1,0:T(8,128)(2,1)S(1)}, bf16[8,8,160,128]{3,2,1,0:T(8,128)(2,1)}, u32[]{:S(2)}) copy-start(bf16[8,8,160,128]{3,2,1,0:T(8,128)(2,1)} %x_ref.5) | copy-start | bytes 7864324
  21.5 1.5 %copy-start.3 = (bf16[3,3,3,128,256]{4,3,2,1,0:T(8,128)(2,1)S(1)}, bf16[3,3,3,128,256]{4,3,2,1,0:T(8,128)(2,1)}, u32[]{:S(2)}) copy-start(bf16[3,3,3,128,256]{4,3,2,1,0:T(8,128)(2,1)} %param.7) | copy-start | bytes 5308420
  22.9 0.7 copy-start.5
  23.6 14.1 %copy-start.4 = (bf16[3,3,3,128,256]{4,3,2,1,0:T(8,128)(2,1)S(1)}, bf16[3,3,3,128,256]{4,3,2,1,0:T(8,128)(2,1)}, u32[]{:S(2)}) copy-start(bf16[3,3,3,128,256]{4,3,2,1,0:T(8,128)(2,1)} %param.7) | copy-start | bytes 5308420
  33.2 16.0 %collective-permute-start.5 = (bf16[10,16,128]{2,1,0:T(8,128)(2,1)S(1)}, bf16[10,16,128]{2,1,0:T(8,128)(2,1)S(1)}, u32[]{:S(2)}, u32[]{:S(2)}) collective-permute-start(bf16[10,16,128]{2,1,0:T(8,128)(2,1)S(1)} %get-tuple-element.13), channel_id=1, source_target_pairs={{0,1},{1,2},{2,3},{4,5},{5,6},{6,7},{8,9},{9,10},{10,11},{12,13},{... | collective-permute-start | bytes 122888 | tf_op jit(solution)/shard_map/ppermute | solution.py:341
  36.4 12.8 %collective-permute-start.6 = (bf16[10,16,128]{2,1,0:T(8,128)(2,1)S(1)}, bf16[10,16,128]{2,1,0:T(8,128)(2,1)S(1)}, u32[]{:S(2)}, u32[]{:S(2)}) collective-permute-start(bf16[10,16,128]{2,1,0:T(8,128)(2,1)S(1)} %get-tuple-element.14), channel_id=1, source_target_pairs={{1,0},{2,1},{3,2},{5,4},{6,5},{7,6},{9,8},{10,9},{11,10},{13,12},{... | collective-permute-start | bytes 122888 | tf_op jit(solution)/shard_map/ppermute | solution.py:342
  37.7 11.5 %copy-start.6 = (s32[4]{0:T(128)S(1)}, s32[4]{0:T(128)}, u32[]{:S(2)}) copy-start(s32[4]{0:T(128)} %frames_ref.7) | copy-start | bytes 52
  44.7 4.5 %copy-start = (bf16[10,10,160,384]{3,2,1,0:T(8,128)(2,1)}, bf16[10,10,160,384]{3,2,1,0:T(8,128)(2,1)S(1)}, u32[]{:S(2)}) copy-start(bf16[10,10,160,384]{3,2,1,0:T(8,128)(2,1)S(1)} %get-tuple-element.17.xc_in) | copy-start | bytes 36864004
  49.2 4.5 %copy-start.1 = (bf16[10,10,160,384]{3,2,1,0:T(8,128)(2,1)S(1)}, bf16[10,10,160,384]{3,2,1,0:T(8,128)(2,1)}, u32[]{:S(2)}) copy-start(bf16[10,10,160,384]{3,2,1,0:T(8,128)(2,1)} %copy-done) | copy-start | bytes 36864004
  53.7 34.0 %copy-start.7 = (f32[256]{0:T(256)S(1)}, f32[256]{0:T(256)}, u32[]{:S(2)}) copy-start(f32[256]{0:T(256)} %param.8) | copy-start | bytes 3076
  53.7 34.0 %copy-start.8 = (f32[256]{0:T(256)S(1)}, f32[256]{0:T(256)}, u32[]{:S(2)}) copy-start(f32[256]{0:T(256)} %param.9) | copy-start | bytes 3076

commit v2 on v1

v2 whole, which is shorter than its diff:
```python
import functools

import jax
import jax.numpy as jnp
from jax import lax
from jax.experimental import pallas as pl
from jax.experimental.pallas import tpu as pltpu
from jax.sharding import PartitionSpec as P

COUT = 256
GROUPS = 32
CLIPS = 4
SHARE = COUT // GROUPS
F, H, W, C = 8, 8, 160, 128
C3 = 3 * C
BF, F32 = jnp.bfloat16, jnp.float32
VMEM = pl.BlockSpec(memory_space=pltpu.VMEM)
SMEM = pl.BlockSpec(memory_space=pltpu.SMEM)
HBM = pl.BlockSpec(memory_space=pltpu.HBM)
HIGH = lax.Precision.HIGHEST


def clip_starts(frames_ref):
    starts = [0]
    for c in range(CLIPS - 1):
        starts.append(starts[-1] + frames_ref[c])
    return starts


def source(starts, first, f, k):
    g = first + f
    start = 0
    for s in starts[1:]:
        start = jnp.where(g >= s, s, start)
    return jnp.maximum(g - 2 + k, start) - first


def clip_index(starts, g):
    c = (g >= starts[1]).astype(jnp.int32)
    for s in starts[2:]:
        c = c + (g >= s).astype(jnp.int32)
    return c


def edges():
    row, col = lax.axis_index("row"), lax.axis_index("col")
    return row == 0, row == lax.axis_size("row") - 1, col == 0, col == lax.axis_size("col") - 1


def pack_kernel(x_ref, tail, top_row, bottom_row, tail_top, tail_bottom, sems):
    pairs = (
        (x_ref.at[:, H - 1], bottom_row),
        (x_ref.at[:, 0], top_row),
        (x_ref.at[F - 2 :], tail),
        (x_ref.at[F - 2 :, H - 1], tail_bottom),
        (x_ref.at[F - 2 :, 0], tail_top),
    )
    copies = [pltpu.make_async_copy(a, b, sems.at[i]) for i, (a, b) in enumerate(pairs)]
    for copy in copies:
        copy.start()
    for copy in copies:
        copy.wait()


def put_columns(xc, at, x):
    _, _, left, right = edges()
    low = jnp.where(left, x[:, :1], jnp.zeros_like(x[:, :1]))
    high = jnp.where(right, x[:, -1:], jnp.zeros_like(x[:, -1:]))
    xc[(*at, slice(None), slice(None), slice(0, C))] = jnp.concatenate([low, x[:, :-1]], axis=1)
    xc[(*at, slice(None), slice(None), slice(C, 2 * C))] = x
    xc[(*at, slice(None), slice(None), slice(2 * C, 3 * C))] = jnp.concatenate([x[:, 1:], high], axis=1)


def time_weights(w_ref, taps):
    return w_ref[taps[0] * 3 * C3 : (taps[-1] + 1) * 3 * C3]


def inner_taps(frames, row, rows, w_ref, taps):
    parts = [
        frame[row - 1 + dy : row - 1 + dy + rows].reshape(rows * W, C3)
        for frame in frames
        for dy in range(3)
    ]
    lhs = jnp.concatenate(parts, axis=1)
    out = jnp.dot(lhs, time_weights(w_ref, taps), preferred_element_type=F32)
    return out.reshape(rows, W, COUT)


def cell_sum(v):
    sublane = lax.broadcasted_iota(jnp.int32, (1, 8, COUT), 1)
    v = jnp.concatenate(
        [
            jnp.where(sublane > 0, v[:, :8], 0.0),
            v[:, 8:-8],
            jnp.where(sublane < 7, v[:, -8:], 0.0),
        ],
        axis=1,
    )
    return jnp.sum(v.reshape(-1, COUT), axis=0, keepdims=True)


def add_stats(stats, f, v):
    off = v - stats[f, 0:1]
    stats[f, 1:2] += cell_sum(off)
    stats[f, 2:3] += cell_sum(off * off)


def start_stats(stats, f, v):
    stats[f] = jnp.zeros((8, COUT), F32)
    stats[f, 0:1] = cell_sum(v) * (1.0 / (v.shape[0] * (W - 2)))
    add_stats(stats, f, v)


def inner_kernel(frames_ref, x_hbm, w_hbm, xc, conv, w_ref, stats, x_ref, x_sems, w_sem):
    first = lax.axis_index("tm") * F
    starts = clip_starts(frames_ref)
    x_copies = [pltpu.make_async_copy(x_hbm.at[f], x_ref.at[f], x_sems.at[f]) for f in range(F)]
    w_copy = pltpu.make_async_copy(w_hbm, w_ref, w_sem)
    for copy in (*x_copies[:2], w_copy, *x_copies[2:]):
        copy.start()
    for f in range(F):
        x_copies[f].wait()
        put_columns(xc, (f,), x_ref[f])
    w_copy.wait()
    for row in (1, 3, 5):
        conv[0, row : row + 2] = inner_taps([xc.at[0]], row, 2, w_ref, (2,))
        frames = [xc.at[source(starts, first, 1, 1)], xc.at[1]]
        conv[1, row : row + 2] = inner_taps(frames, row, 2, w_ref, (1, 2))

    def step(f, carry):
        frames = [xc.at[source(starts, first, f, k)] for k in range(2)] + [xc.at[f]]
        for row in (1, 3, 5):
            out = inner_taps(frames, row, 2, w_ref, (0, 1, 2))
            conv[f, row : row + 2] = out
            (start_stats if row == 1 else add_stats)(stats, f, out)
        return carry

    lax.fori_loop(2, F, step, 0)


def strip_kernel(xc, before, above, below, above_before, below_before, low_out, high_out):
    top, bottom, _, _ = edges()
    for out, at, pick in ((low_out, 0, 0), (high_out, W - 16, 15)):

        def tile(ref, *where):
            return ref[(*where, slice(at, at + 16))].astype(F32)[pick : pick + 1]

        for f in range(F + 2):
            if f < 2:
                rows = [tile(before, f, r) for r in range(H)]
                over, under = tile(above_before, f), tile(below_before, f)
            else:
                g = f - 2
                rows = [
                    xc[g, r, at : at + 16, C : 2 * C].astype(F32)[pick : pick + 1]
                    for r in range(H)
                ]
                over, under = tile(above, g), tile(below, g)
            head = jnp.where(top, rows[0], over)
            tail = jnp.where(bottom, rows[-1], under)
            pad = jnp.zeros((16 - H - 2, C), F32)
            out[f] = jnp.concatenate([head, *rows, tail, pad], axis=0).astype(BF)


def outer_kernel(
    frames_ref,
    w_ref,
    before,
    above,
    below,
    above_before,
    below_before,
    xc,
    conv_in,
    stats_in,
    conv,
    stats,
    early,
    rims,
):
    del conv_in, stats_in
    first = lax.axis_index("tm") * F
    starts = clip_starts(frames_ref)
    top, bottom, _, _ = edges()
    put_columns(early, (0,), before[0])
    put_columns(early, (1,), before[1])
    early[2] = xc[0]
    early[3] = xc[1]
    for f in range(F + 2):
        over, under = (above_before, below_before) if f < 2 else (above, below)
        g = f if f < 2 else f - 2
        own = before.at[f] if f < 2 else xc.at[g, :, :, C : 2 * C]
        rim = jnp.stack([jnp.where(top, own[0], over[g]), jnp.where(bottom, own[H - 1], under[g])])
        put_columns(rims, (f,), rim)

    def outer_rows(f, frame_of):
        parts = []
        for k in range(3):
            s = source(starts, first, f, k)
            frame = frame_of(s)
            upper = [rims[s + 2, 0], frame[0], frame[1]]
            lower = [frame[H - 2], frame[H - 1], rims[s + 2, 1]]
            parts += [jnp.concatenate([u, v], axis=0) for u, v in zip(upper, lower)]
        lhs = jnp.concatenate(parts, axis=1)
        out = jnp.dot(lhs, w_ref[...], preferred_element_type=F32).reshape(2, W, COUT)
        conv[f, 0] = out[0]
        conv[f, H - 1] = out[1]
        return out

    for f, taps in ((0, (0, 1)), (1, (0,))):
        frame_of = lambda s: early.at[s + 2]
        start_stats(stats, f, outer_rows(f, frame_of))
        frames = [frame_of(source(starts, first, f, k)) for k in taps]
        for row in (1, 3, 5):
            out = conv[f, row : row + 2] + inner_taps(frames, row, 2, w_ref, taps)
            conv[f, row : row + 2] = out
            add_stats(stats, f, out)

    def step(f, carry):
        add_stats(stats, f, outer_rows(f, lambda s: xc.at[s]))
        return carry

    lax.fori_loop(2, F, step, 0)


def column_kernel(frames_ref, w_ref, low_ref, high_ref, stats_ref, conv_in, conv, sums):
    del conv_in
    first = lax.axis_index("tm") * F
    starts = clip_starts(frames_ref)
    _, _, left, right = edges()
    total, square = [], []
    pivot = jnp.concatenate([stats_ref[f, 0:1] for f in range(F)], axis=0)
    total = jnp.concatenate([stats_ref[f, 1:2] for f in range(F)], axis=0)
    square = jnp.concatenate([stats_ref[f, 2:3] for f in range(F)], axis=0)
    for ref, edge, dx, at in ((low_ref, left, 0, 0), (high_ref, right, 2, W - 1)):
        lhs = []
        for f in range(F):
            parts = []
            for k in range(3):
                strip = ref[source(starts, first, f, k) + 2].astype(F32)
                strip = jnp.where(edge, 0.0, strip)
                parts += [strip[dy : dy + H] for dy in range(3)]
            lhs.append(jnp.concatenate(parts, axis=1))
        lhs = jnp.concatenate(lhs, axis=0).astype(BF)
        weights = jnp.concatenate(
            [w_ref[(t * 3 + dx) * C : (t * 3 + dx + 1) * C] for t in range(9)], axis=0
        )
        out = jnp.dot(lhs, weights, preferred_element_type=F32)
        added, added_square = [], []
        for f in range(F):
            column = jnp.concatenate([conv[f, r, at : at + 1] for r in range(H)], axis=0)
            column = column + out[f * H : (f + 1) * H]
            for r in range(H):
                conv[f, r, at : at + 1] = column[r : r + 1]
            off = column - pivot[f : f + 1]
            added.append(jnp.sum(off, axis=0, keepdims=True))
            added_square.append(jnp.sum(off * off, axis=0, keepdims=True))
        total = total + jnp.concatenate(added, axis=0)
        square = square + jnp.concatenate(added_square, axis=0)

    cells = float(H * W)
    mean = pivot + total * (1.0 / cells)
    square = square - total * total * (1.0 / cells)
    channel = lax.broadcasted_iota(jnp.int32, (COUT, COUT), 0) // SHARE
    same_group = channel == lax.broadcasted_iota(jnp.int32, (COUT, COUT), 1) // SHARE
    grouped = jnp.dot(mean, same_group.astype(F32), precision=HIGH, preferred_element_type=F32)
    frame_row = lax.broadcasted_iota(jnp.int32, (F, COUT), 0)
    clip = clip_index(starts, first + frame_row)
    clip_sum = clip_count = jnp.zeros((F, COUT), F32)
    for f in range(F):
        same = clip == clip[f : f + 1]
        clip_sum = clip_sum + jnp.where(same, grouped[f : f + 1], 0.0)
        clip_count = clip_count + jnp.where(same, float(SHARE), 0.0)
    centre = clip_sum / clip_count
    off = mean - centre
    square = square + cells * (off * off)
    lane = lax.broadcasted_iota(jnp.int32, (COUT, CLIPS * GROUPS), 1)
    pick = lax.broadcasted_iota(jnp.int32, (COUT, CLIPS * GROUPS), 0) // SHARE == lane % GROUPS
    mine = lax.broadcasted_iota(jnp.int32, (F, CLIPS * GROUPS), 1) // GROUPS
    mine = mine == clip[:, : CLIPS * GROUPS]
    for i, value in enumerate((mean * cells, square)):
        packed = jnp.dot(value, pick.astype(F32), precision=HIGH, preferred_element_type=F32)
        packed = jnp.sum(jnp.where(mine, packed, 0.0), axis=0, keepdims=True)
        sums[:, i * CLIPS * GROUPS : (i + 1) * CLIPS * GROUPS] = packed


def norm_kernel(cells, frames_ref, all_ref, gain, shift, conv, out_ref, held, sems):
    first = lax.axis_index("tm") * F
    starts = clip_starts(frames_ref)
    lanes = CLIPS * GROUPS
    count = all_ref.shape[0]
    value = all_ref[...]
    total, spread = value[:, :lanes], value[:, lanes:]
    which = lax.broadcasted_iota(jnp.int32, (count, lanes), 1) // GROUPS
    begin, length = jnp.zeros_like(which), jnp.zeros_like(which)
    for c in range(CLIPS):
        begin = jnp.where(which == c, starts[c], begin)
        length = jnp.where(which == c, frames_ref[c], length)
    slab = lax.broadcasted_iota(jnp.int32, (count, lanes), 0) // (count // lax.axis_size("tm")) * F
    part = jnp.minimum(slab + F, begin + length) - jnp.maximum(slab, begin)
    part = jnp.maximum(part, 0).astype(F32) * float(H * W * SHARE)
    whole = length[:1].astype(F32) * float(cells * SHARE)
    mean = jnp.sum(total, axis=0, keepdims=True) / whole
    off = total / jnp.maximum(part, 1.0) - mean
    var = jnp.sum(spread + part * (off * off), axis=0, keepdims=True) / whole
    var = var + 1e-06
    scale = lax.rsqrt(var)
    scale = scale * (1.5 - 0.5 * var * scale * scale)

    frame_row = lax.broadcasted_iota(jnp.int32, (F, lanes), 0)
    mine = clip_index(starts, first + frame_row)
    mine = mine == lax.broadcasted_iota(jnp.int32, (F, lanes), 1) // GROUPS
    lane = lax.broadcasted_iota(jnp.int32, (lanes, COUT), 0) % GROUPS
    spreadout = (lane == lax.broadcasted_iota(jnp.int32, (lanes, COUT), 1) // SHARE).astype(F32)

    def per_channel(v):
        v = jnp.where(mine, v, 0.0)
        return jnp.dot(v, spreadout, precision=HIGH, preferred_element_type=F32)

    mean, scale = per_channel(mean), per_channel(scale) * (0.5 * gain[...])
    half = 0.5 * shift[...]

    copies = []
    for f in range(F):

        def row(h, carry):
            u = (conv[f, h] - mean[f : f + 1]) * scale[f : f + 1] + half
            held[f, h] = (u + u * jnp.tanh(u)).astype(BF)
            return carry

        lax.fori_loop(0, H, row, 0)
        copy = pltpu.make_async_copy(held.at[f], out_ref.at[f], sems.at[f])
        copy.start()
        copies.append(copy)
    for copy in copies:
        copy.wait()


def params(mib):
    return pltpu.CompilerParams(vmem_limit_bytes=mib << 20)


def cost(flops, moved):
    return pl.CostEstimate(flops=flops, bytes_accessed=moved, transcendentals=0)


def shards(frames_in, clip_frames, conv_weight, norm_gain, norm_shift):
    n_tm, n_row, n_col = (lax.axis_size(a) for a in ("tm", "row", "col"))
    weights = conv_weight.reshape(27 * C, COUT)
    tail, top_row, bottom_row, tail_top, tail_bottom = pl.pallas_call(
        pack_kernel,
        out_shape=[pltpu.VMEM((2, H, W, C), BF)]
        + [pltpu.VMEM((F, W, C), BF)] * 2
        + [pltpu.VMEM((2, W, C), BF)] * 2,
        in_specs=[HBM],
        out_specs=[VMEM] * 5,
        scratch_shapes=[pltpu.SemaphoreType.DMA((5,))],
        compiler_params=params(8),
        name="pack",
    )(frames_in)
    down = [(i, (i + 1) % n_row) for i in range(n_row)]
    up = [(j, i) for i, j in down]
    later = [(t, (t + 1) % n_tm) for t in range(n_tm)]

    def diagonal(pairs):
        return [(t * n_row + i, u * n_row + j) for t, u in later for i, j in pairs]

    above = lax.ppermute(bottom_row, "row", down)
    below = lax.ppermute(top_row, "row", up)
    before = lax.ppermute(tail, "tm", later)
    above_before = lax.ppermute(tail_bottom, ("tm", "row"), diagonal(down))
    below_before = lax.ppermute(tail_top, ("tm", "row"), diagonal(up))

    conv_shape = pltpu.VMEM((F, H, W, COUT), F32)
    stats_shape = pltpu.VMEM((F, 8, COUT), F32)
    macs = W * 9 * C3 * COUT
    xc, conv, weights, stats = pl.pallas_call(
        inner_kernel,
        out_shape=(
            pltpu.VMEM((F, H, W, C3), BF),
            conv_shape,
            pltpu.VMEM((27 * C, COUT), BF),
            stats_shape,
        ),
        in_specs=[SMEM, HBM, HBM],
        out_specs=[VMEM] * 4,
        scratch_shapes=[
            pltpu.VMEM((F, H, W, C), BF),
            pltpu.SemaphoreType.DMA((F,)),
            pltpu.SemaphoreType.DMA,
        ],
        compiler_params=params(16),
        cost_estimate=cost(2 * 42 * macs, 5 << 20),
        name="inner",
    )(clip_frames, frames_in, weights)
    low, high = pl.pallas_call(
        strip_kernel,
        out_shape=[pltpu.VMEM((F + 2, 16, C), BF)] * 2,
        in_specs=[VMEM] * 6,
        out_specs=[VMEM] * 2,
        compiler_params=params(8),
        cost_estimate=cost(1 << 20, 1 << 16),
        name="strips",
    )(xc, before, above, below, above_before, below_before)
    onward = [(i, (i + 1) % n_col) for i in range(n_col)]
    from_left = lax.ppermute(high, "col", onward)
    from_right = lax.ppermute(low, "col", [(j, i) for i, j in onward])
    conv, stats = pl.pallas_call(
        outer_kernel,
        out_shape=(conv_shape, stats_shape),
        in_specs=[SMEM] + [VMEM] * 9,
        out_specs=[VMEM] * 2,
        input_output_aliases={8: 0, 9: 1},
        scratch_shapes=[
            pltpu.VMEM((4, H, W, C3), BF),
            pltpu.VMEM((F + 2, 2, W, C3), BF),
        ],
        compiler_params=params(18),
        cost_estimate=cost(2 * 22 * macs, 5 << 20),
        name="outer",
    )(clip_frames, weights, before, above, below, above_before, below_before, xc, conv, stats)
    conv, stats = pl.pallas_call(
        column_kernel,
        out_shape=(conv_shape, jax.ShapeDtypeStruct((1, 2 * CLIPS * GROUPS), F32)),
        in_specs=[SMEM] + [VMEM] * 5,
        out_specs=[VMEM] * 2,
        input_output_aliases={5: 0},
        compiler_params=params(12),
        cost_estimate=cost(1 << 27, 1 << 20),
        name="columns",
    )(clip_frames, weights, from_left, from_right, stats, conv)
    count = n_tm * n_row * n_col
    every = jnp.broadcast_to(stats[None], (count, *stats.shape))
    every = lax.all_to_all(every, ("tm", "row", "col"), 0, 0).reshape(count, -1)
    return pl.pallas_call(
        functools.partial(norm_kernel, H * n_row * W * n_col),
        out_shape=jax.ShapeDtypeStruct((F, H, W, COUT), BF),
        in_specs=[SMEM] + [VMEM] * 4,
        out_specs=HBM,
        scratch_shapes=[pltpu.VMEM((F, H, W, COUT), BF), pltpu.SemaphoreType.DMA((F,))],
        compiler_params=params(12),
        cost_estimate=cost(1 << 24, 16 << 20),
        name="norm_silu",
    )(clip_frames, every, norm_gain[None], norm_shift[None], conv)


def solution(mesh):
    return jax.shard_map(
        shards,
        mesh=mesh,
        in_specs=(P("tm", "row", "col", None), P(), P(), P(), P()),
        out_specs=P("tm", "row", "col", None),
        check_vma=False,
    )
```

time: 92.7 us -> 68.3 us (0.74)
  local copies, waits for them, and re-layouts: 16.1 us -> 5.72 us
  starting transfers between devices: 21 us -> 12.9 us
  blocking collectives: 20.4 us -> 15.4 us
    ppermute x7, starting transfers between devices: 21 us -> 12.9 us  [the longest x1 4.02 us: shards(): above_before = lax.ppermute(tail_bottom, ('tm', 'row'), diagonal(down))]
    unnamed x19 -> x15, local copies, waits for them, and re-layouts: 12.8 us -> 5.64 us
    all_to_all x1, blocking collectives: 20.4 us -> 15.4 us  [shards(): every = lax.all_to_all(every, ('tm', 'row', 'col'), 0, 0).reshape(count, -1)]
    slice x3 -> x0, local copies, waits for them, and re-layouts: 3.2 us -> none  [the longest x1 1.13 us: shards(): tail = frames_in[F - 2:]]
    pallas_call x4 -> x5, Pallas kernels: 30 us -> 29.2 us  [the longest x1 17.3 us: shards(): pl.pallas_call(inner_kernel, out_shape=(pltpu.VMEM((F, H, W, C3), BF), co...]
  transfers between devices with their start and end apart: 7 -> 7, of which waited for: 0 -> 0; matrix products, arithmetic and copies ran while one was open for 2% -> 0% of each run, Pallas kernels for 18% -> 40%
where the time goes in v2:
time: 68.3 us; the launch traced here: 68.1 us
  Pallas kernels  33.8 us (49%)
  blocking collectives  15.4 us (23%)
  starting transfers between devices  12.9 us (19%)
  local copies, waits for them, and re-layouts  5.72 us (8%)
    pallas_call x1, Pallas kernels, shards(): pl.pallas_call(inner_kernel, out_shape=(pltpu.VMEM((F, H, W, C3), BF), co...  17.3 us
    all_to_all x1, blocking collectives, shards(): every = lax.all_to_all(every, ('tm', 'row', 'col'), 0, 0).reshape(count, -1)  15.4 us
    pallas_call x1, Pallas kernels, shards(): pl.pallas_call(outer_kernel, out_shape=(conv_shape, stats_shape), in_spec...  9.87 us
    unnamed x15, local copies, waits for them, and re-layouts  5.64 us
    pallas_call x1, Pallas kernels, shards(): pl.pallas_call(functools.partial(norm_kernel, H * n_row * W * n_col), out...  4.53 us
    ppermute x1, starting transfers between devices, shards(): above_before = lax.ppermute(tail_bottom, ('tm', 'row'), diagonal(down))  4.02 us
    ppermute x1, starting transfers between devices, shards(): below = lax.ppermute(top_row, 'row', up)  2.67 us
    ppermute x1, starting transfers between devices, shards(): below_before = lax.ppermute(tail_top, ('tm', 'row'), diagonal(up))  2.2 us
  transfers between devices with their start and end apart: 7, of which 0 were waited for; matrix products, arithmetic and copies ran while one was open for 0% of the time, Pallas kernels for 40%

profile of v2, /device:TPU:1, one launch (start us, length us, event | category | flops | bytes accessed | tf_op | source)
XLA Modules:
  0.0 68.1 jit_solution(17537559238707451830)
XLA Ops:
  0.0 0.0 copy-start
  0.0 1.7 %copy-done = bf16[8,8,160,128]{3,2,1,0:T(8,128)(2,1)S(1)} copy-done((bf16[8,8,160,128]{3,2,1,0:T(8,128)(2,1)S(1)}, bf16[8,8,160,128]{3,2,1,0:T(8,128)(2,1)}, u32[]{:S(2)}) %copy-start) | copy-done | bytes 2621464
  1.7 0.4 pack.1
  2.2 4.0 %collective-permute-start.3 = (bf16[2,160,128]{2,1,0:T(8,128)(2,1)S(1)}, bf16[2,160,128]{2,1,0:T(8,128)(2,1)S(1)}, u32[]{:S(2)}, u32[]{:S(2)}) collective-permute-start(bf16[2,160,128]{2,1,0:T(8,128)(2,1)S(1)} %get-tuple-element.25), channel_id=1, source_target_pairs={{0,20},{4,24},{8,28},{12,16},{16,36},{20,40},{24,44},{28,32},{32,5... | collective-permute-start | bytes 245768 | tf_op jit(solution)/shard_map/ppermute | solution.py:371
  6.2 2.2 %collective-permute-start.4 = (bf16[2,160,128]{2,1,0:T(8,128)(2,1)S(1)}, bf16[2,160,128]{2,1,0:T(8,128)(2,1)S(1)}, u32[]{:S(2)}, u32[]{:S(2)}) collective-permute-start(bf16[2,160,128]{2,1,0:T(8,128)(2,1)S(1)} %get-tuple-element.26), channel_id=1, source_target_pairs={{4,16},{8,20},{12,24},{0,28},{20,32},{24,36},{28,40},{16,44},{36,4... | collective-permute-start | bytes 245768 | tf_op jit(solution)/shard_map/ppermute | solution.py:372
  8.4 0.0 collective-permute-start.1
  8.4 2.7 %collective-permute-start.2 = (bf16[8,160,128]{2,1,0:T(8,128)(2,1)S(1)}, bf16[8,160,128]{2,1,0:T(8,128)(2,1)S(1)}, u32[]{:S(2)}, u32[]{:S(2)}) collective-permute-start(bf16[8,160,128]{2,1,0:T(8,128)(2,1)S(1)} %get-tuple-element.24), channel_id=1, source_target_pairs={{4,0},{8,4},{12,8},{0,12},{5,1},{9,5},{13,9},{1,13},{6,2},{10,6},{... | collective-permute-start | bytes 983048 | tf_op jit(solution)/shard_map/ppermute | solution.py:369
  11.1 0.9 %collective-permute-start = (bf16[2,8,160,128]{3,2,1,0:T(8,128)(2,1)S(1)}, bf16[2,8,160,128]{3,2,1,0:T(8,128)(2,1)S(1)}, u32[]{:S(2)}, u32[]{:S(2)}) collective-permute-start(bf16[2,8,160,128]{3,2,1,0:T(8,128)(2,1)S(1)} %get-tuple-element.22), channel_id=1, source_target_pairs={{0,16},{16,32},{32,48},{48,64},{64,80},{80,96},{96,112},{112,0},{1... | collective-permute-start | bytes 1966088 | tf_op jit(solution)/shard_map/ppermute | solution.py:370
  12.0 0.0 copy-start.1
  12.0 1.7 %copy-done.1 = bf16[8,8,160,128]{3,2,1,0:T(8,128)(2,1)S(1)} copy-done((bf16[8,8,160,128]{3,2,1,0:T(8,128)(2,1)S(1)}, bf16[8,8,160,128]{3,2,1,0:T(8,128)(2,1)}, u32[]{:S(2)}) %copy-start.1) | copy-done | bytes 2621464
  13.7 0.0 copy-start.2
  13.7 0.7 copy-done.2
  14.4 0.0 copy-start.6
  14.4 1.5 %copy-done.6 = bf16[3,3,3,128,256]{4,3,2,1,0:T(8,128)(2,1)S(1)} copy-done((bf16[3,3,3,128,256]{4,3,2,1,0:T(8,128)(2,1)S(1)}, bf16[3,3,3,128,256]{4,3,2,1,0:T(8,128)(2,1)}, u32[]{:S(2)}) %copy-start.6) | copy-done | bytes 1769496
  15.8 17.3 %inner.1 = (bf16[8,8,160,384]{3,2,1,0:T(8,128)(2,1)S(1)}, f32[8,8,160,256]{3,2,1,0:T(8,128)S(1)}, bf16[3456,256]{1,0:T(8,128)(2,1)S(1)}, f32[8,8,256]{2,1,0:T(8,128)S(1)}) custom-call(s32[4]{0:T(128)S(1)} %copy-done.2, bf16[8,8,160,128]{3,2,1,0:T(8,128)(2,1)S(1)} %copy-done.1, bf16[3456,256]{1,0:T(8,128)(2,1)S(1)} %bitcast.11), custom_call_target="tpu_custom_call" | custom-call | flops 11890851840 | bytes 5242880 | tf_op jit(solution)/shard_map/inner/pallas_call | solution.py:377
  33.2 0.0 copy-start.3
  33.2 0.0 collective-permute-done.3.above_before
  33.2 0.0 collective-permute-done.4.below_before
  33.2 0.0 collective-permute-done.1.above
  33.2 0.0 collective-permute-done.2.below
  33.2 0.0 collective-permute-done.before
  33.2 0.1 strips.1
  33.3 1.4 %collective-permute-start.5 = (bf16[10,16,128]{2,1,0:T(8,128)(2,1)S(1)}, bf16[10,16,128]{2,1,0:T(8,128)(2,1)S(1)}, u32[]{:S(2)}, u32[]{:S(2)}) collective-permute-start(bf16[10,16,128]{2,1,0:T(8,128)(2,1)S(1)} %get-tuple-element.27), channel_id=1, source_target_pairs={{0,1},{1,2},{2,3},{3,0},{4,5},{5,6},{6,7},{7,4},{8,9},{9,10},{10,1... | collective-permute-start | bytes 122888 | tf_op jit(solution)/shard_map/ppermute | solution.py:406
  34.7 1.7 %collective-permute-start.6 = (bf16[10,16,128]{2,1,0:T(8,128)(2,1)S(1)}, bf16[10,16,128]{2,1,0:T(8,128)(2,1)S(1)}, u32[]{:S(2)}, u32[]{:S(2)}) collective-permute-start(bf16[10,16,128]{2,1,0:T(8,128)(2,1)S(1)} %get-tuple-element.28), channel_id=1, source_target_pairs={{1,0},{2,1},{3,2},{0,3},{5,4},{6,5},{7,6},{4,7},{9,8},{10,9},{11,1... | collective-permute-start | bytes 122888 | tf_op jit(solution)/shard_map/ppermute | solution.py:407
  36.4 0.0 copy-done.3
  36.4 9.9 %outer.1 = (f32[8,8,160,256]{3,2,1,0:T(8,128)S(1)}, f32[8,8,256]{2,1,0:T(8,128)S(1)}) custom-call(s32[4]{0:T(128)S(1)} %copy-done.3, bf16[3456,256]{1,0:T(8,128)(2,1)S(1)} %get-tuple-element.20.w_ref, bf16[2,8,160,128]{3,2,1,0:T(8,128)(2,1)S(1)} %collective-permute-done.before, ...), custom_call_target="tpu_custom_call", output_to_operand_aliasing={{0}: (8, {}), {1}: (9, {})} | custom-call | flops 6228541440 | bytes 5242880 | tf_op jit(solution)/shard_map/outer/pallas_call | solution.py:408
  46.3 0.0 copy-start.4
  46.3 0.0 copy-start.5
  46.3 0.0 collective-permute-done.5.low_ref
  46.3 0.0 collective-permute-done.6.high_ref
  46.3 1.5 %columns.1 = (f32[8,8,160,256]{3,2,1,0:T(8,128)S(1)}, f32[1,256]{1,0:T(1,128)S(1)}) custom-call(s32[4]{0:T(128)S(1)} %copy-done.3, bf16[3456,256]{1,0:T(8,128)(2,1)S(1)} %get-tuple-element.20.w_ref, bf16[10,16,128]{2,1,0:T(8,128)(2,1)S(1)} %collective-permute-done.5.low_ref, ...), custom_call_target="tpu_custom_call", output_to_operand_aliasing={{0}: (5, {})} | custom-call | flops 134217728 | bytes 1048576 | tf_op jit(solution)/shard_map/columns/pallas_call | solution.py:422
  47.9 0.1 broadcast_in_dim.15
  48.0 15.4 %all_to_all.5 = f32[128,1,256]{2,1,0:T(1,128)S(1)} all-to-all(f32[128,1,256]{2,1,0:T(1,128)S(1)} %broadcast_in_dim.15), channel_id=1, replica_groups=mesh['tm'=8,'row'=4,'col'=4] {'tm','row','col'}, dimensions={0} | all-to-all | bytes 262144 | tf_op jit(solution)/shard_map/all_to_all | solution.py:434
  63.4 0.0 copy-done.4
  63.4 0.0 copy-done.5
  63.4 4.5 %norm_silu.1 = bf16[8,8,160,256]{3,2,1,0:T(8,128)(2,1)} custom-call(s32[4]{0:T(128)S(1)} %copy-done.3, f32[128,256]{1,0:T(8,128)S(1)} %bitcast.7, f32[1,256]{1,0:T(1,128)S(1)} %bitcast.8, f32[1,256]{1,0:T(1,128)S(1)} %bitcast.9, f32[8,8,160,256]{3,2,1,0:T(8,128)S(1)} %get-tuple-element.34.conv), custom_call_target="tpu_custom_call" | custom-call | flops 16777216 | bytes 16777216 | tf_op jit(solution)/shard_map/norm_silu/pallas_call | solution.py:435
  (1 shorter events, 0.0 us)
Async XLA Ops:
  0.0 1.7 %copy-start = (bf16[8,8,160,128]{3,2,1,0:T(8,128)(2,1)S(1)}, bf16[8,8,160,128]{3,2,1,0:T(8,128)(2,1)}, u32[]{:S(2)}) copy-start(bf16[8,8,160,128]{3,2,1,0:T(8,128)(2,1)} %x_ref.1) | copy-start | bytes 7864324
  2.2 31.0 %collective-permute-start.3 = (bf16[2,160,128]{2,1,0:T(8,128)(2,1)S(1)}, bf16[2,160,128]{2,1,0:T(8,128)(2,1)S(1)}, u32[]{:S(2)}, u32[]{:S(2)}) collective-permute-start(bf16[2,160,128]{2,1,0:T(8,128)(2,1)S(1)} %get-tuple-element.25), channel_id=1, source_target_pairs={{0,20},{4,24},{8,28},{12,16},{16,36},{20,40},{24,44},{28,32},{32,5... | collective-permute-start | bytes 245768 | tf_op jit(solution)/shard_map/ppermute | solution.py:371
  6.2 27.0 %collective-permute-start.4 = (bf16[2,160,128]{2,1,0:T(8,128)(2,1)S(1)}, bf16[2,160,128]{2,1,0:T(8,128)(2,1)S(1)}, u32[]{:S(2)}, u32[]{:S(2)}) collective-permute-start(bf16[2,160,128]{2,1,0:T(8,128)(2,1)S(1)} %get-tuple-element.26), channel_id=1, source_target_pairs={{4,16},{8,20},{12,24},{0,28},{20,32},{24,36},{28,40},{16,44},{36,4... | collective-permute-start | bytes 245768 | tf_op jit(solution)/shard_map/ppermute | solution.py:372
  8.4 24.8 %collective-permute-start.1 = (bf16[8,160,128]{2,1,0:T(8,128)(2,1)S(1)}, bf16[8,160,128]{2,1,0:T(8,128)(2,1)S(1)}, u32[]{:S(2)}, u32[]{:S(2)}) collective-permute-start(bf16[8,160,128]{2,1,0:T(8,128)(2,1)S(1)} %get-tuple-element.23), channel_id=1, source_target_pairs={{0,4},{4,8},{8,12},{12,0},{1,5},{5,9},{9,13},{13,1},{2,6},{6,10},{... | collective-permute-start | bytes 983048 | tf_op jit(solution)/shard_map/ppermute | solution.py:368
  8.4 24.8 %collective-permute-start.2 = (bf16[8,160,128]{2,1,0:T(8,128)(2,1)S(1)}, bf16[8,160,128]{2,1,0:T(8,128)(2,1)S(1)}, u32[]{:S(2)}, u32[]{:S(2)}) collective-permute-start(bf16[8,160,128]{2,1,0:T(8,128)(2,1)S(1)} %get-tuple-element.24), channel_id=1, source_target_pairs={{4,0},{8,4},{12,8},{0,12},{5,1},{9,5},{13,9},{1,13},{6,2},{10,6},{... | collective-permute-start | bytes 983048 | tf_op jit(solution)/shard_map/ppermute | solution.py:369
  11.1 22.2 %collective-permute-start = (bf16[2,8,160,128]{3,2,1,0:T(8,128)(2,1)S(1)}, bf16[2,8,160,128]{3,2,1,0:T(8,128)(2,1)S(1)}, u32[]{:S(2)}, u32[]{:S(2)}) collective-permute-start(bf16[2,8,160,128]{3,2,1,0:T(8,128)(2,1)S(1)} %get-tuple-element.22), channel_id=1, source_target_pairs={{0,16},{16,32},{32,48},{48,64},{64,80},{80,96},{96,112},{112,0},{1... | collective-permute-start | bytes 1966088 | tf_op jit(solution)/shard_map/ppermute | solution.py:370
  12.0 1.7 %copy-start.1 = (bf16[8,8,160,128]{3,2,1,0:T(8,128)(2,1)S(1)}, bf16[8,8,160,128]{3,2,1,0:T(8,128)(2,1)}, u32[]{:S(2)}) copy-start(bf16[8,8,160,128]{3,2,1,0:T(8,128)(2,1)} %x_ref.1) | copy-start | bytes 7864324
  13.7 0.7 copy-start.2
  14.4 1.5 %copy-start.6 = (bf16[3,3,3,128,256]{4,3,2,1,0:T(8,128)(2,1)S(1)}, bf16[3,3,3,128,256]{4,3,2,1,0:T(8,128)(2,1)}, u32[]{:S(2)}) copy-start(bf16[3,3,3,128,256]{4,3,2,1,0:T(8,128)(2,1)} %param.7) | copy-start | bytes 5308420
  33.2 3.2 %copy-start.3 = (s32[4]{0:T(128)S(1)}, s32[4]{0:T(128)}, u32[]{:S(2)}) copy-start(s32[4]{0:T(128)} %frames_ref.7) | copy-start | bytes 52
  33.3 13.0 %collective-permute-start.5 = (bf16[10,16,128]{2,1,0:T(8,128)(2,1)S(1)}, bf16[10,16,128]{2,1,0:T(8,128)(2,1)S(1)}, u32[]{:S(2)}, u32[]{:S(2)}) collective-permute-start(bf16[10,16,128]{2,1,0:T(8,128)(2,1)S(1)} %get-tuple-element.27), channel_id=1, source_target_pairs={{0,1},{1,2},{2,3},{3,0},{4,5},{5,6},{6,7},{7,4},{8,9},{9,10},{10,1... | collective-permute-start | bytes 122888 | tf_op jit(solution)/shard_map/ppermute | solution.py:406
  34.7 11.6 %collective-permute-start.6 = (bf16[10,16,128]{2,1,0:T(8,128)(2,1)S(1)}, bf16[10,16,128]{2,1,0:T(8,128)(2,1)S(1)}, u32[]{:S(2)}, u32[]{:S(2)}) collective-permute-start(bf16[10,16,128]{2,1,0:T(8,128)(2,1)S(1)} %get-tuple-element.28), channel_id=1, source_target_pairs={{1,0},{2,1},{3,2},{0,3},{5,4},{6,5},{7,6},{4,7},{9,8},{10,9},{11,1... | collective-permute-start | bytes 122888 | tf_op jit(solution)/shard_map/ppermute | solution.py:407
  46.3 17.1 %copy-start.4 = (f32[256]{0:T(256)S(1)}, f32[256]{0:T(256)}, u32[]{:S(2)}) copy-start(f32[256]{0:T(256)} %param.8) | copy-start | bytes 3076
  46.3 17.1 %copy-start.5 = (f32[256]{0:T(256)S(1)}, f32[256]{0:T(256)}, u32[]{:S(2)}) copy-start(f32[256]{0:T(256)} %param.9) | copy-start | bytes 3076

commit v3 on v2

--- a/solution.py
+++ b/solution.py
@@ -17,7 +17,6 @@
 VMEM = pl.BlockSpec(memory_space=pltpu.VMEM)
 SMEM = pl.BlockSpec(memory_space=pltpu.SMEM)
 HBM = pl.BlockSpec(memory_space=pltpu.HBM)
-HIGH = lax.Precision.HIGHEST
 
 
 def clip_starts(frames_ref):
@@ -45,21 +44,6 @@
 def edges():
     row, col = lax.axis_index("row"), lax.axis_index("col")
     return row == 0, row == lax.axis_size("row") - 1, col == 0, col == lax.axis_size("col") - 1
-
-
-def pack_kernel(x_ref, tail, top_row, bottom_row, tail_top, tail_bottom, sems):
-    pairs = (
-        (x_ref.at[:, H - 1], bottom_row),
-        (x_ref.at[:, 0], top_row),
-        (x_ref.at[F - 2 :], tail),
-        (x_ref.at[F - 2 :, H - 1], tail_bottom),
-        (x_ref.at[F - 2 :, 0], tail_top),
-    )
-    copies = [pltpu.make_async_copy(a, b, sems.at[i]) for i, (a, b) in enumerate(pairs)]
-    for copy in copies:
-        copy.start()
-    for copy in copies:
-        copy.wait()
 
 
 def put_columns(xc, at, x):
@@ -77,13 +61,24 @@
 
 def inner_taps(frames, row, rows, w_ref, taps):
     parts = [
-        frame[row - 1 + dy : row - 1 + dy + rows].reshape(rows * W, C3)
+        frame[pl.ds(row - 1 + dy, rows)].reshape(rows * W, C3)
         for frame in frames
         for dy in range(3)
     ]
     lhs = jnp.concatenate(parts, axis=1)
     out = jnp.dot(lhs, time_weights(w_ref, taps), preferred_element_type=F32)
     return out.reshape(rows, W, COUT)
+
+
+def times_zero_one(v, chosen):
+    parts = []
+    for _ in range(3):
+        parts.append(v.astype(BF))
+        v = v - parts[-1].astype(F32)
+    out = jnp.dot(
+        jnp.concatenate(parts, axis=0), chosen.astype(BF), preferred_element_type=F32
+    ).reshape(3, v.shape[0], -1)
+    return out[0] + (out[1] + out[2])
 
 
 def cell_sum(v):
@@ -111,31 +106,58 @@
     add_stats(stats, f, v)
 
 
-def inner_kernel(frames_ref, x_hbm, w_hbm, xc, conv, w_ref, stats, x_ref, x_sems, w_sem):
+def load_kernel(
+    frames_ref, x_hbm, w_hbm, tail, top_row, bottom_row, tail_top, tail_bottom, xc, w_ref, clips, x_ref, x_sems, w_sem
+):
+    for c in range(CLIPS):
+        clips[c] = frames_ref[c]
+
+    def x_copy(f):
+        return pltpu.make_async_copy(x_hbm.at[f], x_ref.at[f], x_sems.at[f])
+
+    for f in range(F):
+        x_copy(f).start()
+    w_copy = pltpu.make_async_copy(w_hbm, w_ref, w_sem)
+    w_copy.start()
+
+    def columns(f, carry):
+        x_copy(f).wait()
+        top_row[f] = x_ref[f, 0]
+        bottom_row[f] = x_ref[f, H - 1]
+        put_columns(xc, (f,), x_ref[f])
+        return carry
+
+    lax.fori_loop(0, F, columns, 0)
+    tail[...] = x_ref[F - 2 :]
+    tail_top[...] = x_ref[F - 2 :, 0]
+    tail_bottom[...] = x_ref[F - 2 :, H - 1]
+    w_copy.wait()
+
+
+def inner_kernel(frames_ref, xc, w_ref, conv, stats):
     first = lax.axis_index("tm") * F
     starts = clip_starts(frames_ref)
-    x_copies = [pltpu.make_async_copy(x_hbm.at[f], x_ref.at[f], x_sems.at[f]) for f in range(F)]
-    w_copy = pltpu.make_async_copy(w_hbm, w_ref, w_sem)
-    for copy in (*x_copies[:2], w_copy, *x_copies[2:]):
-        copy.start()
-    for f in range(F):
-        x_copies[f].wait()
-        put_columns(xc, (f,), x_ref[f])
-    w_copy.wait()
-    for row in (1, 3, 5):
-        conv[0, row : row + 2] = inner_taps([xc.at[0]], row, 2, w_ref, (2,))
+
+    def first_frames(i, carry):
+        row = 1 + 2 * i
+        conv[0, pl.ds(row, 2)] = inner_taps([xc.at[0]], row, 2, w_ref, (2,))
         frames = [xc.at[source(starts, first, 1, 1)], xc.at[1]]
-        conv[1, row : row + 2] = inner_taps(frames, row, 2, w_ref, (1, 2))
-
-    def step(f, carry):
-        frames = [xc.at[source(starts, first, f, k)] for k in range(2)] + [xc.at[f]]
-        for row in (1, 3, 5):
-            out = inner_taps(frames, row, 2, w_ref, (0, 1, 2))
-            conv[f, row : row + 2] = out
-            (start_stats if row == 1 else add_stats)(stats, f, out)
-        return carry
-
-    lax.fori_loop(2, F, step, 0)
+        conv[1, pl.ds(row, 2)] = inner_taps(frames, row, 2, w_ref, (1, 2))
+        return carry
+
+    lax.fori_loop(0, 3, first_frames, 0, unroll=3)
+
+    def step(i, carry):
+        for j in range(3):
+            f = 2 + 3 * i + j
+            frames = [xc.at[source(starts, first, f, k)] for k in range(2)] + [xc.at[f]]
+            for row in (1, 3, 5):
+                out = inner_taps(frames, row, 2, w_ref, (0, 1, 2))
+                conv[f, row : row + 2] = out
+                (start_stats if row == 1 else add_stats)(stats, f, out)
+        return carry
+
+    lax.fori_loop(0, (F - 2) // 3, step, 0)
 
 
 def strip_kernel(xc, before, above, below, above_before, below_before, low_out, high_out):
@@ -176,30 +198,37 @@
     conv,
     stats,
     early,
+    early_rims,
     rims,
 ):
     del conv_in, stats_in
     first = lax.axis_index("tm") * F
     starts = clip_starts(frames_ref)
     top, bottom, _, _ = edges()
-    put_columns(early, (0,), before[0])
-    put_columns(early, (1,), before[1])
-    early[2] = xc[0]
-    early[3] = xc[1]
-    for f in range(F + 2):
-        over, under = (above_before, below_before) if f < 2 else (above, below)
-        g = f if f < 2 else f - 2
-        own = before.at[f] if f < 2 else xc.at[g, :, :, C : 2 * C]
-        rim = jnp.stack([jnp.where(top, own[0], over[g]), jnp.where(bottom, own[H - 1], under[g])])
-        put_columns(rims, (f,), rim)
-
-    def outer_rows(f, frame_of):
+
+    def fill_rims(ref, at, own, over, under):
+        rim = jnp.stack([jnp.where(top, own[0], over), jnp.where(bottom, own[H - 1], under)])
+        put_columns(ref, (at,), rim)
+
+    for f in range(F):
+        fill_rims(rims, f, xc.at[f, :, :, C : 2 * C], above[f], below[f])
+
+    def fill_early(i):
+        if i == 2:
+            for f in range(2):
+                early[2 + f] = xc[f]
+                early_rims[2 + f] = rims[f]
+        else:
+            put_columns(early, (i,), before[i])
+            fill_rims(early_rims, i, before.at[i], above_before[i], below_before[i])
+
+    def outer_rows(f, place, frames, edge):
         parts = []
         for k in range(3):
-            s = source(starts, first, f, k)
-            frame = frame_of(s)
-            upper = [rims[s + 2, 0], frame[0], frame[1]]
-            lower = [frame[H - 2], frame[H - 1], rims[s + 2, 1]]
+            s = source(starts, first, f, k) + place
+            frame, rim = frames.at[s], edge.at[s]
+            upper = [rim[0], frame[0], frame[1]]
+            lower = [frame[H - 2], frame[H - 1], rim[1]]
             parts += [jnp.concatenate([u, v], axis=0) for u, v in zip(upper, lower)]
         lhs = jnp.concatenate(parts, axis=1)
         out = jnp.dot(lhs, w_ref[...], preferred_element_type=F32).reshape(2, W, COUT)
@@ -207,20 +236,29 @@
         conv[f, H - 1] = out[1]
         return out
 
-    for f, taps in ((0, (0, 1)), (1, (0,))):
-        frame_of = lambda s: early.at[s + 2]
-        start_stats(stats, f, outer_rows(f, frame_of))
-        frames = [frame_of(source(starts, first, f, k)) for k in taps]
-        for row in (1, 3, 5):
-            out = conv[f, row : row + 2] + inner_taps(frames, row, 2, w_ref, taps)
-            conv[f, row : row + 2] = out
+    def step(i, carry):
+        for j in range(6):
+            f = 2 + 6 * i + j
+            add_stats(stats, f, outer_rows(f, 0, xc, rims))
+        return carry
+
+    fill_early(0)
+    fill_early(1)
+    fill_early(2)
+    lax.fori_loop(0, (F - 2) // 6, step, 0)
+    for f in range(2):
+        start_stats(stats, f, outer_rows(f, 2, early, early_rims))
+
+    def first_frames(i, carry):
+        row = 1 + 2 * i
+        for f, taps in ((0, (0, 1)), (1, (0,))):
+            frames = [early.at[source(starts, first, f, k) + 2] for k in taps]
+            out = conv[f, pl.ds(row, 2)] + inner_taps(frames, row, 2, w_ref, taps)
+            conv[f, pl.ds(row, 2)] = out
             add_stats(stats, f, out)
-
-    def step(f, carry):
-        add_stats(stats, f, outer_rows(f, lambda s: xc.at[s]))
-        return carry
-
-    lax.fori_loop(2, F, step, 0)
+        return carry
+
+    lax.fori_loop(0, 3, first_frames, 0, unroll=3)
 
 
 def column_kernel(frames_ref, w_ref, low_ref, high_ref, stats_ref, conv_in, conv, sums):
@@ -263,7 +301,7 @@
     square = square - total * total * (1.0 / cells)
     channel = lax.broadcasted_iota(jnp.int32, (COUT, COUT), 0) // SHARE
     same_group = channel == lax.broadcasted_iota(jnp.int32, (COUT, COUT), 1) // SHARE
-    grouped = jnp.dot(mean, same_group.astype(F32), precision=HIGH, preferred_element_type=F32)
+    grouped = times_zero_one(mean, same_group)
     frame_row = lax.broadcasted_iota(jnp.int32, (F, COUT), 0)
     clip = clip_index(starts, first + frame_row)
     clip_sum = clip_count = jnp.zeros((F, COUT), F32)
@@ -278,13 +316,14 @@
     pick = lax.broadcasted_iota(jnp.int32, (COUT, CLIPS * GROUPS), 0) // SHARE == lane % GROUPS
     mine = lax.broadcasted_iota(jnp.int32, (F, CLIPS * GROUPS), 1) // GROUPS
     mine = mine == clip[:, : CLIPS * GROUPS]
-    for i, value in enumerate((mean * cells, square)):
-        packed = jnp.dot(value, pick.astype(F32), precision=HIGH, preferred_element_type=F32)
-        packed = jnp.sum(jnp.where(mine, packed, 0.0), axis=0, keepdims=True)
-        sums[:, i * CLIPS * GROUPS : (i + 1) * CLIPS * GROUPS] = packed
-
-
-def norm_kernel(cells, frames_ref, all_ref, gain, shift, conv, out_ref, held, sems):
+    packed = times_zero_one(jnp.concatenate([mean * cells, square], axis=0), pick)
+    for i in range(2):
+        value = jnp.where(mine, packed[i * F : (i + 1) * F], 0.0)
+        value = jnp.sum(value, axis=0, keepdims=True)
+        sums[:, i * CLIPS * GROUPS : (i + 1) * CLIPS * GROUPS] = value
+
+
+def norm_kernel(cells, frames_ref, all_ref, gain, shift, conv, out_ref, held, sems, per_frame):
     first = lax.axis_index("tm") * F
     starts = clip_starts(frames_ref)
     lanes = CLIPS * GROUPS
@@ -311,29 +350,28 @@
     mine = clip_index(starts, first + frame_row)
     mine = mine == lax.broadcasted_iota(jnp.int32, (F, lanes), 1) // GROUPS
     lane = lax.broadcasted_iota(jnp.int32, (lanes, COUT), 0) % GROUPS
-    spreadout = (lane == lax.broadcasted_iota(jnp.int32, (lanes, COUT), 1) // SHARE).astype(F32)
-
-    def per_channel(v):
-        v = jnp.where(mine, v, 0.0)
-        return jnp.dot(v, spreadout, precision=HIGH, preferred_element_type=F32)
-
-    mean, scale = per_channel(mean), per_channel(scale) * (0.5 * gain[...])
+    chosen = lane == lax.broadcasted_iota(jnp.int32, (lanes, COUT), 1) // SHARE
+    both = [jnp.where(mine, v, 0.0) for v in (mean, scale)]
+    both = times_zero_one(jnp.concatenate(both, axis=0), chosen)
+    mean, scale = both[:F], both[F:] * (0.5 * gain[...])
     half = 0.5 * shift[...]
 
-    copies = []
+    def out_copy(f):
+        return pltpu.make_async_copy(held.at[f], out_ref.at[f], sems.at[f])
+
     for f in range(F):
-
-        def row(h, carry):
-            u = (conv[f, h] - mean[f : f + 1]) * scale[f : f + 1] + half
+        per_frame[f] = jnp.concatenate([mean[f : f + 1], scale[f : f + 1], half], axis=0)
+
+    def frame(f, carry):
+        for h in range(H):
+            u = (conv[f, h] - per_frame[f, 0:1]) * per_frame[f, 1:2] + per_frame[f, 2:3]
             held[f, h] = (u + u * jnp.tanh(u)).astype(BF)
-            return carry
-
-        lax.fori_loop(0, H, row, 0)
-        copy = pltpu.make_async_copy(held.at[f], out_ref.at[f], sems.at[f])
-        copy.start()
-        copies.append(copy)
-    for copy in copies:
-        copy.wait()
+        out_copy(f).start()
+        return carry
+
+    lax.fori_loop(0, F, frame, 0)
+    for f in range(F):
+        out_copy(f).wait()
 
 
 def params(mib):
@@ -347,17 +385,23 @@
 def shards(frames_in, clip_frames, conv_weight, norm_gain, norm_shift):
     n_tm, n_row, n_col = (lax.axis_size(a) for a in ("tm", "row", "col"))
     weights = conv_weight.reshape(27 * C, COUT)
-    tail, top_row, bottom_row, tail_top, tail_bottom = pl.pallas_call(
-        pack_kernel,
+    tail, top_row, bottom_row, tail_top, tail_bottom, xc, weights, clips = pl.pallas_call(
+        load_kernel,
         out_shape=[pltpu.VMEM((2, H, W, C), BF)]
         + [pltpu.VMEM((F, W, C), BF)] * 2
-        + [pltpu.VMEM((2, W, C), BF)] * 2,
-        in_specs=[HBM],
-        out_specs=[VMEM] * 5,
-        scratch_shapes=[pltpu.SemaphoreType.DMA((5,))],
-        compiler_params=params(8),
-        name="pack",
-    )(frames_in)
+        + [pltpu.VMEM((2, W, C), BF)] * 2
+        + [pltpu.VMEM((F, H, W, C3), BF), pltpu.VMEM((27 * C, COUT), BF)]
+        + [pltpu.SMEM((CLIPS,), jnp.int32)],
+        in_specs=[SMEM] + [HBM] * 2,
+        out_specs=[VMEM] * 7 + [SMEM],
+        scratch_shapes=[
+            pltpu.VMEM((F, H, W, C), BF),
+            pltpu.SemaphoreType.DMA((F,)),
+            pltpu.SemaphoreType.DMA,
+        ],
+        compiler_params=params(52),
+        name="load",
+    )(clip_frames, frames_in, weights)
     down = [(i, (i + 1) % n_row) for i in range(n_row)]
     up = [(j, i) for i, j in down]
     later = [(t, (t + 1) % n_tm) for t in range(n_tm)]
@@ -374,25 +418,15 @@
     conv_shape = pltpu.VMEM((F, H, W, COUT), F32)
     stats_shape = pltpu.VMEM((F, 8, COUT), F32)
     macs = W * 9 * C3 * COUT
-    xc, conv, weights, stats = pl.pallas_call(
+    conv, stats = pl.pallas_call(
         inner_kernel,
-        out_shape=(
-            pltpu.VMEM((F, H, W, C3), BF),
-            conv_shape,
-            pltpu.VMEM((27 * C, COUT), BF),
-            stats_shape,
-        ),
-        in_specs=[SMEM, HBM, HBM],
-        out_specs=[VMEM] * 4,
-        scratch_shapes=[
-            pltpu.VMEM((F, H, W, C), BF),
-            pltpu.SemaphoreType.DMA((F,)),
-            pltpu.SemaphoreType.DMA,
-        ],
-        compiler_params=params(16),
+        out_shape=(conv_shape, stats_shape),
+        in_specs=[SMEM, VMEM, VMEM],
+        out_specs=[VMEM] * 2,
+        compiler_params=params(12),
         cost_estimate=cost(2 * 42 * macs, 5 << 20),
         name="inner",
-    )(clip_frames, frames_in, weights)
+    )(clips, xc, weights)
     low, high = pl.pallas_call(
         strip_kernel,
         out_shape=[pltpu.VMEM((F + 2, 16, C), BF)] * 2,
@@ -413,7 +447,8 @@
         input_output_aliases={8: 0, 9: 1},
         scratch_shapes=[
             pltpu.VMEM((4, H, W, C3), BF),
-            pltpu.VMEM((F + 2, 2, W, C3), BF),
+            pltpu.VMEM((4, 2, W, C3), BF),
+            pltpu.VMEM((F, 2, W, C3), BF),
         ],
         compiler_params=params(18),
         cost_estimate=cost(2 * 22 * macs, 5 << 20),
@@ -437,7 +472,11 @@
         out_shape=jax.ShapeDtypeStruct((F, H, W, COUT), BF),
         in_specs=[SMEM] + [VMEM] * 4,
         out_specs=HBM,
-        scratch_shapes=[pltpu.VMEM((F, H, W, COUT), BF), pltpu.SemaphoreType.DMA((F,))],
+        scratch_shapes=[
+            pltpu.VMEM((F, H, W, COUT), BF),
+            pltpu.SemaphoreType.DMA((F,)),
+            pltpu.VMEM((F, 3, COUT), F32),
+        ],
         compiler_params=params(12),
         cost_estimate=cost(1 << 24, 16 << 20),
         name="norm_silu",

time: 68.3 us -> 59.5 us (0.87)
  local copies, waits for them, and re-layouts: 5.72 us -> 0.1 us
  Pallas kernels: 33.8 us -> 30.6 us
    unnamed x15 -> x7, local copies, waits for them, and re-layouts: 5.64 us -> 0.03 us
    ppermute x1, starting transfers between devices: 4.02 us -> 0.01 us  [shards(): above_before = lax.ppermute(tail_bottom, ('tm', 'row'), diagonal(down))]
    ppermute x1, starting transfers between devices: 0.89 us -> 2.61 us  [shards(): before = lax.ppermute(tail, 'tm', later)]
    ppermute x1, starting transfers between devices: 2.2 us -> 3.88 us  [shards(): below_before = lax.ppermute(tail_top, ('tm', 'row'), diagonal(up))]
    ppermute x1, starting transfers between devices: 0.01 us -> 1.64 us  [shards(): above = lax.ppermute(bottom_row, 'row', down)]
    pallas_call x1, Pallas kernels: 9.87 us -> 8.58 us  [shards(): pl.pallas_call(outer_kernel, out_shape=(conv_shape, stats_shape), in_spec...]
    pallas_call x2, Pallas kernels: 17.8 us -> 16.7 us  [the longest x1 13.2 us: shards(): pl.pallas_call(inner_kernel, out_shape=(conv_shape, stats_shape), in_spec...]
  transfers between devices with their start and end apart: 7 -> 7, of which waited for: 0 -> 0; matrix products, arithmetic and copies ran while one was open for 0% -> 0% of each run, Pallas kernels for 40% -> 37%
where the time goes in v3:
time: 59.5 us; the launch traced here: 59.3 us
  Pallas kernels  30.6 us (51%)
  blocking collectives  15 us (25%)
  starting transfers between devices  13.3 us (22%)
    all_to_all x1, blocking collectives, shards(): every = lax.all_to_all(every, ('tm', 'row', 'col'), 0, 0).reshape(count, -1)  15 us
    pallas_call x1, Pallas kernels, shards(): pl.pallas_call(inner_kernel, out_shape=(conv_shape, stats_shape), in_spec...  13.2 us
    pallas_call x1, Pallas kernels, shards(): pl.pallas_call(outer_kernel, out_shape=(conv_shape, stats_shape), in_spec...  8.58 us
    pallas_call x1, Pallas kernels, shards(): pl.pallas_call(functools.partial(norm_kernel, H * n_row * W * n_col), out...  3.95 us
    ppermute x1, starting transfers between devices, shards(): below_before = lax.ppermute(tail_top, ('tm', 'row'), diagonal(up))  3.88 us
    pallas_call x1, Pallas kernels, shards(): pl.pallas_call(load_kernel, out_shape=[pltpu.VMEM((2, H, W, C), BF)] + [p...  3.59 us
    ppermute x1, starting transfers between devices, shards(): before = lax.ppermute(tail, 'tm', later)  2.61 us
    ppermute x1, starting transfers between devices, shards(): below = lax.ppermute(top_row, 'row', up)  2.12 us
  transfers between devices with their start and end apart: 7, of which 0 were waited for; matrix products, arithmetic and copies ran while one was open for 0% of the time, Pallas kernels for 37%

profile of v3, /device:TPU:1, one launch (start us, length us, event | category | flops | bytes accessed | tf_op | source)
XLA Modules:
  0.0 59.3 jit_solution(11610017750746613083)
XLA Ops:
  0.0 3.6 %load.1 = (bf16[2,8,160,128]{3,2,1,0:T(8,128)(2,1)S(1)}, bf16[8,160,128]{2,1,0:T(8,128)(2,1)S(1)}, bf16[8,160,128]{2,1,0:T(8,128)(2,1)S(1)}, bf16[2,160,128]{2,1...) custom-call(s32[4]{0:T(128)} %frames_ref.7, ...), custom_call_target="tpu_custom_call" | custom-call | tf_op jit(solution)/shard_map/load/pallas_call | solution.py:388
  3.6 2.6 %collective-permute-start = (bf16[2,8,160,128]{3,2,1,0:T(8,128)(2,1)S(1)}, bf16[2,8,160,128]{3,2,1,0:T(8,128)(2,1)S(1)}, u32[]{:S(2)}, u32[]{:S(2)}) collective-permute-start(bf16[2,8,160,128]{3,2,1,0:T(8,128)(2,1)S(1)} %get-tuple-element.23), channel_id=1, source_target_pairs={{0,16},{16,32},{32,48},{48,64},{64,80},{80,96},{96,112},{112,0},{1... | collective-permute-start | bytes 1966088 | tf_op jit(solution)/shard_map/ppermute | solution.py:414
  6.2 1.6 %collective-permute-start.1 = (bf16[8,160,128]{2,1,0:T(8,128)(2,1)S(1)}, bf16[8,160,128]{2,1,0:T(8,128)(2,1)S(1)}, u32[]{:S(2)}, u32[]{:S(2)}) collective-permute-start(bf16[8,160,128]{2,1,0:T(8,128)(2,1)S(1)} %get-tuple-element.24), channel_id=1, source_target_pairs={{0,4},{4,8},{8,12},{12,0},{1,5},{5,9},{9,13},{13,1},{2,6},{6,10},{... | collective-permute-start | bytes 983048 | tf_op jit(solution)/shard_map/ppermute | solution.py:412
  7.8 2.1 %collective-permute-start.2 = (bf16[8,160,128]{2,1,0:T(8,128)(2,1)S(1)}, bf16[8,160,128]{2,1,0:T(8,128)(2,1)S(1)}, u32[]{:S(2)}, u32[]{:S(2)}) collective-permute-start(bf16[8,160,128]{2,1,0:T(8,128)(2,1)S(1)} %get-tuple-element.25), channel_id=1, source_target_pairs={{4,0},{8,4},{12,8},{0,12},{5,1},{9,5},{13,9},{1,13},{6,2},{10,6},{... | collective-permute-start | bytes 983048 | tf_op jit(solution)/shard_map/ppermute | solution.py:413
  10.0 0.0 collective-permute-start.3
  10.0 3.9 %collective-permute-start.4 = (bf16[2,160,128]{2,1,0:T(8,128)(2,1)S(1)}, bf16[2,160,128]{2,1,0:T(8,128)(2,1)S(1)}, u32[]{:S(2)}, u32[]{:S(2)}) collective-permute-start(bf16[2,160,128]{2,1,0:T(8,128)(2,1)S(1)} %get-tuple-element.27), channel_id=1, source_target_pairs={{4,16},{8,20},{12,24},{0,28},{20,32},{24,36},{28,40},{16,44},{36,4... | collective-permute-start | bytes 245768 | tf_op jit(solution)/shard_map/ppermute | solution.py:416
  13.9 13.2 %inner.1 = (f32[8,8,160,256]{3,2,1,0:T(8,128)S(1)}, f32[8,8,256]{2,1,0:T(8,128)S(1)}) custom-call(s32[4]{0:T(128)S(4)} %get-tuple-element.30.frames_ref, bf16[8,8,160,384]{3,2,1,0:T(8,128)(2,1)S(1)} %get-tuple-element.22.xc, bf16[3456,256]{1,0:T(8,128)(2,1)S(1)} %get-tuple-element.21.w_ref), custom_call_target="tpu_custom_call" | custom-call | flops 11890851840 | bytes 5242880 | tf_op jit(solution)/shard_map/inner/pallas_call | solution.py:421
  27.0 0.0 copy-start
  27.0 0.0 collective-permute-done.3.above_before
  27.0 0.0 collective-permute-done.4.below_before
  27.1 0.0 collective-permute-done.1.above
  27.1 0.0 collective-permute-done.2.below
  27.1 0.0 collective-permute-done.before
  27.1 0.1 strips.1
  27.2 1.4 %collective-permute-start.5 = (bf16[10,16,128]{2,1,0:T(8,128)(2,1)S(1)}, bf16[10,16,128]{2,1,0:T(8,128)(2,1)S(1)}, u32[]{:S(2)}, u32[]{:S(2)}) collective-permute-start(bf16[10,16,128]{2,1,0:T(8,128)(2,1)S(1)} %get-tuple-element.28), channel_id=1, source_target_pairs={{0,1},{1,2},{2,3},{3,0},{4,5},{5,6},{6,7},{7,4},{8,9},{9,10},{10,1... | collective-permute-start | bytes 122888 | tf_op jit(solution)/shard_map/ppermute | solution.py:440
  28.5 1.7 %collective-permute-start.6 = (bf16[10,16,128]{2,1,0:T(8,128)(2,1)S(1)}, bf16[10,16,128]{2,1,0:T(8,128)(2,1)S(1)}, u32[]{:S(2)}, u32[]{:S(2)}) collective-permute-start(bf16[10,16,128]{2,1,0:T(8,128)(2,1)S(1)} %get-tuple-element.29), channel_id=1, source_target_pairs={{1,0},{2,1},{3,2},{0,3},{5,4},{6,5},{7,6},{4,7},{9,8},{10,9},{11,1... | collective-permute-start | bytes 122888 | tf_op jit(solution)/shard_map/ppermute | solution.py:441
  30.2 0.0 copy-done
  30.3 8.6 %outer.1 = (f32[8,8,160,256]{3,2,1,0:T(8,128)S(1)}, f32[8,8,256]{2,1,0:T(8,128)S(1)}) custom-call(s32[4]{0:T(128)S(1)} %copy-done, bf16[3456,256]{1,0:T(8,128)(2,1)S(1)} %get-tuple-element.21.w_ref, bf16[2,8,160,128]{3,2,1,0:T(8,128)(2,1)S(1)} %collective-permute-done.before, ...), custom_call_target="tpu_custom_call", output_to_operand_aliasing={{0}: (8, {}), {1}: (9, {})} | custom-call | flops 6228541440 | bytes 5242880 | tf_op jit(solution)/shard_map/outer/pallas_call | solution.py:442
  38.8 0.0 copy-start.1
  38.8 0.0 copy-start.2
  38.9 0.0 collective-permute-done.5.low_ref
  38.9 0.0 collective-permute-done.6.high_ref
  38.9 1.2 %columns.1 = (f32[8,8,160,256]{3,2,1,0:T(8,128)S(1)}, f32[1,256]{1,0:T(1,128)S(1)}) custom-call(s32[4]{0:T(128)S(1)} %copy-done, bf16[3456,256]{1,0:T(8,128)(2,1)S(1)} %get-tuple-element.21.w_ref, bf16[10,16,128]{2,1,0:T(8,128)(2,1)S(1)} %collective-permute-done.5.low_ref, ...), custom_call_target="tpu_custom_call", output_to_operand_aliasing={{0}: (5, {})} | custom-call | flops 134217728 | bytes 1048576 | tf_op jit(solution)/shard_map/columns/pallas_call | solution.py:457
  40.1 0.1 broadcast_in_dim.15
  40.2 15.0 %all_to_all.5 = f32[128,1,256]{2,1,0:T(1,128)S(1)} all-to-all(f32[128,1,256]{2,1,0:T(1,128)S(1)} %broadcast_in_dim.15), channel_id=1, replica_groups=mesh['tm'=8,'row'=4,'col'=4] {'tm','row','col'}, dimensions={0} | all-to-all | bytes 262144 | tf_op jit(solution)/shard_map/all_to_all | solution.py:469
  55.2 0.0 copy-done.1
  55.2 0.0 copy-done.2
  55.2 4.0 %norm_silu.1 = bf16[8,8,160,256]{3,2,1,0:T(8,128)(2,1)} custom-call(s32[4]{0:T(128)S(1)} %copy-done, f32[128,256]{1,0:T(8,128)S(1)} %bitcast.7, f32[1,256]{1,0:T(1,128)S(1)} %bitcast.8, f32[1,256]{1,0:T(1,128)S(1)} %bitcast.9, f32[8,8,160,256]{3,2,1,0:T(8,128)S(1)} %get-tuple-element.36.conv), custom_call_target="tpu_custom_call" | custom-call | flops 16777216 | bytes 16777216 | tf_op jit(solution)/shard_map/norm_silu/pallas_call | solution.py:470
  (1 shorter events, 0.0 us)
Async XLA Ops:
  3.6 23.5 %collective-permute-start = (bf16[2,8,160,128]{3,2,1,0:T(8,128)(2,1)S(1)}, bf16[2,8,160,128]{3,2,1,0:T(8,128)(2,1)S(1)}, u32[]{:S(2)}, u32[]{:S(2)}) collective-permute-start(bf16[2,8,160,128]{3,2,1,0:T(8,128)(2,1)S(1)} %get-tuple-element.23), channel_id=1, source_target_pairs={{0,16},{16,32},{32,48},{48,64},{64,80},{80,96},{96,112},{112,0},{1... | collective-permute-start | bytes 1966088 | tf_op jit(solution)/shard_map/ppermute | solution.py:414
  6.2 20.8 %collective-permute-start.1 = (bf16[8,160,128]{2,1,0:T(8,128)(2,1)S(1)}, bf16[8,160,128]{2,1,0:T(8,128)(2,1)S(1)}, u32[]{:S(2)}, u32[]{:S(2)}) collective-permute-start(bf16[8,160,128]{2,1,0:T(8,128)(2,1)S(1)} %get-tuple-element.24), channel_id=1, source_target_pairs={{0,4},{4,8},{8,12},{12,0},{1,5},{5,9},{9,13},{13,1},{2,6},{6,10},{... | collective-permute-start | bytes 983048 | tf_op jit(solution)/shard_map/ppermute | solution.py:412
  7.8 19.2 %collective-permute-start.2 = (bf16[8,160,128]{2,1,0:T(8,128)(2,1)S(1)}, bf16[8,160,128]{2,1,0:T(8,128)(2,1)S(1)}, u32[]{:S(2)}, u32[]{:S(2)}) collective-permute-start(bf16[8,160,128]{2,1,0:T(8,128)(2,1)S(1)} %get-tuple-element.25), channel_id=1, source_target_pairs={{4,0},{8,4},{12,8},{0,12},{5,1},{9,5},{13,9},{1,13},{6,2},{10,6},{... | collective-permute-start | bytes 983048 | tf_op jit(solution)/shard_map/ppermute | solution.py:413
  10.0 17.1 %collective-permute-start.3 = (bf16[2,160,128]{2,1,0:T(8,128)(2,1)S(1)}, bf16[2,160,128]{2,1,0:T(8,128)(2,1)S(1)}, u32[]{:S(2)}, u32[]{:S(2)}) collective-permute-start(bf16[2,160,128]{2,1,0:T(8,128)(2,1)S(1)} %get-tuple-element.26), channel_id=1, source_target_pairs={{0,20},{4,24},{8,28},{12,16},{16,36},{20,40},{24,44},{28,32},{32,5... | collective-permute-start | bytes 245768 | tf_op jit(solution)/shard_map/ppermute | solution.py:415
  10.0 17.1 %collective-permute-start.4 = (bf16[2,160,128]{2,1,0:T(8,128)(2,1)S(1)}, bf16[2,160,128]{2,1,0:T(8,128)(2,1)S(1)}, u32[]{:S(2)}, u32[]{:S(2)}) collective-permute-start(bf16[2,160,128]{2,1,0:T(8,128)(2,1)S(1)} %get-tuple-element.27), channel_id=1, source_target_pairs={{4,16},{8,20},{12,24},{0,28},{20,32},{24,36},{28,40},{16,44},{36,4... | collective-permute-start | bytes 245768 | tf_op jit(solution)/shard_map/ppermute | solution.py:416
  27.0 3.2 %copy-start = (s32[4]{0:T(128)S(1)}, s32[4]{0:T(128)}, u32[]{:S(2)}) copy-start(s32[4]{0:T(128)} %frames_ref.7) | copy-start | bytes 52
  27.2 11.7 %collective-permute-start.5 = (bf16[10,16,128]{2,1,0:T(8,128)(2,1)S(1)}, bf16[10,16,128]{2,1,0:T(8,128)(2,1)S(1)}, u32[]{:S(2)}, u32[]{:S(2)}) collective-permute-start(bf16[10,16,128]{2,1,0:T(8,128)(2,1)S(1)} %get-tuple-element.28), channel_id=1, source_target_pairs={{0,1},{1,2},{2,3},{3,0},{4,5},{5,6},{6,7},{7,4},{8,9},{9,10},{10,1... | collective-permute-start | bytes 122888 | tf_op jit(solution)/shard_map/ppermute | solution.py:440
  28.5 10.3 %collective-permute-start.6 = (bf16[10,16,128]{2,1,0:T(8,128)(2,1)S(1)}, bf16[10,16,128]{2,1,0:T(8,128)(2,1)S(1)}, u32[]{:S(2)}, u32[]{:S(2)}) collective-permute-start(bf16[10,16,128]{2,1,0:T(8,128)(2,1)S(1)} %get-tuple-element.29), channel_id=1, source_target_pairs={{1,0},{2,1},{3,2},{0,3},{5,4},{6,5},{7,6},{4,7},{9,8},{10,9},{11,1... | collective-permute-start | bytes 122888 | tf_op jit(solution)/shard_map/ppermute | solution.py:441
  38.8 16.4 %copy-start.1 = (f32[256]{0:T(256)S(1)}, f32[256]{0:T(256)}, u32[]{:S(2)}) copy-start(f32[256]{0:T(256)} %param.8) | copy-start | bytes 3076
  38.8 16.4 %copy-start.2 = (f32[256]{0:T(256)S(1)}, f32[256]{0:T(256)}, u32[]{:S(2)}) copy-start(f32[256]{0:T(256)} %param.9) | copy-start | bytes 3076

commit v4 on v3

--- a/solution.py
+++ b/solution.py
@@ -13,6 +13,7 @@
 SHARE = COUT // GROUPS
 F, H, W, C = 8, 8, 160, 128
 C3 = 3 * C
+LATE = 6
 BF, F32 = jnp.bfloat16, jnp.float32
 VMEM = pl.BlockSpec(memory_space=pltpu.VMEM)
 SMEM = pl.BlockSpec(memory_space=pltpu.SMEM)
@@ -107,10 +108,10 @@
 
 
 def load_kernel(
-    frames_ref, x_hbm, w_hbm, tail, top_row, bottom_row, tail_top, tail_bottom, xc, w_ref, clips, x_ref, x_sems, w_sem
+    frames_hbm, x_hbm, w_hbm, tail, top_row, bottom_row, tail_top, tail_bottom, xc, w_ref, clips, x_ref, x_sems, w_sem, c_sem
 ):
-    for c in range(CLIPS):
-        clips[c] = frames_ref[c]
+    c_copy = pltpu.make_async_copy(frames_hbm, clips, c_sem)
+    c_copy.start()
 
     def x_copy(f):
         return pltpu.make_async_copy(x_hbm.at[f], x_ref.at[f], x_sems.at[f])
@@ -132,6 +133,15 @@
     tail_top[...] = x_ref[F - 2 :, 0]
     tail_bottom[...] = x_ref[F - 2 :, H - 1]
     w_copy.wait()
+    c_copy.wait()
+
+
+def inner_frame(f, first, starts, xc, w_ref, conv, stats):
+    frames = [xc.at[source(starts, first, f, k)] for k in range(2)] + [xc.at[f]]
+    for row in (1, 3, 5):
+        out = inner_taps(frames, row, 2, w_ref, (0, 1, 2))
+        conv[f, row : row + 2] = out
+        (start_stats if row == 1 else add_stats)(stats, f, out)
 
 
 def inner_kernel(frames_ref, xc, w_ref, conv, stats):
@@ -147,17 +157,8 @@
 
     lax.fori_loop(0, 3, first_frames, 0, unroll=3)
 
-    def step(i, carry):
-        for j in range(3):
-            f = 2 + 3 * i + j
-            frames = [xc.at[source(starts, first, f, k)] for k in range(2)] + [xc.at[f]]
-            for row in (1, 3, 5):
-                out = inner_taps(frames, row, 2, w_ref, (0, 1, 2))
-                conv[f, row : row + 2] = out
-                (start_stats if row == 1 else add_stats)(stats, f, out)
-        return carry
-
-    lax.fori_loop(0, (F - 2) // 3, step, 0)
+    for f in range(2, LATE):
+        inner_frame(f, first, starts, xc, w_ref, conv, stats)
 
 
 def strip_kernel(xc, before, above, below, above_before, below_before, low_out, high_out):
@@ -210,9 +211,6 @@
         rim = jnp.stack([jnp.where(top, own[0], over), jnp.where(bottom, own[H - 1], under)])
         put_columns(ref, (at,), rim)
 
-    for f in range(F):
-        fill_rims(rims, f, xc.at[f, :, :, C : 2 * C], above[f], below[f])
-
     def fill_early(i):
         if i == 2:
             for f in range(2):
@@ -236,16 +234,15 @@
         conv[f, H - 1] = out[1]
         return out
 
-    def step(i, carry):
-        for j in range(6):
-            f = 2 + 6 * i + j
-            add_stats(stats, f, outer_rows(f, 0, xc, rims))
-        return carry
-
-    fill_early(0)
-    fill_early(1)
-    fill_early(2)
-    lax.fori_loop(0, (F - 2) // 6, step, 0)
+    for f in range(LATE, F):
+        for g in range(f - LATE, F, F - LATE):
+            fill_rims(rims, g, xc.at[g, :, :, C : 2 * C], above[g], below[g])
+        if f == F - 1:
+            for i in range(3):
+                fill_early(i)
+        inner_frame(f, first, starts, xc, w_ref, conv, stats)
+    for f in range(2, F):
+        add_stats(stats, f, outer_rows(f, 0, xc, rims))
     for f in range(2):
         start_stats(stats, f, outer_rows(f, 2, early, early_rims))
 
@@ -354,17 +351,17 @@
     both = [jnp.where(mine, v, 0.0) for v in (mean, scale)]
     both = times_zero_one(jnp.concatenate(both, axis=0), chosen)
     mean, scale = both[:F], both[F:] * (0.5 * gain[...])
-    half = 0.5 * shift[...]
+    offset = 0.5 * shift[...] - mean * scale
 
     def out_copy(f):
         return pltpu.make_async_copy(held.at[f], out_ref.at[f], sems.at[f])
 
     for f in range(F):
-        per_frame[f] = jnp.concatenate([mean[f : f + 1], scale[f : f + 1], half], axis=0)
+        per_frame[f] = jnp.concatenate([scale[f : f + 1], offset[f : f + 1]], axis=0)
 
     def frame(f, carry):
         for h in range(H):
-            u = (conv[f, h] - per_frame[f, 0:1]) * per_frame[f, 1:2] + per_frame[f, 2:3]
+            u = conv[f, h] * per_frame[f, 0:1] + per_frame[f, 1:2]
             held[f, h] = (u + u * jnp.tanh(u)).astype(BF)
         out_copy(f).start()
         return carry
@@ -392,11 +389,12 @@
         + [pltpu.VMEM((2, W, C), BF)] * 2
         + [pltpu.VMEM((F, H, W, C3), BF), pltpu.VMEM((27 * C, COUT), BF)]
         + [pltpu.SMEM((CLIPS,), jnp.int32)],
-        in_specs=[SMEM] + [HBM] * 2,
+        in_specs=[HBM] * 3,
         out_specs=[VMEM] * 7 + [SMEM],
         scratch_shapes=[
             pltpu.VMEM((F, H, W, C), BF),
             pltpu.SemaphoreType.DMA((F,)),
+            pltpu.SemaphoreType.DMA,
             pltpu.SemaphoreType.DMA,
         ],
         compiler_params=params(52),
@@ -475,7 +473,7 @@
         scratch_shapes=[
             pltpu.VMEM((F, H, W, COUT), BF),
             pltpu.SemaphoreType.DMA((F,)),
-            pltpu.VMEM((F, 3, COUT), F32),
+            pltpu.VMEM((F, 2, COUT), F32),
         ],
         compiler_params=params(12),
         cost_estimate=cost(1 << 24, 16 << 20),

time: 59.5 us -> 58 us (0.975)
  Pallas kernels: 30.6 us -> 29.2 us
    pallas_call x1, Pallas kernels: 13.2 us -> 9.15 us  [shards(): pl.pallas_call(inner_kernel, out_shape=(conv_shape, stats_shape), in_spec...]
    pallas_call x1, Pallas kernels: 8.58 us -> 12.1 us  [shards(): pl.pallas_call(outer_kernel, out_shape=(conv_shape, stats_shape), in_spec...]
    pallas_call x1, Pallas kernels: 3.59 us -> 2.94 us  [shards(): pl.pallas_call(load_kernel, out_shape=[pltpu.VMEM((2, H, W, C), BF)] + [p...]
where the time goes in v4:
time: 58 us; the launch traced here: 57.9 us
  Pallas kernels  29.2 us (50%)
  blocking collectives  15 us (26%)
  starting transfers between devices  13.3 us (23%)
    all_to_all x1, blocking collectives, shards(): every = lax.all_to_all(every, ('tm', 'row', 'col'), 0, 0).reshape(count, -1)  15 us
    pallas_call x1, Pallas kernels, shards(): pl.pallas_call(outer_kernel, out_shape=(conv_shape, stats_shape), in_spec...  12.1 us
    pallas_call x1, Pallas kernels, shards(): pl.pallas_call(inner_kernel, out_shape=(conv_shape, stats_shape), in_spec...  9.15 us
    ppermute x1, starting transfers between devices, shards(): below_before = lax.ppermute(tail_top, ('tm', 'row'), diagonal(up))  3.88 us
    pallas_call x1, Pallas kernels, shards(): pl.pallas_call(functools.partial(norm_kernel, H * n_row * W * n_col), out...  3.61 us
    pallas_call x1, Pallas kernels, shards(): pl.pallas_call(load_kernel, out_shape=[pltpu.VMEM((2, H, W, C), BF)] + [p...  2.94 us
    ppermute x1, starting transfers between devices, shards(): before = lax.ppermute(tail, 'tm', later)  2.61 us
    ppermute x1, starting transfers between devices, shards(): below = lax.ppermute(top_row, 'row', up)  2.12 us
  transfers between devices with their start and end apart: 7, of which 0 were waited for; matrix products, arithmetic and copies ran while one was open for 0% of the time, Pallas kernels for 37%

profile of v4, /device:TPU:1, one launch (start us, length us, event | category | flops | bytes accessed | tf_op | source)
XLA Modules:
  0.0 57.9 jit_solution(4558579304924337571)
XLA Ops:
  0.0 2.9 %load.1 = (bf16[2,8,160,128]{3,2,1,0:T(8,128)(2,1)S(1)}, bf16[8,160,128]{2,1,0:T(8,128)(2,1)S(1)}, bf16[8,160,128]{2,1,0:T(8,128)(2,1)S(1)}, bf16[2,160,128]{2,1...) custom-call(s32[4]{0:T(128)} %frames_ref.5, ...), custom_call_target="tpu_custom_call" | custom-call | tf_op jit(solution)/shard_map/load/pallas_call | solution.py:385
  2.9 2.6 %collective-permute-start = (bf16[2,8,160,128]{3,2,1,0:T(8,128)(2,1)S(1)}, bf16[2,8,160,128]{3,2,1,0:T(8,128)(2,1)S(1)}, u32[]{:S(2)}, u32[]{:S(2)}) collective-permute-start(bf16[2,8,160,128]{3,2,1,0:T(8,128)(2,1)S(1)} %get-tuple-element.23), channel_id=1, source_target_pairs={{0,16},{16,32},{32,48},{48,64},{64,80},{80,96},{96,112},{112,0},{1... | collective-permute-start | bytes 1966088 | tf_op jit(solution)/shard_map/ppermute | solution.py:412
  5.6 1.6 %collective-permute-start.1 = (bf16[8,160,128]{2,1,0:T(8,128)(2,1)S(1)}, bf16[8,160,128]{2,1,0:T(8,128)(2,1)S(1)}, u32[]{:S(2)}, u32[]{:S(2)}) collective-permute-start(bf16[8,160,128]{2,1,0:T(8,128)(2,1)S(1)} %get-tuple-element.24), channel_id=1, source_target_pairs={{0,4},{4,8},{8,12},{12,0},{1,5},{5,9},{9,13},{13,1},{2,6},{6,10},{... | collective-permute-start | bytes 983048 | tf_op jit(solution)/shard_map/ppermute | solution.py:410
  7.2 2.1 %collective-permute-start.2 = (bf16[8,160,128]{2,1,0:T(8,128)(2,1)S(1)}, bf16[8,160,128]{2,1,0:T(8,128)(2,1)S(1)}, u32[]{:S(2)}, u32[]{:S(2)}) collective-permute-start(bf16[8,160,128]{2,1,0:T(8,128)(2,1)S(1)} %get-tuple-element.25), channel_id=1, source_target_pairs={{4,0},{8,4},{12,8},{0,12},{5,1},{9,5},{13,9},{1,13},{6,2},{10,6},{... | collective-permute-start | bytes 983048 | tf_op jit(solution)/shard_map/ppermute | solution.py:411
  9.3 0.0 collective-permute-start.3
  9.3 3.9 %collective-permute-start.4 = (bf16[2,160,128]{2,1,0:T(8,128)(2,1)S(1)}, bf16[2,160,128]{2,1,0:T(8,128)(2,1)S(1)}, u32[]{:S(2)}, u32[]{:S(2)}) collective-permute-start(bf16[2,160,128]{2,1,0:T(8,128)(2,1)S(1)} %get-tuple-element.27), channel_id=1, source_target_pairs={{4,16},{8,20},{12,24},{0,28},{20,32},{24,36},{28,40},{16,44},{36,4... | collective-permute-start | bytes 245768 | tf_op jit(solution)/shard_map/ppermute | solution.py:414
  13.2 9.2 %inner.1 = (f32[8,8,160,256]{3,2,1,0:T(8,128)S(1)}, f32[8,8,256]{2,1,0:T(8,128)S(1)}) custom-call(s32[4]{0:T(128)S(4)} %get-tuple-element.30.frames_ref, bf16[8,8,160,384]{3,2,1,0:T(8,128)(2,1)S(1)} %get-tuple-element.22.xc, bf16[3456,256]{1,0:T(8,128)(2,1)S(1)} %get-tuple-element.21.w_ref), custom_call_target="tpu_custom_call" | custom-call | flops 11890851840 | bytes 5242880 | tf_op jit(solution)/shard_map/inner/pallas_call | solution.py:419
  22.4 0.0 copy-start
  22.4 0.0 collective-permute-done.3.above_before
  22.4 0.0 collective-permute-done.4.below_before
  22.4 0.0 collective-permute-done.1.above
  22.4 0.0 collective-permute-done.2.below
  22.4 0.0 collective-permute-done.before
  22.4 0.1 strips.1
  22.5 1.4 %collective-permute-start.5 = (bf16[10,16,128]{2,1,0:T(8,128)(2,1)S(1)}, bf16[10,16,128]{2,1,0:T(8,128)(2,1)S(1)}, u32[]{:S(2)}, u32[]{:S(2)}) collective-permute-start(bf16[10,16,128]{2,1,0:T(8,128)(2,1)S(1)} %get-tuple-element.28), channel_id=1, source_target_pairs={{0,1},{1,2},{2,3},{3,0},{4,5},{5,6},{6,7},{7,4},{8,9},{9,10},{10,1... | collective-permute-start | bytes 122888 | tf_op jit(solution)/shard_map/ppermute | solution.py:438
  23.9 1.7 %collective-permute-start.6 = (bf16[10,16,128]{2,1,0:T(8,128)(2,1)S(1)}, bf16[10,16,128]{2,1,0:T(8,128)(2,1)S(1)}, u32[]{:S(2)}, u32[]{:S(2)}) collective-permute-start(bf16[10,16,128]{2,1,0:T(8,128)(2,1)S(1)} %get-tuple-element.29), channel_id=1, source_target_pairs={{1,0},{2,1},{3,2},{0,3},{5,4},{6,5},{7,6},{4,7},{9,8},{10,9},{11,1... | collective-permute-start | bytes 122888 | tf_op jit(solution)/shard_map/ppermute | solution.py:439
  25.6 0.0 copy-done
  25.6 12.1 %outer.1 = (f32[8,8,160,256]{3,2,1,0:T(8,128)S(1)}, f32[8,8,256]{2,1,0:T(8,128)S(1)}) custom-call(s32[4]{0:T(128)S(1)} %copy-done, bf16[3456,256]{1,0:T(8,128)(2,1)S(1)} %get-tuple-element.21.w_ref, bf16[2,8,160,128]{3,2,1,0:T(8,128)(2,1)S(1)} %collective-permute-done.before, ...), custom_call_target="tpu_custom_call", output_to_operand_aliasing={{0}: (8, {}), {1}: (9, {})} | custom-call | flops 6228541440 | bytes 5242880 | tf_op jit(solution)/shard_map/outer/pallas_call | solution.py:440
  37.7 0.0 copy-start.1
  37.8 0.0 copy-start.2
  37.8 0.0 collective-permute-done.5.low_ref
  37.8 0.0 collective-permute-done.6.high_ref
  37.8 1.2 %columns.1 = (f32[8,8,160,256]{3,2,1,0:T(8,128)S(1)}, f32[1,256]{1,0:T(1,128)S(1)}) custom-call(s32[4]{0:T(128)S(1)} %copy-done, bf16[3456,256]{1,0:T(8,128)(2,1)S(1)} %get-tuple-element.21.w_ref, bf16[10,16,128]{2,1,0:T(8,128)(2,1)S(1)} %collective-permute-done.5.low_ref, ...), custom_call_target="tpu_custom_call", output_to_operand_aliasing={{0}: (5, {})} | custom-call | flops 134217728 | bytes 1048576 | tf_op jit(solution)/shard_map/columns/pallas_call | solution.py:455
  39.0 0.1 broadcast_in_dim.15
  39.1 15.0 %all_to_all.5 = f32[128,1,256]{2,1,0:T(1,128)S(1)} all-to-all(f32[128,1,256]{2,1,0:T(1,128)S(1)} %broadcast_in_dim.15), channel_id=1, replica_groups=mesh['tm'=8,'row'=4,'col'=4] {'tm','row','col'}, dimensions={0} | all-to-all | bytes 262144 | tf_op jit(solution)/shard_map/all_to_all | solution.py:467
  54.1 0.0 copy-done.1
  54.1 0.0 copy-done.2
  54.1 3.6 %norm_silu.1 = bf16[8,8,160,256]{3,2,1,0:T(8,128)(2,1)} custom-call(s32[4]{0:T(128)S(1)} %copy-done, f32[128,256]{1,0:T(8,128)S(1)} %bitcast.7, f32[1,256]{1,0:T(1,128)S(1)} %bitcast.8, f32[1,256]{1,0:T(1,128)S(1)} %bitcast.9, f32[8,8,160,256]{3,2,1,0:T(8,128)S(1)} %get-tuple-element.36.conv), custom_call_target="tpu_custom_call" | custom-call | flops 16777216 | bytes 16777216 | tf_op jit(solution)/shard_map/norm_silu/pallas_call | solution.py:468
  (1 shorter events, 0.0 us)
Async XLA Ops:
  2.9 19.5 %collective-permute-start = (bf16[2,8,160,128]{3,2,1,0:T(8,128)(2,1)S(1)}, bf16[2,8,160,128]{3,2,1,0:T(8,128)(2,1)S(1)}, u32[]{:S(2)}, u32[]{:S(2)}) collective-permute-start(bf16[2,8,160,128]{3,2,1,0:T(8,128)(2,1)S(1)} %get-tuple-element.23), channel_id=1, source_target_pairs={{0,16},{16,32},{32,48},{48,64},{64,80},{80,96},{96,112},{112,0},{1... | collective-permute-start | bytes 1966088 | tf_op jit(solution)/shard_map/ppermute | solution.py:412
  5.6 16.8 %collective-permute-start.1 = (bf16[8,160,128]{2,1,0:T(8,128)(2,1)S(1)}, bf16[8,160,128]{2,1,0:T(8,128)(2,1)S(1)}, u32[]{:S(2)}, u32[]{:S(2)}) collective-permute-start(bf16[8,160,128]{2,1,0:T(8,128)(2,1)S(1)} %get-tuple-element.24), channel_id=1, source_target_pairs={{0,4},{4,8},{8,12},{12,0},{1,5},{5,9},{9,13},{13,1},{2,6},{6,10},{... | collective-permute-start | bytes 983048 | tf_op jit(solution)/shard_map/ppermute | solution.py:410
  7.2 15.2 %collective-permute-start.2 = (bf16[8,160,128]{2,1,0:T(8,128)(2,1)S(1)}, bf16[8,160,128]{2,1,0:T(8,128)(2,1)S(1)}, u32[]{:S(2)}, u32[]{:S(2)}) collective-permute-start(bf16[8,160,128]{2,1,0:T(8,128)(2,1)S(1)} %get-tuple-element.25), channel_id=1, source_target_pairs={{4,0},{8,4},{12,8},{0,12},{5,1},{9,5},{13,9},{1,13},{6,2},{10,6},{... | collective-permute-start | bytes 983048 | tf_op jit(solution)/shard_map/ppermute | solution.py:411
  9.3 13.1 %collective-permute-start.3 = (bf16[2,160,128]{2,1,0:T(8,128)(2,1)S(1)}, bf16[2,160,128]{2,1,0:T(8,128)(2,1)S(1)}, u32[]{:S(2)}, u32[]{:S(2)}) collective-permute-start(bf16[2,160,128]{2,1,0:T(8,128)(2,1)S(1)} %get-tuple-element.26), channel_id=1, source_target_pairs={{0,20},{4,24},{8,28},{12,16},{16,36},{20,40},{24,44},{28,32},{32,5... | collective-permute-start | bytes 245768 | tf_op jit(solution)/shard_map/ppermute | solution.py:413
  9.3 13.1 %collective-permute-start.4 = (bf16[2,160,128]{2,1,0:T(8,128)(2,1)S(1)}, bf16[2,160,128]{2,1,0:T(8,128)(2,1)S(1)}, u32[]{:S(2)}, u32[]{:S(2)}) collective-permute-start(bf16[2,160,128]{2,1,0:T(8,128)(2,1)S(1)} %get-tuple-element.27), channel_id=1, source_target_pairs={{4,16},{8,20},{12,24},{0,28},{20,32},{24,36},{28,40},{16,44},{36,4... | collective-permute-start | bytes 245768 | tf_op jit(solution)/shard_map/ppermute | solution.py:414
  22.4 3.2 %copy-start = (s32[4]{0:T(128)S(1)}, s32[4]{0:T(128)}, u32[]{:S(2)}) copy-start(s32[4]{0:T(128)} %frames_ref.5) | copy-start | bytes 52
  22.5 15.2 %collective-permute-start.5 = (bf16[10,16,128]{2,1,0:T(8,128)(2,1)S(1)}, bf16[10,16,128]{2,1,0:T(8,128)(2,1)S(1)}, u32[]{:S(2)}, u32[]{:S(2)}) collective-permute-start(bf16[10,16,128]{2,1,0:T(8,128)(2,1)S(1)} %get-tuple-element.28), channel_id=1, source_target_pairs={{0,1},{1,2},{2,3},{3,0},{4,5},{5,6},{6,7},{7,4},{8,9},{9,10},{10,1... | collective-permute-start | bytes 122888 | tf_op jit(solution)/shard_map/ppermute | solution.py:438
  23.9 13.9 %collective-permute-start.6 = (bf16[10,16,128]{2,1,0:T(8,128)(2,1)S(1)}, bf16[10,16,128]{2,1,0:T(8,128)(2,1)S(1)}, u32[]{:S(2)}, u32[]{:S(2)}) collective-permute-start(bf16[10,16,128]{2,1,0:T(8,128)(2,1)S(1)} %get-tuple-element.29), channel_id=1, source_target_pairs={{1,0},{2,1},{3,2},{0,3},{5,4},{6,5},{7,6},{4,7},{9,8},{10,9},{11,1... | collective-permute-start | bytes 122888 | tf_op jit(solution)/shard_map/ppermute | solution.py:439
  37.7 16.4 %copy-start.1 = (f32[256]{0:T(256)S(1)}, f32[256]{0:T(256)}, u32[]{:S(2)}) copy-start(f32[256]{0:T(256)} %param.8) | copy-start | bytes 3076
  37.8 16.4 %copy-start.2 = (f32[256]{0:T(256)S(1)}, f32[256]{0:T(256)}, u32[]{:S(2)}) copy-start(f32[256]{0:T(256)} %param.9) | copy-start | bytes 3076

commit v5 on v4

--- a/solution.py
+++ b/solution.py
@@ -13,7 +13,6 @@
 SHARE = COUT // GROUPS
 F, H, W, C = 8, 8, 160, 128
 C3 = 3 * C
-LATE = 6
 BF, F32 = jnp.bfloat16, jnp.float32
 VMEM = pl.BlockSpec(memory_space=pltpu.VMEM)
 SMEM = pl.BlockSpec(memory_space=pltpu.SMEM)
@@ -144,21 +143,35 @@
         (start_stats if row == 1 else add_stats)(stats, f, out)
 
 
-def inner_kernel(frames_ref, xc, w_ref, conv, stats):
+def inner_kernel(frames, opening, frames_ref, xc, w_ref, *refs):
+    conv, stats = refs[:2] if opening else refs[-3:-1]
     first = lax.axis_index("tm") * F
     starts = clip_starts(frames_ref)
-
-    def first_frames(i, carry):
-        row = 1 + 2 * i
-        conv[0, pl.ds(row, 2)] = inner_taps([xc.at[0]], row, 2, w_ref, (2,))
-        frames = [xc.at[source(starts, first, 1, 1)], xc.at[1]]
-        conv[1, pl.ds(row, 2)] = inner_taps(frames, row, 2, w_ref, (1, 2))
-        return carry
-
-    lax.fori_loop(0, 3, first_frames, 0, unroll=3)
-
-    for f in range(2, LATE):
+    for f in frames:
         inner_frame(f, first, starts, xc, w_ref, conv, stats)
+    if opening:
+        for row in (1, 3, 5):
+            conv[0, row : row + 2] = inner_taps([xc.at[0]], row, 2, w_ref, (2,))
+            own = [xc.at[source(starts, first, 1, 1)], xc.at[1]]
+            conv[1, row : row + 2] = inner_taps(own, row, 2, w_ref, (1, 2))
+
+
+def inner_part(frames, opening, clips, xc, weights, conv, stats, passed):
+    out_shape = [pltpu.VMEM((F, H, W, COUT), F32), pltpu.VMEM((F, 8, COUT), F32)]
+    held = [] if opening else [conv, stats, passed]
+    if not opening:
+        out_shape.append(pltpu.VMEM(passed.shape, passed.dtype))
+    count = 3 * len(frames) + 3 * opening
+    return pl.pallas_call(
+        functools.partial(inner_kernel, frames, opening),
+        out_shape=out_shape,
+        in_specs=[SMEM] + [VMEM] * (2 + len(held)),
+        out_specs=[VMEM] * len(out_shape),
+        input_output_aliases={3 + i: i for i in range(len(held))},
+        compiler_params=params(12),
+        cost_estimate=cost(2 * count * 2 * W * 9 * C3 * COUT, 5 << 20),
+        name="inner",
+    )(clips, xc, weights, *held)
 
 
 def strip_kernel(xc, before, above, below, above_before, below_before, low_out, high_out):
@@ -194,6 +207,7 @@
     above_before,
     below_before,
     xc,
+    arrived,
     conv_in,
     stats_in,
     conv,
@@ -202,7 +216,7 @@
     early_rims,
     rims,
 ):
-    del conv_in, stats_in
+    del arrived, conv_in, stats_in
     first = lax.axis_index("tm") * F
     starts = clip_starts(frames_ref)
     top, bottom, _, _ = edges()
@@ -234,13 +248,10 @@
         conv[f, H - 1] = out[1]
         return out
 
-    for f in range(LATE, F):
-        for g in range(f - LATE, F, F - LATE):
-            fill_rims(rims, g, xc.at[g, :, :, C : 2 * C], above[g], below[g])
-        if f == F - 1:
-            for i in range(3):
-                fill_early(i)
-        inner_frame(f, first, starts, xc, w_ref, conv, stats)
+    for f in range(F):
+        fill_rims(rims, f, xc.at[f, :, :, C : 2 * C], above[f], below[f])
+    for i in range(3):
+        fill_early(i)
     for f in range(2, F):
         add_stats(stats, f, outer_rows(f, 0, xc, rims))
     for f in range(2):
@@ -354,21 +365,25 @@
     offset = 0.5 * shift[...] - mean * scale
 
     def out_copy(f):
-        return pltpu.make_async_copy(held.at[f], out_ref.at[f], sems.at[f])
+        f, h = f // 2, f % 2 * (H // 2)
+        rows = (f, pl.ds(h, H // 2))
+        return pltpu.make_async_copy(held.at[rows], out_ref.at[rows], sems.at[2 * f + h // (H // 2)])
 
     for f in range(F):
         per_frame[f] = jnp.concatenate([scale[f : f + 1], offset[f : f + 1]], axis=0)
 
-    def frame(f, carry):
-        for h in range(H):
+    def half_frame(i, carry):
+        f = i // 2
+        for r in range(H // 2):
+            h = i % 2 * (H // 2) + r
             u = conv[f, h] * per_frame[f, 0:1] + per_frame[f, 1:2]
             held[f, h] = (u + u * jnp.tanh(u)).astype(BF)
-        out_copy(f).start()
+        out_copy(i).start()
         return carry
 
-    lax.fori_loop(0, F, frame, 0)
-    for f in range(F):
-        out_copy(f).wait()
+    lax.fori_loop(0, 2 * F, half_frame, 0)
+    for i in range(2 * F):
+        out_copy(i).wait()
 
 
 def params(mib):
@@ -407,24 +422,16 @@
     def diagonal(pairs):
         return [(t * n_row + i, u * n_row + j) for t, u in later for i, j in pairs]
 
+    conv_shape = pltpu.VMEM((F, H, W, COUT), F32)
+    stats_shape = pltpu.VMEM((F, 8, COUT), F32)
+    macs = W * 9 * C3 * COUT
+    part = lambda *args: inner_part(args[0], args[1], clips, xc, weights, *args[2:])
     above = lax.ppermute(bottom_row, "row", down)
     below = lax.ppermute(top_row, "row", up)
     before = lax.ppermute(tail, "tm", later)
     above_before = lax.ppermute(tail_bottom, ("tm", "row"), diagonal(down))
     below_before = lax.ppermute(tail_top, ("tm", "row"), diagonal(up))
-
-    conv_shape = pltpu.VMEM((F, H, W, COUT), F32)
-    stats_shape = pltpu.VMEM((F, 8, COUT), F32)
-    macs = W * 9 * C3 * COUT
-    conv, stats = pl.pallas_call(
-        inner_kernel,
-        out_shape=(conv_shape, stats_shape),
-        in_specs=[SMEM, VMEM, VMEM],
-        out_specs=[VMEM] * 2,
-        compiler_params=params(12),
-        cost_estimate=cost(2 * 42 * macs, 5 << 20),
-        name="inner",
-    )(clips, xc, weights)
+    conv, stats = part((2, 3, 4, 5, 6), True, None, None, None)
     low, high = pl.pallas_call(
         strip_kernel,
         out_shape=[pltpu.VMEM((F + 2, 16, C), BF)] * 2,
@@ -436,13 +443,14 @@
     )(xc, before, above, below, above_before, below_before)
     onward = [(i, (i + 1) % n_col) for i in range(n_col)]
     from_left = lax.ppermute(high, "col", onward)
+    conv, stats, low = part((7,), False, conv, stats, low)
     from_right = lax.ppermute(low, "col", [(j, i) for i, j in onward])
     conv, stats = pl.pallas_call(
         outer_kernel,
         out_shape=(conv_shape, stats_shape),
-        in_specs=[SMEM] + [VMEM] * 9,
+        in_specs=[SMEM] + [VMEM] * 10,
         out_specs=[VMEM] * 2,
-        input_output_aliases={8: 0, 9: 1},
+        input_output_aliases={9: 0, 10: 1},
         scratch_shapes=[
             pltpu.VMEM((4, H, W, C3), BF),
             pltpu.VMEM((4, 2, W, C3), BF),
@@ -451,7 +459,7 @@
         compiler_params=params(18),
         cost_estimate=cost(2 * 22 * macs, 5 << 20),
         name="outer",
-    )(clip_frames, weights, before, above, below, above_before, below_before, xc, conv, stats)
+    )(clips, weights, before, above, below, above_before, below_before, xc, from_left, conv, stats)
     conv, stats = pl.pallas_call(
         column_kernel,
         out_shape=(conv_shape, jax.ShapeDtypeStruct((1, 2 * CLIPS * GROUPS), F32)),
@@ -461,7 +469,7 @@
         compiler_params=params(12),
         cost_estimate=cost(1 << 27, 1 << 20),
         name="columns",
-    )(clip_frames, weights, from_left, from_right, stats, conv)
+    )(clips, weights, from_left, from_right, stats, conv)
     count = n_tm * n_row * n_col
     every = jnp.broadcast_to(stats[None], (count, *stats.shape))
     every = lax.all_to_all(every, ("tm", "row", "col"), 0, 0).reshape(count, -1)
@@ -472,13 +480,13 @@
         out_specs=HBM,
         scratch_shapes=[
             pltpu.VMEM((F, H, W, COUT), BF),
-            pltpu.SemaphoreType.DMA((F,)),
+            pltpu.SemaphoreType.DMA((2 * F,)),
             pltpu.VMEM((F, 2, COUT), F32),
         ],
         compiler_params=params(12),
         cost_estimate=cost(1 << 24, 16 << 20),
         name="norm_silu",
-    )(clip_frames, every, norm_gain[None], norm_shift[None], conv)
+    )(clips, every, norm_gain[None], norm_shift[None], conv)
 
 
 def solution(mesh):

time: 58 us -> 56.9 us (0.981)
  Pallas kernels: 29.2 us -> 27.9 us
  blocking collectives: 15 us -> 15.7 us
    pallas_call x1, Pallas kernels: 12.1 us -> 8.03 us  [shards(): pl.pallas_call(outer_kernel, out_shape=(conv_shape, stats_shape), in_spec...]
    ppermute x1, starting transfers between devices: 0.01 us -> 4.02 us  [shards(): above_before = lax.ppermute(tail_bottom, ('tm', 'row'), diagonal(down))]
    pallas_call x1 -> x2, Pallas kernels: 9.15 us -> 12.9 us  [inner_part(): pl.pallas_call(functools.partial(inner_kernel, frames, opening), out_shap...]
    ppermute x1, starting transfers between devices: 2.61 us -> 0.89 us  [shards(): before = lax.ppermute(tail, 'tm', later)]
    ppermute x1, starting transfers between devices: 3.88 us -> 2.2 us  [shards(): below_before = lax.ppermute(tail_top, ('tm', 'row'), diagonal(up))]
    ppermute x1, starting transfers between devices: 1.64 us -> 0.01 us  [shards(): above = lax.ppermute(bottom_row, 'row', down)]
    all_to_all x1, blocking collectives: 15 us -> 15.7 us  [shards(): every = lax.all_to_all(every, ('tm', 'row', 'col'), 0, 0).reshape(count, -1)]
where the time goes in v5:
time: 56.9 us; the launch traced here: 56.8 us
  Pallas kernels  27.9 us (49%)
  blocking collectives  15.7 us (28%)
  starting transfers between devices  12.9 us (23%)
    all_to_all x1, blocking collectives, shards(): every = lax.all_to_all(every, ('tm', 'row', 'col'), 0, 0).reshape(count, -1)  15.7 us
    pallas_call x2, Pallas kernels, inner_part(): pl.pallas_call(functools.partial(inner_kernel, frames, opening), out_shap...  12.9 us
    pallas_call x1, Pallas kernels, shards(): pl.pallas_call(outer_kernel, out_shape=(conv_shape, stats_shape), in_spec...  8.03 us
    ppermute x1, starting transfers between devices, shards(): above_before = lax.ppermute(tail_bottom, ('tm', 'row'), diagonal(down))  4.02 us
    pallas_call x1, Pallas kernels, shards(): pl.pallas_call(functools.partial(norm_kernel, H * n_row * W * n_col), out...  3.2 us
    pallas_call x1, Pallas kernels, shards(): pl.pallas_call(load_kernel, out_shape=[pltpu.VMEM((2, H, W, C), BF)] + [p...  2.94 us
    ppermute x1, starting transfers between devices, shards(): below = lax.ppermute(top_row, 'row', up)  2.67 us
    ppermute x1, starting transfers between devices, shards(): below_before = lax.ppermute(tail_top, ('tm', 'row'), diagonal(up))  2.2 us
  transfers between devices with their start and end apart: 7, of which 0 were waited for; matrix products, arithmetic and copies ran while one was open for 0% of the time, Pallas kernels for 37%

profile of v5, /device:TPU:1, one launch (start us, length us, event | category | flops | bytes accessed | tf_op | source)
XLA Modules:
  0.0 56.8 jit_solution(5087807365287171773)
XLA Ops:
  0.0 2.9 %load.1 = (bf16[2,8,160,128]{3,2,1,0:T(8,128)(2,1)S(1)}, bf16[8,160,128]{2,1,0:T(8,128)(2,1)S(1)}, bf16[8,160,128]{2,1,0:T(8,128)(2,1)S(1)}, bf16[2,160,128]{2,1...) custom-call(s32[4]{0:T(128)} %frames_hbm.1, ...), custom_call_target="tpu_custom_call" | custom-call | tf_op jit(solution)/shard_map/load/pallas_call | solution.py:400
  2.9 4.0 %collective-permute-start.3 = (bf16[2,160,128]{2,1,0:T(8,128)(2,1)S(1)}, bf16[2,160,128]{2,1,0:T(8,128)(2,1)S(1)}, u32[]{:S(2)}, u32[]{:S(2)}) collective-permute-start(bf16[2,160,128]{2,1,0:T(8,128)(2,1)S(1)} %get-tuple-element.30), channel_id=1, source_target_pairs={{0,20},{4,24},{8,28},{12,16},{16,36},{20,40},{24,44},{28,32},{32,5... | collective-permute-start | bytes 245768 | tf_op jit(solution)/shard_map/ppermute | solution.py:432
  7.0 2.2 %collective-permute-start.4 = (bf16[2,160,128]{2,1,0:T(8,128)(2,1)S(1)}, bf16[2,160,128]{2,1,0:T(8,128)(2,1)S(1)}, u32[]{:S(2)}, u32[]{:S(2)}) collective-permute-start(bf16[2,160,128]{2,1,0:T(8,128)(2,1)S(1)} %get-tuple-element.31), channel_id=1, source_target_pairs={{4,16},{8,20},{12,24},{0,28},{20,32},{24,36},{28,40},{16,44},{36,4... | collective-permute-start | bytes 245768 | tf_op jit(solution)/shard_map/ppermute | solution.py:433
  9.2 0.0 collective-permute-start.1
  9.2 2.7 %collective-permute-start.2 = (bf16[8,160,128]{2,1,0:T(8,128)(2,1)S(1)}, bf16[8,160,128]{2,1,0:T(8,128)(2,1)S(1)}, u32[]{:S(2)}, u32[]{:S(2)}) collective-permute-start(bf16[8,160,128]{2,1,0:T(8,128)(2,1)S(1)} %get-tuple-element.29), channel_id=1, source_target_pairs={{4,0},{8,4},{12,8},{0,12},{5,1},{9,5},{13,9},{1,13},{6,2},{10,6},{... | collective-permute-start | bytes 983048 | tf_op jit(solution)/shard_map/ppermute | solution.py:430
  11.9 0.9 %collective-permute-start = (bf16[2,8,160,128]{3,2,1,0:T(8,128)(2,1)S(1)}, bf16[2,8,160,128]{3,2,1,0:T(8,128)(2,1)S(1)}, u32[]{:S(2)}, u32[]{:S(2)}) collective-permute-start(bf16[2,8,160,128]{3,2,1,0:T(8,128)(2,1)S(1)} %get-tuple-element.27), channel_id=1, source_target_pairs={{0,16},{16,32},{32,48},{48,64},{64,80},{80,96},{96,112},{112,0},{1... | collective-permute-start | bytes 1966088 | tf_op jit(solution)/shard_map/ppermute | solution.py:431
  12.7 10.9 %inner.2 = (f32[8,8,160,256]{3,2,1,0:T(8,128)S(1)}, f32[8,8,256]{2,1,0:T(8,128)S(1)}) custom-call(s32[4]{0:T(128)S(4)} %get-tuple-element.24.frames_ref, bf16[8,8,160,384]{3,2,1,0:T(8,128)(2,1)S(1)} %get-tuple-element.26.xc, bf16[3456,256]{1,0:T(8,128)(2,1)S(1)} %get-tuple-element.25.w_ref), custom_call_target="tpu_custom_call" | custom-call | flops 10192158720 | bytes 5242880 | tf_op jit(solution)/shard_map/inner/pallas_call | solution.py:165
  23.7 0.0 collective-permute-done.3.above_before
  23.7 0.0 collective-permute-done.4.below_before
  23.7 0.0 collective-permute-done.1.above
  23.7 0.0 collective-permute-done.2.below
  23.7 0.0 collective-permute-done.before
  23.7 0.1 strips.1
  23.8 1.4 %collective-permute-start.5 = (bf16[10,16,128]{2,1,0:T(8,128)(2,1)S(1)}, bf16[10,16,128]{2,1,0:T(8,128)(2,1)S(1)}, u32[]{:S(2)}, u32[]{:S(2)}) collective-permute-start(bf16[10,16,128]{2,1,0:T(8,128)(2,1)S(1)} %get-tuple-element.32), channel_id=1, source_target_pairs={{0,1},{1,2},{2,3},{3,0},{4,5},{5,6},{6,7},{7,4},{8,9},{9,10},{10,1... | collective-permute-start | bytes 122888 | tf_op jit(solution)/shard_map/ppermute | solution.py:445
  25.2 2.0 %inner.3 = (f32[8,8,160,256]{3,2,1,0:T(8,128)S(1)}, f32[8,8,256]{2,1,0:T(8,128)S(1)}, bf16[10,16,128]{2,1,0:T(8,128)(2,1)S(1)}) custom-call(s32[4]{0:T(128)S(4)} %get-tuple-element.24.frames_ref, bf16[8,8,160,384]{3,2,1,0:T(8,128)(2,1)S(1)} %get-tuple-element.26.xc, ...), custom_call_target="tpu_custom_call", output_to_operand_aliasing={{0}: (3, {}), {1}: (4, {}), {2}: (5, {})} | custom-call | flops 1698693120 | bytes 5242880 | tf_op jit(solution)/shard_map/inner/pallas_call | solution.py:165
  27.2 1.7 %collective-permute-start.6 = (bf16[10,16,128]{2,1,0:T(8,128)(2,1)S(1)}, bf16[10,16,128]{2,1,0:T(8,128)(2,1)S(1)}, u32[]{:S(2)}, u32[]{:S(2)}) collective-permute-start(bf16[10,16,128]{2,1,0:T(8,128)(2,1)S(1)} %get-tuple-element.36), channel_id=1, source_target_pairs={{1,0},{2,1},{3,2},{0,3},{5,4},{6,5},{7,6},{4,7},{9,8},{10,9},{11,1... | collective-permute-start | bytes 122888 | tf_op jit(solution)/shard_map/ppermute | solution.py:447
  28.9 0.0 collective-permute-done.5.arrived.low_ref
  28.9 8.0 %outer.1 = (f32[8,8,160,256]{3,2,1,0:T(8,128)S(1)}, f32[8,8,256]{2,1,0:T(8,128)S(1)}) custom-call(s32[4]{0:T(128)S(4)} %get-tuple-element.24.frames_ref, bf16[3456,256]{1,0:T(8,128)(2,1)S(1)} %get-tuple-element.25.w_ref, bf16[2,8,160,128]{3,2,1,0:T(8,128)(2,1)S(1)} %collective-permute-done.before, ...), custom_call_target="tpu_custom_call", output_to_operand_aliasing={{0}: (9, {}), {1}: (10, {})} | custom-call | flops 6228541440 | bytes 5242880 | tf_op jit(solution)/shard_map/outer/pallas_call | solution.py:448
  36.9 0.0 copy-start
  36.9 0.0 copy-start.1
  36.9 0.0 collective-permute-done.6.high_ref
  36.9 0.7 %columns.1 = (f32[8,8,160,256]{3,2,1,0:T(8,128)S(1)}, f32[1,256]{1,0:T(1,128)S(1)}) custom-call(s32[4]{0:T(128)S(4)} %get-tuple-element.24.frames_ref, bf16[3456,256]{1,0:T(8,128)(2,1)S(1)} %get-tuple-element.25.w_ref, bf16[10,16,128]{2,1,0:T(8,128)(2,1)S(1)} %collective-permute-done.5.arrived.low_ref, ...), custom_call_target="tpu_custom_call", output_to_operand_aliasing={{0}: (5, {})} | custom-call | flops 134217728 | bytes 1048576 | tf_op jit(solution)/shard_map/columns/pallas_call | solution.py:463
  37.7 0.1 broadcast_in_dim.15
  37.7 15.7 %all_to_all.5 = f32[128,1,256]{2,1,0:T(1,128)S(1)} all-to-all(f32[128,1,256]{2,1,0:T(1,128)S(1)} %broadcast_in_dim.15), channel_id=1, replica_groups=mesh['tm'=8,'row'=4,'col'=4] {'tm','row','col'}, dimensions={0} | all-to-all | bytes 262144 | tf_op jit(solution)/shard_map/all_to_all | solution.py:475
  53.4 0.0 copy-done
  53.4 0.0 copy-done.1
  53.4 3.2 %norm_silu.1 = bf16[8,8,160,256]{3,2,1,0:T(8,128)(2,1)} custom-call(s32[4]{0:T(128)S(4)} %get-tuple-element.24.frames_ref, f32[128,256]{1,0:T(8,128)S(1)} %bitcast.7, f32[1,256]{1,0:T(1,128)S(1)} %bitcast.8, f32[1,256]{1,0:T(1,128)S(1)} %bitcast.9, f32[8,8,160,256]{3,2,1,0:T(8,128)S(1)} %get-tuple-element.42.conv), custom_call_target="tpu_custom_call" | custom-call | flops 16777216 | bytes 16777216 | tf_op jit(solution)/shard_map/norm_silu/pallas_call | solution.py:476
  (1 shorter events, 0.0 us)
Async XLA Ops:
  2.9 20.7 %collective-permute-start.3 = (bf16[2,160,128]{2,1,0:T(8,128)(2,1)S(1)}, bf16[2,160,128]{2,1,0:T(8,128)(2,1)S(1)}, u32[]{:S(2)}, u32[]{:S(2)}) collective-permute-start(bf16[2,160,128]{2,1,0:T(8,128)(2,1)S(1)} %get-tuple-element.30), channel_id=1, source_target_pairs={{0,20},{4,24},{8,28},{12,16},{16,36},{20,40},{24,44},{28,32},{32,5... | collective-permute-start | bytes 245768 | tf_op jit(solution)/shard_map/ppermute | solution.py:432
  7.0 16.7 %collective-permute-start.4 = (bf16[2,160,128]{2,1,0:T(8,128)(2,1)S(1)}, bf16[2,160,128]{2,1,0:T(8,128)(2,1)S(1)}, u32[]{:S(2)}, u32[]{:S(2)}) collective-permute-start(bf16[2,160,128]{2,1,0:T(8,128)(2,1)S(1)} %get-tuple-element.31), channel_id=1, source_target_pairs={{4,16},{8,20},{12,24},{0,28},{20,32},{24,36},{28,40},{16,44},{36,4... | collective-permute-start | bytes 245768 | tf_op jit(solution)/shard_map/ppermute | solution.py:433
  9.2 14.5 %collective-permute-start.1 = (bf16[8,160,128]{2,1,0:T(8,128)(2,1)S(1)}, bf16[8,160,128]{2,1,0:T(8,128)(2,1)S(1)}, u32[]{:S(2)}, u32[]{:S(2)}) collective-permute-start(bf16[8,160,128]{2,1,0:T(8,128)(2,1)S(1)} %get-tuple-element.28), channel_id=1, source_target_pairs={{0,4},{4,8},{8,12},{12,0},{1,5},{5,9},{9,13},{13,1},{2,6},{6,10},{... | collective-permute-start | bytes 983048 | tf_op jit(solution)/shard_map/ppermute | solution.py:429
  9.2 14.5 %collective-permute-start.2 = (bf16[8,160,128]{2,1,0:T(8,128)(2,1)S(1)}, bf16[8,160,128]{2,1,0:T(8,128)(2,1)S(1)}, u32[]{:S(2)}, u32[]{:S(2)}) collective-permute-start(bf16[8,160,128]{2,1,0:T(8,128)(2,1)S(1)} %get-tuple-element.29), channel_id=1, source_target_pairs={{4,0},{8,4},{12,8},{0,12},{5,1},{9,5},{13,9},{1,13},{6,2},{10,6},{... | collective-permute-start | bytes 983048 | tf_op jit(solution)/shard_map/ppermute | solution.py:430
  11.9 11.9 %collective-permute-start = (bf16[2,8,160,128]{3,2,1,0:T(8,128)(2,1)S(1)}, bf16[2,8,160,128]{3,2,1,0:T(8,128)(2,1)S(1)}, u32[]{:S(2)}, u32[]{:S(2)}) collective-permute-start(bf16[2,8,160,128]{3,2,1,0:T(8,128)(2,1)S(1)} %get-tuple-element.27), channel_id=1, source_target_pairs={{0,16},{16,32},{32,48},{48,64},{64,80},{80,96},{96,112},{112,0},{1... | collective-permute-start | bytes 1966088 | tf_op jit(solution)/shard_map/ppermute | solution.py:431
  23.8 5.0 %collective-permute-start.5 = (bf16[10,16,128]{2,1,0:T(8,128)(2,1)S(1)}, bf16[10,16,128]{2,1,0:T(8,128)(2,1)S(1)}, u32[]{:S(2)}, u32[]{:S(2)}) collective-permute-start(bf16[10,16,128]{2,1,0:T(8,128)(2,1)S(1)} %get-tuple-element.32), channel_id=1, source_target_pairs={{0,1},{1,2},{2,3},{3,0},{4,5},{5,6},{6,7},{7,4},{8,9},{9,10},{10,1... | collective-permute-start | bytes 122888 | tf_op jit(solution)/shard_map/ppermute | solution.py:445
  27.2 9.8 %collective-permute-start.6 = (bf16[10,16,128]{2,1,0:T(8,128)(2,1)S(1)}, bf16[10,16,128]{2,1,0:T(8,128)(2,1)S(1)}, u32[]{:S(2)}, u32[]{:S(2)}) collective-permute-start(bf16[10,16,128]{2,1,0:T(8,128)(2,1)S(1)} %get-tuple-element.36), channel_id=1, source_target_pairs={{1,0},{2,1},{3,2},{0,3},{5,4},{6,5},{7,6},{4,7},{9,8},{10,9},{11,1... | collective-permute-start | bytes 122888 | tf_op jit(solution)/shard_map/ppermute | solution.py:447
  36.9 16.5 %copy-start = (f32[256]{0:T(256)S(1)}, f32[256]{0:T(256)}, u32[]{:S(2)}) copy-start(f32[256]{0:T(256)} %param.8) | copy-start | bytes 3076
  36.9 16.5 %copy-start.1 = (f32[256]{0:T(256)S(1)}, f32[256]{0:T(256)}, u32[]{:S(2)}) copy-start(f32[256]{0:T(256)} %param.9) | copy-start | bytes 3076

commit v6 on v5

--- a/solution.py
+++ b/solution.py
@@ -46,12 +46,13 @@
     return row == 0, row == lax.axis_size("row") - 1, col == 0, col == lax.axis_size("col") - 1
 
 
-def put_columns(xc, at, x):
+def put_columns(xc, at, x, middle=True):
     _, _, left, right = edges()
     low = jnp.where(left, x[:, :1], jnp.zeros_like(x[:, :1]))
     high = jnp.where(right, x[:, -1:], jnp.zeros_like(x[:, -1:]))
     xc[(*at, slice(None), slice(None), slice(0, C))] = jnp.concatenate([low, x[:, :-1]], axis=1)
-    xc[(*at, slice(None), slice(None), slice(C, 2 * C))] = x
+    if middle:
+        xc[(*at, slice(None), slice(None), slice(C, 2 * C))] = x
     xc[(*at, slice(None), slice(None), slice(2 * C, 3 * C))] = jnp.concatenate([x[:, 1:], high], axis=1)
 
 
@@ -107,13 +108,28 @@
 
 
 def load_kernel(
-    frames_hbm, x_hbm, w_hbm, tail, top_row, bottom_row, tail_top, tail_bottom, xc, w_ref, clips, x_ref, x_sems, w_sem, c_sem
+    frames_hbm,
+    x_hbm,
+    w_hbm,
+    tail,
+    top_row,
+    bottom_row,
+    tail_top,
+    tail_bottom,
+    xc,
+    w_ref,
+    clips,
+    x_sems,
+    w_sem,
+    c_sem,
 ):
     c_copy = pltpu.make_async_copy(frames_hbm, clips, c_sem)
     c_copy.start()
 
+    own = xc.at[:, :, :, C : 2 * C]
+
     def x_copy(f):
-        return pltpu.make_async_copy(x_hbm.at[f], x_ref.at[f], x_sems.at[f])
+        return pltpu.make_async_copy(x_hbm.at[f], own.at[f], x_sems.at[f])
 
     for f in range(F):
         x_copy(f).start()
@@ -122,15 +138,15 @@
 
     def columns(f, carry):
         x_copy(f).wait()
-        top_row[f] = x_ref[f, 0]
-        bottom_row[f] = x_ref[f, H - 1]
-        put_columns(xc, (f,), x_ref[f])
+        top_row[f] = own[f, 0]
+        bottom_row[f] = own[f, H - 1]
+        put_columns(xc, (f,), own[f], middle=False)
         return carry
 
     lax.fori_loop(0, F, columns, 0)
-    tail[...] = x_ref[F - 2 :]
-    tail_top[...] = x_ref[F - 2 :, 0]
-    tail_bottom[...] = x_ref[F - 2 :, H - 1]
+    tail[...] = own[F - 2 :]
+    tail_top[...] = own[F - 2 :, 0]
+    tail_bottom[...] = own[F - 2 :, H - 1]
     w_copy.wait()
     c_copy.wait()
 
@@ -407,7 +423,6 @@
         in_specs=[HBM] * 3,
         out_specs=[VMEM] * 7 + [SMEM],
         scratch_shapes=[
-            pltpu.VMEM((F, H, W, C), BF),
             pltpu.SemaphoreType.DMA((F,)),
             pltpu.SemaphoreType.DMA,
             pltpu.SemaphoreType.DMA,

time: 56.9 us -> 56.7 us (level)
  no operation moved by 1% of the time
where the time goes in v6:
time: 56.7 us; the launch traced here: 56.5 us
  Pallas kernels  27.6 us (49%)
  blocking collectives  15.7 us (28%)
  starting transfers between devices  12.9 us (23%)
    all_to_all x1, blocking collectives, shards(): every = lax.all_to_all(every, ('tm', 'row', 'col'), 0, 0).reshape(count, -1)  15.7 us
    pallas_call x2, Pallas kernels, inner_part(): pl.pallas_call(functools.partial(inner_kernel, frames, opening), out_shap...  12.9 us
    pallas_call x1, Pallas kernels, shards(): pl.pallas_call(outer_kernel, out_shape=(conv_shape, stats_shape), in_spec...  8.03 us
    ppermute x1, starting transfers between devices, shards(): above_before = lax.ppermute(tail_bottom, ('tm', 'row'), diagonal(down))  4.02 us
    pallas_call x1, Pallas kernels, shards(): pl.pallas_call(functools.partial(norm_kernel, H * n_row * W * n_col), out...  3.2 us
    ppermute x1, starting transfers between devices, shards(): below = lax.ppermute(top_row, 'row', up)  2.67 us
    pallas_call x1, Pallas kernels, shards(): pl.pallas_call(load_kernel, out_shape=[pltpu.VMEM((2, H, W, C), BF)] + [p...  2.67 us
    ppermute x1, starting transfers between devices, shards(): below_before = lax.ppermute(tail_top, ('tm', 'row'), diagonal(up))  2.2 us
  transfers between devices with their start and end apart: 7, of which 0 were waited for; matrix products, arithmetic and copies ran while one was open for 0% of the time, Pallas kernels for 37%

profile of v6, /device:TPU:1, one launch (start us, length us, event | category | flops | bytes accessed | tf_op | source)
XLA Modules:
  0.0 56.5 jit_solution(16445376106894184990)
XLA Ops:
  0.0 2.7 %load.1 = (bf16[2,8,160,128]{3,2,1,0:T(8,128)(2,1)S(1)}, bf16[8,160,128]{2,1,0:T(8,128)(2,1)S(1)}, bf16[8,160,128]{2,1,0:T(8,128)(2,1)S(1)}, bf16[2,160,128]{2,1...) custom-call(s32[4]{0:T(128)} %frames_hbm.1, ...), custom_call_target="tpu_custom_call" | custom-call | tf_op jit(solution)/shard_map/load/pallas_call | solution.py:416
  2.7 4.0 %collective-permute-start.3 = (bf16[2,160,128]{2,1,0:T(8,128)(2,1)S(1)}, bf16[2,160,128]{2,1,0:T(8,128)(2,1)S(1)}, u32[]{:S(2)}, u32[]{:S(2)}) collective-permute-start(bf16[2,160,128]{2,1,0:T(8,128)(2,1)S(1)} %get-tuple-element.30), channel_id=1, source_target_pairs={{0,20},{4,24},{8,28},{12,16},{16,36},{20,40},{24,44},{28,32},{32,5... | collective-permute-start | bytes 245768 | tf_op jit(solution)/shard_map/ppermute | solution.py:447
  6.7 2.2 %collective-permute-start.4 = (bf16[2,160,128]{2,1,0:T(8,128)(2,1)S(1)}, bf16[2,160,128]{2,1,0:T(8,128)(2,1)S(1)}, u32[]{:S(2)}, u32[]{:S(2)}) collective-permute-start(bf16[2,160,128]{2,1,0:T(8,128)(2,1)S(1)} %get-tuple-element.31), channel_id=1, source_target_pairs={{4,16},{8,20},{12,24},{0,28},{20,32},{24,36},{28,40},{16,44},{36,4... | collective-permute-start | bytes 245768 | tf_op jit(solution)/shard_map/ppermute | solution.py:448
  8.9 0.0 collective-permute-start.1
  8.9 2.7 %collective-permute-start.2 = (bf16[8,160,128]{2,1,0:T(8,128)(2,1)S(1)}, bf16[8,160,128]{2,1,0:T(8,128)(2,1)S(1)}, u32[]{:S(2)}, u32[]{:S(2)}) collective-permute-start(bf16[8,160,128]{2,1,0:T(8,128)(2,1)S(1)} %get-tuple-element.29), channel_id=1, source_target_pairs={{4,0},{8,4},{12,8},{0,12},{5,1},{9,5},{13,9},{1,13},{6,2},{10,6},{... | collective-permute-start | bytes 983048 | tf_op jit(solution)/shard_map/ppermute | solution.py:445
  11.6 0.9 %collective-permute-start = (bf16[2,8,160,128]{3,2,1,0:T(8,128)(2,1)S(1)}, bf16[2,8,160,128]{3,2,1,0:T(8,128)(2,1)S(1)}, u32[]{:S(2)}, u32[]{:S(2)}) collective-permute-start(bf16[2,8,160,128]{3,2,1,0:T(8,128)(2,1)S(1)} %get-tuple-element.27), channel_id=1, source_target_pairs={{0,16},{16,32},{32,48},{48,64},{64,80},{80,96},{96,112},{112,0},{1... | collective-permute-start | bytes 1966088 | tf_op jit(solution)/shard_map/ppermute | solution.py:446
  12.5 10.9 %inner.2 = (f32[8,8,160,256]{3,2,1,0:T(8,128)S(1)}, f32[8,8,256]{2,1,0:T(8,128)S(1)}) custom-call(s32[4]{0:T(128)S(4)} %get-tuple-element.24.frames_ref, bf16[8,8,160,384]{3,2,1,0:T(8,128)(2,1)S(1)} %get-tuple-element.26.xc, bf16[3456,256]{1,0:T(8,128)(2,1)S(1)} %get-tuple-element.25.w_ref), custom_call_target="tpu_custom_call" | custom-call | flops 10192158720 | bytes 5242880 | tf_op jit(solution)/shard_map/inner/pallas_call | solution.py:181
  23.4 0.0 collective-permute-done.3.above_before
  23.4 0.0 collective-permute-done.4.below_before
  23.4 0.0 collective-permute-done.1.above
  23.4 0.0 collective-permute-done.2.below
  23.5 0.0 collective-permute-done.before
  23.5 0.1 strips.1
  23.6 1.4 %collective-permute-start.5 = (bf16[10,16,128]{2,1,0:T(8,128)(2,1)S(1)}, bf16[10,16,128]{2,1,0:T(8,128)(2,1)S(1)}, u32[]{:S(2)}, u32[]{:S(2)}) collective-permute-start(bf16[10,16,128]{2,1,0:T(8,128)(2,1)S(1)} %get-tuple-element.32), channel_id=1, source_target_pairs={{0,1},{1,2},{2,3},{3,0},{4,5},{5,6},{6,7},{7,4},{8,9},{9,10},{10,1... | collective-permute-start | bytes 122888 | tf_op jit(solution)/shard_map/ppermute | solution.py:460
  24.9 2.0 %inner.3 = (f32[8,8,160,256]{3,2,1,0:T(8,128)S(1)}, f32[8,8,256]{2,1,0:T(8,128)S(1)}, bf16[10,16,128]{2,1,0:T(8,128)(2,1)S(1)}) custom-call(s32[4]{0:T(128)S(4)} %get-tuple-element.24.frames_ref, bf16[8,8,160,384]{3,2,1,0:T(8,128)(2,1)S(1)} %get-tuple-element.26.xc, ...), custom_call_target="tpu_custom_call", output_to_operand_aliasing={{0}: (3, {}), {1}: (4, {}), {2}: (5, {})} | custom-call | flops 1698693120 | bytes 5242880 | tf_op jit(solution)/shard_map/inner/pallas_call | solution.py:181
  26.9 1.7 %collective-permute-start.6 = (bf16[10,16,128]{2,1,0:T(8,128)(2,1)S(1)}, bf16[10,16,128]{2,1,0:T(8,128)(2,1)S(1)}, u32[]{:S(2)}, u32[]{:S(2)}) collective-permute-start(bf16[10,16,128]{2,1,0:T(8,128)(2,1)S(1)} %get-tuple-element.36), channel_id=1, source_target_pairs={{1,0},{2,1},{3,2},{0,3},{5,4},{6,5},{7,6},{4,7},{9,8},{10,9},{11,1... | collective-permute-start | bytes 122888 | tf_op jit(solution)/shard_map/ppermute | solution.py:462
  28.6 0.0 collective-permute-done.5.arrived.low_ref
  28.6 8.0 %outer.1 = (f32[8,8,160,256]{3,2,1,0:T(8,128)S(1)}, f32[8,8,256]{2,1,0:T(8,128)S(1)}) custom-call(s32[4]{0:T(128)S(4)} %get-tuple-element.24.frames_ref, bf16[3456,256]{1,0:T(8,128)(2,1)S(1)} %get-tuple-element.25.w_ref, bf16[2,8,160,128]{3,2,1,0:T(8,128)(2,1)S(1)} %collective-permute-done.before, ...), custom_call_target="tpu_custom_call", output_to_operand_aliasing={{0}: (9, {}), {1}: (10, {})} | custom-call | flops 6228541440 | bytes 5242880 | tf_op jit(solution)/shard_map/outer/pallas_call | solution.py:463
  36.6 0.0 copy-start
  36.7 0.0 copy-start.1
  36.7 0.0 collective-permute-done.6.high_ref
  36.7 0.7 %columns.1 = (f32[8,8,160,256]{3,2,1,0:T(8,128)S(1)}, f32[1,256]{1,0:T(1,128)S(1)}) custom-call(s32[4]{0:T(128)S(4)} %get-tuple-element.24.frames_ref, bf16[3456,256]{1,0:T(8,128)(2,1)S(1)} %get-tuple-element.25.w_ref, bf16[10,16,128]{2,1,0:T(8,128)(2,1)S(1)} %collective-permute-done.5.arrived.low_ref, ...), custom_call_target="tpu_custom_call", output_to_operand_aliasing={{0}: (5, {})} | custom-call | flops 134217728 | bytes 1048576 | tf_op jit(solution)/shard_map/columns/pallas_call | solution.py:478
  37.4 0.1 broadcast_in_dim.15
  37.5 15.7 %all_to_all.5 = f32[128,1,256]{2,1,0:T(1,128)S(1)} all-to-all(f32[128,1,256]{2,1,0:T(1,128)S(1)} %broadcast_in_dim.15), channel_id=1, replica_groups=mesh['tm'=8,'row'=4,'col'=4] {'tm','row','col'}, dimensions={0} | all-to-all | bytes 262144 | tf_op jit(solution)/shard_map/all_to_all | solution.py:490
  53.2 0.0 copy-done
  53.2 0.0 copy-done.1
  53.2 3.2 %norm_silu.1 = bf16[8,8,160,256]{3,2,1,0:T(8,128)(2,1)} custom-call(s32[4]{0:T(128)S(4)} %get-tuple-element.24.frames_ref, f32[128,256]{1,0:T(8,128)S(1)} %bitcast.7, f32[1,256]{1,0:T(1,128)S(1)} %bitcast.8, f32[1,256]{1,0:T(1,128)S(1)} %bitcast.9, f32[8,8,160,256]{3,2,1,0:T(8,128)S(1)} %get-tuple-element.42.conv), custom_call_target="tpu_custom_call" | custom-call | flops 16777216 | bytes 16777216 | tf_op jit(solution)/shard_map/norm_silu/pallas_call | solution.py:491
  (1 shorter events, 0.0 us)
Async XLA Ops:
  2.7 20.7 %collective-permute-start.3 = (bf16[2,160,128]{2,1,0:T(8,128)(2,1)S(1)}, bf16[2,160,128]{2,1,0:T(8,128)(2,1)S(1)}, u32[]{:S(2)}, u32[]{:S(2)}) collective-permute-start(bf16[2,160,128]{2,1,0:T(8,128)(2,1)S(1)} %get-tuple-element.30), channel_id=1, source_target_pairs={{0,20},{4,24},{8,28},{12,16},{16,36},{20,40},{24,44},{28,32},{32,5... | collective-permute-start | bytes 245768 | tf_op jit(solution)/shard_map/ppermute | solution.py:447
  6.7 16.7 %collective-permute-start.4 = (bf16[2,160,128]{2,1,0:T(8,128)(2,1)S(1)}, bf16[2,160,128]{2,1,0:T(8,128)(2,1)S(1)}, u32[]{:S(2)}, u32[]{:S(2)}) collective-permute-start(bf16[2,160,128]{2,1,0:T(8,128)(2,1)S(1)} %get-tuple-element.31), channel_id=1, source_target_pairs={{4,16},{8,20},{12,24},{0,28},{20,32},{24,36},{28,40},{16,44},{36,4... | collective-permute-start | bytes 245768 | tf_op jit(solution)/shard_map/ppermute | solution.py:448
  8.9 14.5 %collective-permute-start.1 = (bf16[8,160,128]{2,1,0:T(8,128)(2,1)S(1)}, bf16[8,160,128]{2,1,0:T(8,128)(2,1)S(1)}, u32[]{:S(2)}, u32[]{:S(2)}) collective-permute-start(bf16[8,160,128]{2,1,0:T(8,128)(2,1)S(1)} %get-tuple-element.28), channel_id=1, source_target_pairs={{0,4},{4,8},{8,12},{12,0},{1,5},{5,9},{9,13},{13,1},{2,6},{6,10},{... | collective-permute-start | bytes 983048 | tf_op jit(solution)/shard_map/ppermute | solution.py:444
  8.9 14.5 %collective-permute-start.2 = (bf16[8,160,128]{2,1,0:T(8,128)(2,1)S(1)}, bf16[8,160,128]{2,1,0:T(8,128)(2,1)S(1)}, u32[]{:S(2)}, u32[]{:S(2)}) collective-permute-start(bf16[8,160,128]{2,1,0:T(8,128)(2,1)S(1)} %get-tuple-element.29), channel_id=1, source_target_pairs={{4,0},{8,4},{12,8},{0,12},{5,1},{9,5},{13,9},{1,13},{6,2},{10,6},{... | collective-permute-start | bytes 983048 | tf_op jit(solution)/shard_map/ppermute | solution.py:445
  11.6 11.9 %collective-permute-start = (bf16[2,8,160,128]{3,2,1,0:T(8,128)(2,1)S(1)}, bf16[2,8,160,128]{3,2,1,0:T(8,128)(2,1)S(1)}, u32[]{:S(2)}, u32[]{:S(2)}) collective-permute-start(bf16[2,8,160,128]{3,2,1,0:T(8,128)(2,1)S(1)} %get-tuple-element.27), channel_id=1, source_target_pairs={{0,16},{16,32},{32,48},{48,64},{64,80},{80,96},{96,112},{112,0},{1... | collective-permute-start | bytes 1966088 | tf_op jit(solution)/shard_map/ppermute | solution.py:446
  23.6 5.0 %collective-permute-start.5 = (bf16[10,16,128]{2,1,0:T(8,128)(2,1)S(1)}, bf16[10,16,128]{2,1,0:T(8,128)(2,1)S(1)}, u32[]{:S(2)}, u32[]{:S(2)}) collective-permute-start(bf16[10,16,128]{2,1,0:T(8,128)(2,1)S(1)} %get-tuple-element.32), channel_id=1, source_target_pairs={{0,1},{1,2},{2,3},{3,0},{4,5},{5,6},{6,7},{7,4},{8,9},{9,10},{10,1... | collective-permute-start | bytes 122888 | tf_op jit(solution)/shard_map/ppermute | solution.py:460
  26.9 9.8 %collective-permute-start.6 = (bf16[10,16,128]{2,1,0:T(8,128)(2,1)S(1)}, bf16[10,16,128]{2,1,0:T(8,128)(2,1)S(1)}, u32[]{:S(2)}, u32[]{:S(2)}) collective-permute-start(bf16[10,16,128]{2,1,0:T(8,128)(2,1)S(1)} %get-tuple-element.36), channel_id=1, source_target_pairs={{1,0},{2,1},{3,2},{0,3},{5,4},{6,5},{7,6},{4,7},{9,8},{10,9},{11,1... | collective-permute-start | bytes 122888 | tf_op jit(solution)/shard_map/ppermute | solution.py:462
  36.6 16.5 %copy-start = (f32[256]{0:T(256)S(1)}, f32[256]{0:T(256)}, u32[]{:S(2)}) copy-start(f32[256]{0:T(256)} %param.8) | copy-start | bytes 3076
  36.7 16.5 %copy-start.1 = (f32[256]{0:T(256)S(1)}, f32[256]{0:T(256)}, u32[]{:S(2)}) copy-start(f32[256]{0:T(256)} %param.9) | copy-start | bytes 3076

commit v7 on v6

--- a/solution.py
+++ b/solution.py
@@ -126,7 +126,7 @@
     c_copy = pltpu.make_async_copy(frames_hbm, clips, c_sem)
     c_copy.start()
 
-    own = xc.at[:, :, :, C : 2 * C]
+    own = xc.at[2:, :, :, C : 2 * C]
 
     def x_copy(f):
         return pltpu.make_async_copy(x_hbm.at[f], own.at[f], x_sems.at[f])
@@ -140,7 +140,7 @@
         x_copy(f).wait()
         top_row[f] = own[f, 0]
         bottom_row[f] = own[f, H - 1]
-        put_columns(xc, (f,), own[f], middle=False)
+        put_columns(xc, (f + 2,), own[f], middle=False)
         return carry
 
     lax.fori_loop(0, F, columns, 0)
@@ -152,7 +152,7 @@
 
 
 def inner_frame(f, first, starts, xc, w_ref, conv, stats):
-    frames = [xc.at[source(starts, first, f, k)] for k in range(2)] + [xc.at[f]]
+    frames = [xc.at[source(starts, first, f, k) + 2] for k in range(2)] + [xc.at[f + 2]]
     for row in (1, 3, 5):
         out = inner_taps(frames, row, 2, w_ref, (0, 1, 2))
         conv[f, row : row + 2] = out
@@ -167,8 +167,8 @@
         inner_frame(f, first, starts, xc, w_ref, conv, stats)
     if opening:
         for row in (1, 3, 5):
-            conv[0, row : row + 2] = inner_taps([xc.at[0]], row, 2, w_ref, (2,))
-            own = [xc.at[source(starts, first, 1, 1)], xc.at[1]]
+            conv[0, row : row + 2] = inner_taps([xc.at[2]], row, 2, w_ref, (2,))
+            own = [xc.at[source(starts, first, 1, 1) + 2], xc.at[3]]
             conv[1, row : row + 2] = inner_taps(own, row, 2, w_ref, (1, 2))
 
 
@@ -204,7 +204,7 @@
             else:
                 g = f - 2
                 rows = [
-                    xc[g, r, at : at + 16, C : 2 * C].astype(F32)[pick : pick + 1]
+                    xc[f, r, at : at + 16, C : 2 * C].astype(F32)[pick : pick + 1]
                     for r in range(H)
                 ]
                 over, under = tile(above, g), tile(below, g)
@@ -222,17 +222,16 @@
     below,
     above_before,
     below_before,
-    xc,
     arrived,
+    xc_in,
     conv_in,
     stats_in,
+    xc,
     conv,
     stats,
-    early,
-    early_rims,
     rims,
 ):
-    del arrived, conv_in, stats_in
+    del arrived, xc_in, conv_in, stats_in
     first = lax.axis_index("tm") * F
     starts = clip_starts(frames_ref)
     top, bottom, _, _ = edges()
@@ -241,20 +240,11 @@
         rim = jnp.stack([jnp.where(top, own[0], over), jnp.where(bottom, own[H - 1], under)])
         put_columns(ref, (at,), rim)
 
-    def fill_early(i):
-        if i == 2:
-            for f in range(2):
-                early[2 + f] = xc[f]
-                early_rims[2 + f] = rims[f]
-        else:
-            put_columns(early, (i,), before[i])
-            fill_rims(early_rims, i, before.at[i], above_before[i], below_before[i])
-
-    def outer_rows(f, place, frames, edge):
+    def outer_rows(f):
         parts = []
         for k in range(3):
-            s = source(starts, first, f, k) + place
-            frame, rim = frames.at[s], edge.at[s]
+            s = source(starts, first, f, k) + 2
+            frame, rim = xc.at[s], rims.at[s]
             upper = [rim[0], frame[0], frame[1]]
             lower = [frame[H - 2], frame[H - 1], rim[1]]
             parts += [jnp.concatenate([u, v], axis=0) for u, v in zip(upper, lower)]
@@ -264,19 +254,20 @@
         conv[f, H - 1] = out[1]
         return out
 
+    for f in range(2):
+        put_columns(xc, (f,), before[f])
+        fill_rims(rims, f, before.at[f], above_before[f], below_before[f])
     for f in range(F):
-        fill_rims(rims, f, xc.at[f, :, :, C : 2 * C], above[f], below[f])
-    for i in range(3):
-        fill_early(i)
+        fill_rims(rims, f + 2, xc.at[f + 2, :, :, C : 2 * C], above[f], below[f])
     for f in range(2, F):
-        add_stats(stats, f, outer_rows(f, 0, xc, rims))
+        add_stats(stats, f, outer_rows(f))
     for f in range(2):
-        start_stats(stats, f, outer_rows(f, 2, early, early_rims))
+        start_stats(stats, f, outer_rows(f))
 
     def first_frames(i, carry):
         row = 1 + 2 * i
         for f, taps in ((0, (0, 1)), (1, (0,))):
-            frames = [early.at[source(starts, first, f, k) + 2] for k in taps]
+            frames = [xc.at[source(starts, first, f, k) + 2] for k in taps]
             out = conv[f, pl.ds(row, 2)] + inner_taps(frames, row, 2, w_ref, taps)
             conv[f, pl.ds(row, 2)] = out
             add_stats(stats, f, out)
@@ -418,7 +409,7 @@
         out_shape=[pltpu.VMEM((2, H, W, C), BF)]
         + [pltpu.VMEM((F, W, C), BF)] * 2
         + [pltpu.VMEM((2, W, C), BF)] * 2
-        + [pltpu.VMEM((F, H, W, C3), BF), pltpu.VMEM((27 * C, COUT), BF)]
+        + [pltpu.VMEM((F + 2, H, W, C3), BF), pltpu.VMEM((27 * C, COUT), BF)]
         + [pltpu.SMEM((CLIPS,), jnp.int32)],
         in_specs=[HBM] * 3,
         out_specs=[VMEM] * 7 + [SMEM],
@@ -427,7 +418,7 @@
             pltpu.SemaphoreType.DMA,
             pltpu.SemaphoreType.DMA,
         ],
-        compiler_params=params(52),
+        compiler_params=params(50),
         name="load",
     )(clip_frames, frames_in, weights)
     down = [(i, (i + 1) % n_row) for i in range(n_row)]
@@ -438,6 +429,7 @@
         return [(t * n_row + i, u * n_row + j) for t, u in later for i, j in pairs]
 
     conv_shape = pltpu.VMEM((F, H, W, COUT), F32)
+    xc_shape = pltpu.VMEM((F + 2, H, W, C3), BF)
     stats_shape = pltpu.VMEM((F, 8, COUT), F32)
     macs = W * 9 * C3 * COUT
     part = lambda *args: inner_part(args[0], args[1], clips, xc, weights, *args[2:])
@@ -460,21 +452,17 @@
     from_left = lax.ppermute(high, "col", onward)
     conv, stats, low = part((7,), False, conv, stats, low)
     from_right = lax.ppermute(low, "col", [(j, i) for i, j in onward])
-    conv, stats = pl.pallas_call(
+    _, conv, stats = pl.pallas_call(
         outer_kernel,
-        out_shape=(conv_shape, stats_shape),
+        out_shape=(xc_shape, conv_shape, stats_shape),
         in_specs=[SMEM] + [VMEM] * 10,
-        out_specs=[VMEM] * 2,
-        input_output_aliases={9: 0, 10: 1},
-        scratch_shapes=[
-            pltpu.VMEM((4, H, W, C3), BF),
-            pltpu.VMEM((4, 2, W, C3), BF),
-            pltpu.VMEM((F, 2, W, C3), BF),
-        ],
+        out_specs=[VMEM] * 3,
+        input_output_aliases={8: 0, 9: 1, 10: 2},
+        scratch_shapes=[pltpu.VMEM((F + 2, 2, W, C3), BF)],
         compiler_params=params(18),
         cost_estimate=cost(2 * 22 * macs, 5 << 20),
         name="outer",
-    )(clips, weights, before, above, below, above_before, below_before, xc, from_left, conv, stats)
+    )(clips, weights, before, above, below, above_before, below_before, from_left, xc, conv, stats)
     conv, stats = pl.pallas_call(
         column_kernel,
         out_shape=(conv_shape, jax.ShapeDtypeStruct((1, 2 * CLIPS * GROUPS), F32)),

time: 56.7 us -> 56.6 us (level)
  no operation moved by 1% of the time
where the time goes in v7:
time: 56.6 us; the launch traced here: 56.4 us
  Pallas kernels  27.5 us (49%)
  blocking collectives  15.7 us (28%)
  starting transfers between devices  12.9 us (23%)
    all_to_all x1, blocking collectives, shards(): every = lax.all_to_all(every, ('tm', 'row', 'col'), 0, 0).reshape(count, -1)  15.7 us
    pallas_call x2, Pallas kernels, inner_part(): pl.pallas_call(functools.partial(inner_kernel, frames, opening), out_shap...  12.9 us
    pallas_call x1, Pallas kernels, shards(): pl.pallas_call(outer_kernel, out_shape=(xc_shape, conv_shape, stats_shape...  7.93 us
    ppermute x1, starting transfers between devices, shards(): above_before = lax.ppermute(tail_bottom, ('tm', 'row'), diagonal(down))  4.02 us
    pallas_call x1, Pallas kernels, shards(): pl.pallas_call(functools.partial(norm_kernel, H * n_row * W * n_col), out...  3.2 us
    ppermute x1, starting transfers between devices, shards(): below = lax.ppermute(top_row, 'row', up)  2.67 us
    pallas_call x1, Pallas kernels, shards(): pl.pallas_call(load_kernel, out_shape=[pltpu.VMEM((2, H, W, C), BF)] + [p...  2.67 us
    ppermute x1, starting transfers between devices, shards(): below_before = lax.ppermute(tail_top, ('tm', 'row'), diagonal(up))  2.2 us
  transfers between devices with their start and end apart: 7, of which 0 were waited for; matrix products, arithmetic and copies ran while one was open for 0% of the time, Pallas kernels for 37%

profile of v7, /device:TPU:1, one launch (start us, length us, event | category | flops | bytes accessed | tf_op | source)
XLA Modules:
  0.0 56.4 jit_solution(683989247739045169)
XLA Ops:
  0.0 2.7 %load.1 = (bf16[2,8,160,128]{3,2,1,0:T(8,128)(2,1)S(1)}, bf16[8,160,128]{2,1,0:T(8,128)(2,1)S(1)}, bf16[8,160,128]{2,1,0:T(8,128)(2,1)S(1)}, bf16[2,160,128]{2,1...) custom-call(s32[4]{0:T(128)} %frames_hbm.1, ...), custom_call_target="tpu_custom_call" | custom-call | tf_op jit(solution)/shard_map/load/pallas_call | solution.py:407
  2.7 4.0 %collective-permute-start.3 = (bf16[2,160,128]{2,1,0:T(8,128)(2,1)S(1)}, bf16[2,160,128]{2,1,0:T(8,128)(2,1)S(1)}, u32[]{:S(2)}, u32[]{:S(2)}) collective-permute-start(bf16[2,160,128]{2,1,0:T(8,128)(2,1)S(1)} %get-tuple-element.30), channel_id=1, source_target_pairs={{0,20},{4,24},{8,28},{12,16},{16,36},{20,40},{24,44},{28,32},{32,5... | collective-permute-start | bytes 245768 | tf_op jit(solution)/shard_map/ppermute | solution.py:439
  6.7 2.2 %collective-permute-start.4 = (bf16[2,160,128]{2,1,0:T(8,128)(2,1)S(1)}, bf16[2,160,128]{2,1,0:T(8,128)(2,1)S(1)}, u32[]{:S(2)}, u32[]{:S(2)}) collective-permute-start(bf16[2,160,128]{2,1,0:T(8,128)(2,1)S(1)} %get-tuple-element.31), channel_id=1, source_target_pairs={{4,16},{8,20},{12,24},{0,28},{20,32},{24,36},{28,40},{16,44},{36,4... | collective-permute-start | bytes 245768 | tf_op jit(solution)/shard_map/ppermute | solution.py:440
  8.9 0.0 collective-permute-start.1
  8.9 2.7 %collective-permute-start.2 = (bf16[8,160,128]{2,1,0:T(8,128)(2,1)S(1)}, bf16[8,160,128]{2,1,0:T(8,128)(2,1)S(1)}, u32[]{:S(2)}, u32[]{:S(2)}) collective-permute-start(bf16[8,160,128]{2,1,0:T(8,128)(2,1)S(1)} %get-tuple-element.29), channel_id=1, source_target_pairs={{4,0},{8,4},{12,8},{0,12},{5,1},{9,5},{13,9},{1,13},{6,2},{10,6},{... | collective-permute-start | bytes 983048 | tf_op jit(solution)/shard_map/ppermute | solution.py:437
  11.6 0.9 %collective-permute-start = (bf16[2,8,160,128]{3,2,1,0:T(8,128)(2,1)S(1)}, bf16[2,8,160,128]{3,2,1,0:T(8,128)(2,1)S(1)}, u32[]{:S(2)}, u32[]{:S(2)}) collective-permute-start(bf16[2,8,160,128]{3,2,1,0:T(8,128)(2,1)S(1)} %get-tuple-element.27), channel_id=1, source_target_pairs={{0,16},{16,32},{32,48},{48,64},{64,80},{80,96},{96,112},{112,0},{1... | collective-permute-start | bytes 1966088 | tf_op jit(solution)/shard_map/ppermute | solution.py:438
  12.5 10.9 %inner.2 = (f32[8,8,160,256]{3,2,1,0:T(8,128)S(1)}, f32[8,8,256]{2,1,0:T(8,128)S(1)}) custom-call(s32[4]{0:T(128)S(4)} %get-tuple-element.24.frames_ref, bf16[10,8,160,384]{3,2,1,0:T(8,128)(2,1)S(1)} %get-tuple-element.26.xc.xc_in, bf16[3456,256]{1,0:T(8,128)(2,1)S(1)} %get-tuple-element.25.w_ref), custom_call_target="tpu_custom_call" | custom-call | flops 10192158720 | bytes 5242880 | tf_op jit(solution)/shard_map/inner/pallas_call | solution.py:181
  23.4 0.0 collective-permute-done.3.above_before
  23.4 0.0 collective-permute-done.4.below_before
  23.4 0.0 collective-permute-done.1.above
  23.4 0.0 collective-permute-done.2.below
  23.5 0.0 collective-permute-done.before
  23.5 0.1 strips.1
  23.6 1.4 %collective-permute-start.5 = (bf16[10,16,128]{2,1,0:T(8,128)(2,1)S(1)}, bf16[10,16,128]{2,1,0:T(8,128)(2,1)S(1)}, u32[]{:S(2)}, u32[]{:S(2)}) collective-permute-start(bf16[10,16,128]{2,1,0:T(8,128)(2,1)S(1)} %get-tuple-element.32), channel_id=1, source_target_pairs={{0,1},{1,2},{2,3},{3,0},{4,5},{5,6},{6,7},{7,4},{8,9},{9,10},{10,1... | collective-permute-start | bytes 122888 | tf_op jit(solution)/shard_map/ppermute | solution.py:452
  24.9 2.0 %inner.3 = (f32[8,8,160,256]{3,2,1,0:T(8,128)S(1)}, f32[8,8,256]{2,1,0:T(8,128)S(1)}, bf16[10,16,128]{2,1,0:T(8,128)(2,1)S(1)}) custom-call(s32[4]{0:T(128)S(4)} %get-tuple-element.24.frames_ref, bf16[10,8,160,384]{3,2,1,0:T(8,128)(2,1)S(1)} %get-tuple-element.26.xc.xc_in, ...), custom_call_target="tpu_custom_call", output_to_operand_aliasing={{0}: (3, {}), {1}: (4, {}), {2}: (5, {})} | custom-call | flops 1698693120 | bytes 5242880 | tf_op jit(solution)/shard_map/inner/pallas_call | solution.py:181
  26.9 1.7 %collective-permute-start.6 = (bf16[10,16,128]{2,1,0:T(8,128)(2,1)S(1)}, bf16[10,16,128]{2,1,0:T(8,128)(2,1)S(1)}, u32[]{:S(2)}, u32[]{:S(2)}) collective-permute-start(bf16[10,16,128]{2,1,0:T(8,128)(2,1)S(1)} %get-tuple-element.36), channel_id=1, source_target_pairs={{1,0},{2,1},{3,2},{0,3},{5,4},{6,5},{7,6},{4,7},{9,8},{10,9},{11,1... | collective-permute-start | bytes 122888 | tf_op jit(solution)/shard_map/ppermute | solution.py:454
  28.6 0.0 collective-permute-done.5.arrived.low_ref
  28.6 7.9 %outer.1 = (bf16[10,8,160,384]{3,2,1,0:T(8,128)(2,1)S(1)}, f32[8,8,160,256]{3,2,1,0:T(8,128)S(1)}, f32[8,8,256]{2,1,0:T(8,128)S(1)}) custom-call(s32[4]{0:T(128)S(4)} %get-tuple-element.24.frames_ref, bf16[3456,256]{1,0:T(8,128)(2,1)S(1)} %get-tuple-element.25.w_ref, ...), custom_call_target="tpu_custom_call", output_to_operand_aliasing={{0}: (8, {}), {1}: (9, {}), {2}: (10, {})} | custom-call | flops 6228541440 | bytes 5242880 | tf_op jit(solution)/shard_map/outer/pallas_call | solution.py:455
  36.5 0.0 copy-start
  36.6 0.0 copy-start.1
  36.6 0.0 collective-permute-done.6.high_ref
  36.6 0.7 %columns.1 = (f32[8,8,160,256]{3,2,1,0:T(8,128)S(1)}, f32[1,256]{1,0:T(1,128)S(1)}) custom-call(s32[4]{0:T(128)S(4)} %get-tuple-element.24.frames_ref, bf16[3456,256]{1,0:T(8,128)(2,1)S(1)} %get-tuple-element.25.w_ref, bf16[10,16,128]{2,1,0:T(8,128)(2,1)S(1)} %collective-permute-done.5.arrived.low_ref, ...), custom_call_target="tpu_custom_call", output_to_operand_aliasing={{0}: (5, {})} | custom-call | flops 134217728 | bytes 1048576 | tf_op jit(solution)/shard_map/columns/pallas_call | solution.py:466
  37.3 0.1 broadcast_in_dim.15
  37.4 15.7 %all_to_all.5 = f32[128,1,256]{2,1,0:T(1,128)S(1)} all-to-all(f32[128,1,256]{2,1,0:T(1,128)S(1)} %broadcast_in_dim.15), channel_id=1, replica_groups=mesh['tm'=8,'row'=4,'col'=4] {'tm','row','col'}, dimensions={0} | all-to-all | bytes 262144 | tf_op jit(solution)/shard_map/all_to_all | solution.py:478
  53.1 0.0 copy-done
  53.1 0.0 copy-done.1
  53.1 3.2 %norm_silu.1 = bf16[8,8,160,256]{3,2,1,0:T(8,128)(2,1)} custom-call(s32[4]{0:T(128)S(4)} %get-tuple-element.24.frames_ref, f32[128,256]{1,0:T(8,128)S(1)} %bitcast.7, f32[1,256]{1,0:T(1,128)S(1)} %bitcast.8, f32[1,256]{1,0:T(1,128)S(1)} %bitcast.9, f32[8,8,160,256]{3,2,1,0:T(8,128)S(1)} %get-tuple-element.42.conv), custom_call_target="tpu_custom_call" | custom-call | flops 16777216 | bytes 16777216 | tf_op jit(solution)/shard_map/norm_silu/pallas_call | solution.py:479
  (1 shorter events, 0.0 us)
Async XLA Ops:
  2.7 20.7 %collective-permute-start.3 = (bf16[2,160,128]{2,1,0:T(8,128)(2,1)S(1)}, bf16[2,160,128]{2,1,0:T(8,128)(2,1)S(1)}, u32[]{:S(2)}, u32[]{:S(2)}) collective-permute-start(bf16[2,160,128]{2,1,0:T(8,128)(2,1)S(1)} %get-tuple-element.30), channel_id=1, source_target_pairs={{0,20},{4,24},{8,28},{12,16},{16,36},{20,40},{24,44},{28,32},{32,5... | collective-permute-start | bytes 245768 | tf_op jit(solution)/shard_map/ppermute | solution.py:439
  6.7 16.7 %collective-permute-start.4 = (bf16[2,160,128]{2,1,0:T(8,128)(2,1)S(1)}, bf16[2,160,128]{2,1,0:T(8,128)(2,1)S(1)}, u32[]{:S(2)}, u32[]{:S(2)}) collective-permute-start(bf16[2,160,128]{2,1,0:T(8,128)(2,1)S(1)} %get-tuple-element.31), channel_id=1, source_target_pairs={{4,16},{8,20},{12,24},{0,28},{20,32},{24,36},{28,40},{16,44},{36,4... | collective-permute-start | bytes 245768 | tf_op jit(solution)/shard_map/ppermute | solution.py:440
  8.9 14.5 %collective-permute-start.1 = (bf16[8,160,128]{2,1,0:T(8,128)(2,1)S(1)}, bf16[8,160,128]{2,1,0:T(8,128)(2,1)S(1)}, u32[]{:S(2)}, u32[]{:S(2)}) collective-permute-start(bf16[8,160,128]{2,1,0:T(8,128)(2,1)S(1)} %get-tuple-element.28), channel_id=1, source_target_pairs={{0,4},{4,8},{8,12},{12,0},{1,5},{5,9},{9,13},{13,1},{2,6},{6,10},{... | collective-permute-start | bytes 983048 | tf_op jit(solution)/shard_map/ppermute | solution.py:436
  8.9 14.5 %collective-permute-start.2 = (bf16[8,160,128]{2,1,0:T(8,128)(2,1)S(1)}, bf16[8,160,128]{2,1,0:T(8,128)(2,1)S(1)}, u32[]{:S(2)}, u32[]{:S(2)}) collective-permute-start(bf16[8,160,128]{2,1,0:T(8,128)(2,1)S(1)} %get-tuple-element.29), channel_id=1, source_target_pairs={{4,0},{8,4},{12,8},{0,12},{5,1},{9,5},{13,9},{1,13},{6,2},{10,6},{... | collective-permute-start | bytes 983048 | tf_op jit(solution)/shard_map/ppermute | solution.py:437
  11.6 11.9 %collective-permute-start = (bf16[2,8,160,128]{3,2,1,0:T(8,128)(2,1)S(1)}, bf16[2,8,160,128]{3,2,1,0:T(8,128)(2,1)S(1)}, u32[]{:S(2)}, u32[]{:S(2)}) collective-permute-start(bf16[2,8,160,128]{3,2,1,0:T(8,128)(2,1)S(1)} %get-tuple-element.27), channel_id=1, source_target_pairs={{0,16},{16,32},{32,48},{48,64},{64,80},{80,96},{96,112},{112,0},{1... | collective-permute-start | bytes 1966088 | tf_op jit(solution)/shard_map/ppermute | solution.py:438
  23.6 5.0 %collective-permute-start.5 = (bf16[10,16,128]{2,1,0:T(8,128)(2,1)S(1)}, bf16[10,16,128]{2,1,0:T(8,128)(2,1)S(1)}, u32[]{:S(2)}, u32[]{:S(2)}) collective-permute-start(bf16[10,16,128]{2,1,0:T(8,128)(2,1)S(1)} %get-tuple-element.32), channel_id=1, source_target_pairs={{0,1},{1,2},{2,3},{3,0},{4,5},{5,6},{6,7},{7,4},{8,9},{9,10},{10,1... | collective-permute-start | bytes 122888 | tf_op jit(solution)/shard_map/ppermute | solution.py:452
  26.9 9.7 %collective-permute-start.6 = (bf16[10,16,128]{2,1,0:T(8,128)(2,1)S(1)}, bf16[10,16,128]{2,1,0:T(8,128)(2,1)S(1)}, u32[]{:S(2)}, u32[]{:S(2)}) collective-permute-start(bf16[10,16,128]{2,1,0:T(8,128)(2,1)S(1)} %get-tuple-element.36), channel_id=1, source_target_pairs={{1,0},{2,1},{3,2},{0,3},{5,4},{6,5},{7,6},{4,7},{9,8},{10,9},{11,1... | collective-permute-start | bytes 122888 | tf_op jit(solution)/shard_map/ppermute | solution.py:454
  36.5 16.5 %copy-start = (f32[256]{0:T(256)S(1)}, f32[256]{0:T(256)}, u32[]{:S(2)}) copy-start(f32[256]{0:T(256)} %param.8) | copy-start | bytes 3076
  36.6 16.5 %copy-start.1 = (f32[256]{0:T(256)S(1)}, f32[256]{0:T(256)}, u32[]{:S(2)}) copy-start(f32[256]{0:T(256)} %param.9) | copy-start | bytes 3076
